TPU v7x, 32 devices: a whole 2x2x4 slice. The times are simulated.
32 devices in a mesh: band: 8 (over z, y), tm: 4 (over x, core).
Axes of the slice: x: 2, y: 2, z: 4, core: 2. Of those that a mesh axis runs over, the one named last changes fastest.
Arguments:
- fields: bfloat16 [512, 704, 1440], P('tm', 'band'), may hold values from -6 to 6
- wave_table: int32 [384], replicated, may hold values from 0 to 383, as said below
- day_of_year: int32 [512], P('tm'), may hold values from 0 to 364, as said below
- ar_coef: float32 [384, 384], P('band'), may hold values from -0.9 to 0.9
- log_var: float32 [384, 384], P('band'), may hold values from 0 to 2.5
Outputs:
- innovation: bfloat16 [512, 2, 384, 384], P('tm', None, 'band')
- grad_coef: float32 [384, 384], P('band', 'tm')
- grad_var: float32 [384, 384], P('band', 'tm')
Inputs may be any that keep to these rules, and one draw needn't show every extreme that they name: `wave_table`: every wavenumber below 384 appears once; slots 2 k and 2 k + 1 hold some m and 383 - m. `day_of_year`: consecutive days follow one another in the year, 364 being followed by 0; both 364 and 0 occur.
All inputs are finite; a program needn't handle non-finite values.
Results may differ from a plain program's by a relative error of at most 0.008.
Values may be sent and summed in bfloat16 or wider, within the bound.
No kernel may reach another device: no remote copies, remote signals or barrier semaphores. Data moves between devices by JAX's collectives and lax.ppermute only.
A program may use at most 256 MiB of HBM per device.

v0:
```python
import functools
import math

import jax
import jax.numpy as jnp
from jax import lax
from jax.experimental import pallas as pl
from jax.experimental.pallas import tpu as pltpu
from jax.sharding import PartitionSpec as P

LANES = 128
TILE = 16
PITCH = TILE + 1
HALF = TILE // 4
ROWS = 80
DAY_ROWS = 32
VMEM_LIMIT = 56 * 1024 * 1024


def round_up(value, unit):
    return -(-value // unit) * unit


def fourier_kernel(coarse_cos_ref, coarse_sin_ref, fine_cos_ref, fine_sin_ref, out_ref):
    lon_count = out_ref.shape[1]
    fine_cos, fine_sin = fine_cos_ref[...], fine_sin_ref[...]
    for index in range(-(-lon_count // LANES)):
        width = min(LANES, lon_count - index * LANES)
        coarse_cos = coarse_cos_ref[:, index : index + 1]
        coarse_sin = coarse_sin_ref[:, index : index + 1]
        values = (coarse_cos * fine_cos - coarse_sin * fine_sin).astype(jnp.bfloat16)
        out_ref[:, index * LANES : index * LANES + width] = values[:, :width]


def fourier_rows(waves, lon_count):
    blocks, slots = waves.shape
    rows = blocks * 2 * slots

    def parts(step):
        lons = jnp.arange(LANES, dtype=jnp.int32) * step
        phase = waves[:, :, None] * lons % lon_count
        angle = phase.astype(jnp.float32) * (2.0 * math.pi / lon_count)
        return jnp.cos(angle), jnp.sin(angle)

    def both(first, second):
        return jnp.stack([first, second], axis=1).reshape(rows, LANES)

    coarse_cos, coarse_sin = parts(LANES)
    fine_cos, fine_sin = parts(1)
    return pl.pallas_call(
        fourier_kernel,
        out_shape=jax.ShapeDtypeStruct((rows, lon_count), jnp.bfloat16),
        compiler_params=pltpu.CompilerParams(vmem_limit_bytes=VMEM_LIMIT),
    )(
        both(coarse_cos, -coarse_sin),
        both(coarse_sin, coarse_cos),
        both(fine_cos, fine_cos),
        both(fine_sin, fine_sin),
    )


def transform_kernel(in_ref, table_ref, *out_refs):
    lats, _, days = in_ref.shape
    for lat in range(0, lats, 2):
        both = jnp.concatenate([in_ref[lat], in_ref[lat + 1]], axis=1)
        sums = jnp.dot(table_ref[...], both, preferred_element_type=jnp.float32).astype(jnp.bfloat16)
        begin = 0
        for out_ref in out_refs:
            piece = sums[begin : begin + out_ref.shape[1]]
            begin += out_ref.shape[1]
            out_ref[lat] = piece[:, :days]
            out_ref[lat + 1] = piece[:, days:]


def longitude_sums(fields, table, block_rows):
    lats, lon_count, days = fields.shape
    group = 8 if lats % 8 == 0 else 2
    rows = table.shape[0]
    blocks = rows // block_rows
    return pl.pallas_call(
        transform_kernel,
        grid=(lats // group,),
        in_specs=[
            pl.BlockSpec((group, lon_count, days), lambda i: (i, 0, 0)),
            pl.BlockSpec((rows, lon_count), lambda i: (0, 0)),
        ],
        out_specs=[pl.BlockSpec((group, block_rows, days), lambda i: (i, 0, 0))] * blocks,
        out_shape=[jax.ShapeDtypeStruct((lats, block_rows, days), jnp.bfloat16)] * blocks,
        compiler_params=pltpu.CompilerParams(vmem_limit_bytes=VMEM_LIMIT),
    )(fields, table)


def table_kernel(steps, lane_tiles, top, low_ref, first_ref, second_ref, cos_ref, weight_ref, out_ref, rows_ref, scale_ref):
    tiles = range(lane_tiles)
    low = low_ref[...]
    high = top - low
    low_next = low + 1.0
    lat_count = out_ref.shape[2]
    pairs = out_ref.shape[0]

    def lanes(ref, tile):
        return ref[:, tile * LANES : (tile + 1) * LANES]

    cosines = [lanes(cos_ref, t) for t in tiles]
    weights = [lanes(weight_ref, t) for t in tiles]
    second = [lanes(second_ref, t) for t in tiles]
    for t in tiles:
        half = jnp.exp(0.5 * second[t])
        scale_ref[2, :, t * LANES : (t + 1) * LANES] = half * weights[t]
        scale_ref[3, :, t * LANES : (t + 1) * LANES] = half

    def block(index, carry):
        current, lagged, scale, last_inverse = carry
        for t in tiles:
            largest = jnp.maximum(jnp.maximum(jnp.abs(current[t]), jnp.abs(lagged[t])), 1.0)
            current[t] = current[t] / largest
            lagged[t] = lagged[t] / largest
            scale[t] = scale[t] + jnp.log(largest)
            half = jnp.exp(0.5 * scale[t])
            scale_ref[0, :, t * LANES : (t + 1) * LANES] = half * weights[t]
            scale_ref[1, :, t * LANES : (t + 1) * LANES] = half
        begin = (index * TILE).astype(jnp.float32)
        for step in range(TILE):
            row = begin + float(step)
            after = low < row
            above = row - jnp.where(after, low_next, 0.0)
            order = jnp.where(after, low, high)
            degree = above + order
            spread = above * (degree + order)
            square = 4.0 * degree * degree - 1.0
            root = lax.rsqrt(jnp.maximum(square * spread, 1.0))
            factor = square * root
            inverse = spread * root
            fresh = above == 0.0
            for t in tiles:
                advanced = factor * (cosines[t] * current[t] - last_inverse * lagged[t])
                lagged[t] = current[t]
                current[t] = jnp.where(fresh, 1.0, advanced)
                rows_ref[t, pl.ds(step, pairs, stride=TILE), :] = current[t]
            last_inverse = inverse
        renewed = (low_next >= begin) & (low_next < begin + float(TILE))
        for t in tiles:
            scale[t] = jnp.where(renewed, second[t], scale[t])
        row_index = lax.broadcasted_iota(jnp.int32, (TILE, LANES), 0).astype(jnp.float32) + begin
        for pair in range(pairs):
            mark = low[pair : pair + 1, :]
            before = (row_index <= mark) | (mark + 1.0 < begin)
            for t in tiles:
                span = slice(t * LANES, min((t + 1) * LANES, lat_count))
                width = span.stop - span.start
                here = slice(t * LANES, (t + 1) * LANES)
                values = rows_ref[t, pair * TILE : (pair + 1) * TILE, :]
                one = jnp.where(before, scale_ref[0, pair : pair + 1, here], scale_ref[2, pair : pair + 1, here])
                two = jnp.where(before, scale_ref[1, pair : pair + 1, here], scale_ref[3, pair : pair + 1, here])
                values = (values * one * two).astype(jnp.bfloat16)
                out_ref[pair, pl.ds(pl.multiple_of(index * TILE, TILE), TILE), span] = values[:, :width]
        return current, lagged, scale, last_inverse

    zeros = jnp.zeros((pairs, LANES), jnp.float32)
    start = (
        [zeros for _ in tiles],
        [zeros for _ in tiles],
        [lanes(first_ref, t) for t in tiles],
        zeros,
    )
    lax.fori_loop(0, steps // TILE, block, start)


def packed_table(low_waves, lats, lat_count, degree_count, steps):
    pair_count = low_waves.shape[0]
    lat_half = lats.shape[0]
    lane_tiles = -(-lat_half // LANES)
    width = lane_tiles * LANES
    top = float(degree_count - 1)
    index = jnp.pad(lats, (0, width - lat_half), mode="edge")
    colatitude = (index.astype(jnp.float32) + 0.5) * (math.pi / lat_count)
    sines = jnp.sin(colatitude)
    log_sines = jnp.log(sines)
    low = low_waves.astype(jnp.float32)

    def log_start(order):
        base = 0.5 * (
            jnp.log(order + 0.5)
            + jax.scipy.special.gammaln(order + 0.5)
            - jax.scipy.special.gammaln(order + 1.0)
            - 0.5 * math.log(math.pi)
        )
        return base[:, None] + order[:, None] * log_sines[None, :]

    def spread(row):
        return jnp.broadcast_to(row[None, :], (pair_count, width))

    return pl.pallas_call(
        functools.partial(table_kernel, steps, lane_tiles, top),
        out_shape=jax.ShapeDtypeStruct((pair_count, steps, lat_half), jnp.bfloat16),
        scratch_shapes=[
            pltpu.VMEM((lane_tiles, pair_count * TILE, LANES), jnp.float32),
            pltpu.VMEM((4, pair_count, width), jnp.float32),
        ],
        compiler_params=pltpu.CompilerParams(vmem_limit_bytes=VMEM_LIMIT),
    )(
        jnp.broadcast_to(low[:, None], (pair_count, LANES)),
        log_start(top - low),
        log_start(low),
        spread(jnp.cos(colatitude)),
        spread(sines * (math.pi / lat_count)),
    )


def gather_slots(in_refs, flat_ref, slot_ref):
    lats, rows, days = in_refs[0].shape
    lat_half = len(in_refs) * lats
    step = 8 if lats % 8 == 0 else lats

    for part in range(2):
        for source, in_ref in enumerate(in_refs):

            def spread(index, carry, source=source, in_ref=in_ref, part=part):
                first = index * step
                values = in_ref[pl.ds(first, step), part * TILE : (part + 1) * TILE, :].astype(jnp.float32)
                begin = source * lats + first
                if step == 8:
                    window = flat_ref.at[pl.ds(pl.multiple_of(begin * PITCH, 8), 8 * PITCH)]
                else:
                    window = flat_ref.at[begin * PITCH : (begin + step) * PITCH]
                for lat in range(step):
                    window[lat * PITCH : lat * PITCH + TILE, :] = values[lat]
                return carry

            if step == 8:
                lax.fori_loop(0, lats // step, spread, 0)
            else:
                spread(0, 0)
        for slot in range(TILE):
            column = flat_ref[pl.ds(slot, lat_half, stride=PITCH), :]
            slot_ref[slot, :, part * days : (part + 1) * days] = column.astype(jnp.bfloat16)


def pair_sum(pair, low, table_ref, slot_ref):
    table = table_ref[pair]
    high_sum = jnp.dot(table, slot_ref[2 * pair], preferred_element_type=jnp.float32)
    low_sum = jnp.dot(table, slot_ref[2 * pair + 1], preferred_element_type=jnp.float32)
    row = lax.broadcasted_iota(jnp.int32, high_sum.shape, 0)
    return jnp.where(row <= low, high_sum, low_sum)


def by_halves(one):
    def two(step, carry):
        one(0, step)
        one(1, step)
        return carry

    lax.fori_loop(0, HALF, two, 0)


def partial_kernel(degrees, low_ref, table_ref, *rest):
    *in_refs, first_ref, second_ref, flat_ref, slot_ref, last_ref = rest
    out_refs = (first_ref, second_ref)
    gather_slots(in_refs, flat_ref, slot_ref)
    last_ref[...] = jnp.zeros_like(last_ref)
    last_row = lax.broadcasted_iota(jnp.int32, last_ref.shape[1:], 0)

    def one(half, step):
        pair = half * HALF + step
        sums = pair_sum(pair, low_ref[pair], table_ref, slot_ref)
        begin = pl.multiple_of(step * degrees, TILE)
        out_refs[half][pl.ds(begin, degrees), :] = sums[:degrees].astype(jnp.bfloat16)
        last_ref[half] = jnp.where(last_row == step, sums[degrees : degrees + 1], last_ref[half])

    by_halves(one)
    for half in range(2):
        out_refs[half][HALF * degrees :, :] = last_ref[half].astype(jnp.bfloat16)


def pack_kernel(low_ref, in_ref, ar_ref, half_ref):
    pairs, _, width = in_ref.shape
    steps = ar_ref.shape[1]
    lane = lax.broadcasted_iota(jnp.int32, (1, width), 1)
    degrees = round_up(steps, LANES) - LANES

    def one(pair, carry):
        low = low_ref[pair]
        rows = in_ref[pair]
        high_rows = pltpu.roll(rows, width - (degrees - 1 - low), 1)
        low_rows = pltpu.roll(rows, 1, 1)
        for index, out_ref in enumerate((ar_ref, half_ref)):
            packed = jnp.where(
                lane <= low, high_rows[2 * index : 2 * index + 1], low_rows[2 * index + 1 : 2 * index + 2]
            )
            out_ref[pair] = jnp.broadcast_to(packed, (LANES, width)).T[:steps]
        return carry

    lax.fori_loop(0, pairs, one, 0)


def packed_columns(low, values, steps):
    pairs = values.shape[0]
    return pl.pallas_call(
        pack_kernel,
        in_specs=[pl.BlockSpec(memory_space=pltpu.SMEM), pl.BlockSpec(memory_space=pltpu.VMEM)],
        out_shape=[jax.ShapeDtypeStruct((pairs, steps, LANES), jnp.float32)] * 2,
        compiler_params=pltpu.CompilerParams(vmem_limit_bytes=VMEM_LIMIT),
    )(low, values)


def finish_kernel(sources, low_ref, swap_ref, table_ref, first_ref, second_ref, ar_ref, half_ref, season_ref, *rest):
    out_ref, misc_ref, flat_ref, slot_ref, turned_ref, innovation_ref, stacked_ref = rest[-7:]
    steps = table_ref.shape[1]
    days = out_ref.shape[0]
    degrees = out_ref.shape[3]
    lane_tiles = degrees // LANES
    width = degrees + LANES
    gather_slots(rest[:sources], flat_ref, slot_ref)
    lane = lax.broadcasted_iota(jnp.int32, (ROWS, LANES), 1)
    degree = lax.broadcasted_iota(jnp.int32, (DAY_ROWS, degrees), 1)
    last_row = lax.broadcasted_iota(jnp.int32, (TILE, 2 * days), 0)
    turn = (
        lax.broadcasted_iota(jnp.int32, (days, days), 0) == lax.broadcasted_iota(jnp.int32, (days, days), 1)
    ).astype(jnp.bfloat16)
    pick_row = lax.broadcasted_iota(jnp.int32, (TILE, LANES), 0)
    pick_lane = lax.broadcasted_iota(jnp.int32, (TILE, LANES), 1)
    pick = (pick_lane == jnp.where(pick_row < 8, pick_row, pick_row + (LANES // 2 - 8))).astype(jnp.bfloat16)
    transposed = (((1,), (1,)), ((), ()))
    other_refs = (first_ref, second_ref)

    for half in range(2):
        stacked_ref[half, :, steps:] = jnp.zeros((2 * days + TILE, width - steps), jnp.float32)

    def one(part_of, step):
        pair = part_of * HALF + step
        low = low_ref[pair]
        other_ref = other_refs[part_of]
        begin = pl.multiple_of(step * degrees, TILE)
        last = jnp.where(last_row == step, other_ref[HALF * degrees :, :].astype(jnp.float32), 0.0)
        last = jnp.where(last_row == 0, jnp.sum(last, axis=0, keepdims=True), 0.0)
        table = table_ref[pair]
        high_sum = jnp.dot(table, slot_ref[2 * pair], preferred_element_type=jnp.float32)
        low_sum = jnp.dot(table, slot_ref[2 * pair + 1], preferred_element_type=jnp.float32)
        for first in range(0, steps, ROWS):
            here = slice(first, first + ROWS)
            row = lax.broadcasted_iota(jnp.int32, (ROWS, 2 * days), 0) + first
            own = jnp.where(row <= low, high_sum[here], low_sum[here])
            count = min(ROWS, degrees - first)
            other = other_ref[pl.ds(begin + first, count), :].astype(jnp.float32)
            if count < ROWS:
                other = jnp.concatenate([other, last], axis=0)
            total = own + other
            ar = ar_ref[pair, here]
            half = half_ref[pair, here]
            shifted_parts = []
            sum_coef = sum_var = 0.0
            for part in range(2):
                spectral = total[:, part * days : (part + 1) * days]
                shifted = pltpu.roll(spectral, 1, 1)
                shifted_parts.append(shifted)
                previous = jnp.where(lane == 0, 0.0, shifted)
                residual = spectral - ar * previous
                innovation_ref[part_of, part, here] = (residual * season_ref[0:1, :] * half).astype(jnp.bfloat16)
                weighted = residual * season_ref[1:2, :]
                sum_coef = sum_coef + weighted * previous
                sum_var = sum_var + weighted * residual
            sum_coef = jnp.sum(sum_coef, axis=1, keepdims=True)
            sum_var = jnp.sum(sum_var, axis=1, keepdims=True)
            misc = jnp.where(
                lane < 2,
                shifted_parts[0],
                jnp.where(lane < 4, pltpu.roll(shifted_parts[1], 2, 1), jnp.where(lane == 4, sum_coef, sum_var)),
            )
            misc_high = misc.astype(jnp.bfloat16).astype(jnp.float32)
            misc_low = pltpu.roll(misc - misc_high, LANES // 2, 1)
            misc = jnp.where(lane < LANES // 2, misc_high, misc_low)
            innovation_ref[part_of, 2, here] = misc.astype(jnp.bfloat16)
        for part in range(3):
            placer = turn if part < 2 else pick
            stacked_ref[part_of, part * days : part * days + placer.shape[0], :steps] = lax.dot_general(
                placer, innovation_ref[part_of, part], transposed, preferred_element_type=jnp.float32
            )
        high = degrees - 1 - low
        swap = swap_ref[pair]
        for shift, start, slot in ((high, high, 2 * pair + swap), (width - 1, low, 2 * pair + 1 - swap)):
            for first in range(0, 2 * days, DAY_ROWS):
                stacked = stacked_ref[part_of, first : first + DAY_ROWS, :]
                placed = jnp.where(degree >= start, pltpu.roll(stacked, shift, 1)[:, :degrees], 0.0)
                part, day = divmod(first, days)
                for t in range(lane_tiles):
                    turned_ref[part, t, pl.ds(day * PITCH + slot, DAY_ROWS, stride=PITCH), :] = placed[
                        :, t * LANES : (t + 1) * LANES
                    ]
            stacked = stacked_ref[part_of, 2 * days :, :]
            placed = jnp.where(degree[:TILE] >= start, pltpu.roll(stacked, shift, 1)[:, :degrees], 0.0)
            misc_ref[slot] = placed[:8] + placed[8:]

    by_halves(one)

    def write(step, carry):
        begin = pl.multiple_of(step * 8 * PITCH, 8)
        for part in range(2):
            for t in range(lane_tiles):
                window = turned_ref.at[part, t, pl.ds(begin, 8 * PITCH)]
                for day in range(8):
                    values = window[day * PITCH : day * PITCH + TILE, :]
                    out_ref[step * 8 + day, part, :, t * LANES : (t + 1) * LANES] = values.astype(jnp.bfloat16)
        return carry

    lax.fori_loop(0, days // 8, write, 0)


def leading(shape, chunk):
    return pl.BlockSpec(shape, lambda i: (chunk,) + (0,) * (len(shape) - 1))


def partial_sums(chunk, place, low, blocks, table, degrees):
    lats, rows, days = blocks[0].shape
    steps, lat_half = table.shape[1:]
    out_rows = HALF * degrees + TILE
    pairs = TILE // 2
    return pl.pallas_call(
        functools.partial(partial_kernel, degrees),
        grid=(1,),
        in_specs=[
            pl.BlockSpec(memory_space=pltpu.SMEM),
            leading((pairs, steps, lat_half), chunk),
        ]
        + [pl.BlockSpec((lats, 2 * TILE, days), lambda i: (0, place, 0)) for _ in blocks],
        out_specs=[leading((out_rows, 2 * days), 0)] * 2,
        out_shape=[jax.ShapeDtypeStruct((out_rows, 2 * days), jnp.bfloat16)] * 2,
        scratch_shapes=[
            pltpu.VMEM((lat_half * PITCH, days), jnp.float32),
            pltpu.VMEM((TILE, lat_half, 2 * days), jnp.bfloat16),
            pltpu.VMEM((2, TILE, 2 * days), jnp.float32),
        ],
        compiler_params=pltpu.CompilerParams(vmem_limit_bytes=VMEM_LIMIT),
    )(low, table, *blocks)


def finish(chunk, low, swap, blocks, table, other, columns, season, held, slot_total, degrees):
    lats, rows, days = blocks[0].shape
    steps, lat_half = table.shape[1:]
    pairs = TILE // 2
    smem = pl.BlockSpec(memory_space=pltpu.SMEM)
    operands = [low, swap, table, *other, *columns, season, *blocks]
    in_specs = [
        smem,
        smem,
        leading((pairs, steps, lat_half), chunk),
        leading(other[0].shape, 0),
        leading(other[1].shape, 0),
        leading((pairs, steps, LANES), chunk),
        leading((pairs, steps, LANES), chunk),
        leading((8, LANES), 0),
    ] + [leading(block.shape, 0) for block in blocks]
    aliases = {}
    if held is not None:
        operands.append(held)
        in_specs.append(pl.BlockSpec(memory_space=pl.ANY))
        aliases = {len(operands) - 1: 0}
    return pl.pallas_call(
        functools.partial(finish_kernel, len(blocks)),
        grid=(1,),
        in_specs=in_specs,
        out_specs=[
            pl.BlockSpec((days, 2, TILE, degrees), lambda i: (0, 0, chunk, 0)),
            leading((TILE, 8, degrees), 0),
        ],
        out_shape=[
            jax.ShapeDtypeStruct((days, 2, slot_total, degrees), jnp.bfloat16),
            jax.ShapeDtypeStruct((TILE, 8, degrees), jnp.float32),
        ],
        input_output_aliases=aliases,
        scratch_shapes=[
            pltpu.VMEM((lat_half * PITCH, days), jnp.float32),
            pltpu.VMEM((TILE, lat_half, 2 * days), jnp.bfloat16),
            pltpu.VMEM((2, degrees // LANES, days * PITCH, LANES), jnp.float32),
            pltpu.VMEM((2, 3, steps, LANES), jnp.bfloat16),
            pltpu.VMEM((2, 2 * days + TILE, degrees + LANES), jnp.float32),
        ],
        compiler_params=pltpu.CompilerParams(vmem_limit_bytes=VMEM_LIMIT),
    )(*operands)


def after(values, waited):
    return lax.optimization_barrier((values, waited))[0]


def per_device(fields, wave_table, day_of_year, ar_coef, log_var):
    band_count = lax.axis_size("band")
    time_count = lax.axis_size("tm")
    band = lax.axis_index("band")
    slot_count, degree_count = ar_coef.shape
    day_count, lat_local, lon_count = fields.shape
    lat_count = lat_local * band_count
    group = band_count // 2
    steps = round_up(degree_count + 1, TILE)
    total_days = day_count * time_count
    slot_pad = round_up(slot_count, TILE)
    chunks = slot_pad // TILE
    pairs = slot_pad // 2
    half_index = band // group
    rank = band % group
    mirror = [(i, (i + group) % band_count) for i in range(band_count)]
    peers = [rank ^ k for k in range(group)]

    fields = fields.transpose(1, 2, 0)

    waves = wave_table.reshape(2, group, slot_count // 2, 2)
    high_low = jnp.stack([waves.max(-1), waves.min(-1)], axis=-1)
    high_low = jnp.pad(high_low, ((0, 0), (0, 0), (0, pairs - slot_count // 2), (0, 0)))
    ordered = high_low.reshape(2, group, slot_pad)
    present = jnp.arange(slot_pad) < slot_count

    def by_peer(side):
        table = lax.dynamic_index_in_dim(ordered, side, 0, keepdims=False)
        return jnp.stack([lax.dynamic_index_in_dim(table, peer, 0, keepdims=False) for peer in peers])

    own_waves, far_waves = by_peer(half_index), by_peer(1 - half_index)
    own_low, far_low = own_waves[0, 1::2], far_waves[0, 1::2]
    lats = jnp.concatenate(
        [(half_index * group + peer) * lat_local + jnp.arange(lat_local, dtype=jnp.int32) for peer in peers]
    )

    def table_of(waves_of, first, count):
        picked = waves_of[:, first * TILE : (first + count) * TILE].reshape(group * count, TILE)
        table = fourier_rows(picked, lon_count)
        if slot_pad != slot_count:
            mask = present[first * TILE : (first + count) * TILE].reshape(count, 1, TILE)
            mask = jnp.broadcast_to(mask, (group, count, 2, TILE)).reshape(-1, 1)
            table = table * mask.astype(jnp.bfloat16)
        return table

    across, along = list(range(group // 2, group)), list(range(1, group // 2))

    def exchange(blocks, order):
        moved = [blocks[0]] + [None] * (group - 1)
        for k in order:
            moved[k] = lax.ppermute(blocks[k], "band", [(i, i ^ k) for i in range(band_count)])
        return moved

    blocks = longitude_sums(fields, table_of(far_waves, 0, 1), 2 * TILE)
    far = [exchange(blocks, across + along)]
    if chunks > 1:
        later = after(fields, blocks[0])
        blocks = longitude_sums(later, table_of(far_waves, 1, chunks - 1), (chunks - 1) * 2 * TILE)
        far.append(exchange(blocks, across[:1] + along + across[1:]))
    far_table = packed_table(after(far_low, blocks[0]), lats, lat_count, degree_count, steps)

    others = []

    def send_sums(chunk, waited):
        low = far_low[chunk * TILE // 2 : (chunk + 1) * TILE // 2]
        sums = partial_sums(chunk, max(chunk - 1, 0), after(low, waited), far[min(chunk, 1)], far_table, degree_count)
        sums = after(sums, others[-1]) if others else sums
        others.append([lax.ppermute(part, "band", mirror) for part in sums])
        return sums

    sums = send_sums(0, blocks[0])

    fields, own_waves, own_low, ar_coef, log_var = after((fields, own_waves, own_low, ar_coef, log_var), sums)
    blocks = longitude_sums(fields, table_of(own_waves, 0, chunks), 2 * TILE)
    own_table = packed_table(after(own_low, blocks[0]), lats, lat_count, degree_count, steps)
    slot_waves = lax.dynamic_slice_in_dim(wave_table, band * slot_count, slot_count)
    pad_slots = (0, slot_pad - slot_count)
    swap = (jnp.pad(slot_waves, pad_slots)[::2] == own_low).astype(jnp.int32)

    def by_pair(values):
        values = jnp.pad(values, (pad_slots, (0, LANES))).reshape(pairs, 2, degree_count + LANES)
        return jnp.where(swap[:, None, None] == 1, values[:, ::-1], values)

    values = jnp.concatenate([by_pair(ar_coef), by_pair(jnp.exp(-0.5 * log_var))], axis=1)
    columns = packed_columns(own_low, jnp.pad(values, ((0, 0), (0, 4), (0, 0))), steps)
    for chunk in range(1, chunks):
        send_sums(chunk, own_table if chunk == 1 else columns[0])

    season = 1.0 + 0.5 * jnp.cos(day_of_year.astype(jnp.float32) * (2.0 * math.pi / 365.0))
    later = (jnp.arange(day_count) > 0).astype(jnp.float32)
    season_rows = jnp.pad(jnp.stack([lax.rsqrt(season), later / season]), ((0, 6), (0, 0)))

    own = [exchange(after(blocks[::chunks], (far[-1], own_table)), across + along)]
    innovation = None
    misc = []
    for chunk in range(chunks):
        if chunk + 1 < chunks:
            own.append(exchange(after(blocks[chunk + 1 :: chunks], (own[-1], misc[:chunk])), across + along))
        span = slice(chunk * TILE // 2, (chunk + 1) * TILE // 2)
        innovation, rows = finish(
            chunk, own_low[span], swap[span], own[chunk], own_table, others[chunk], columns, season_rows,
            innovation, slot_pad, degree_count,
        )
        misc.append(rows)
    innovation = innovation[:, :, :slot_count]
    misc = jnp.concatenate(misc, axis=0)[:slot_count, :6]

    degree_list = jnp.arange(degree_count, dtype=jnp.int32)
    valid_mask = (degree_list[None, :] >= slot_waves[:, None]).astype(jnp.float32)
    edges = misc.transpose(1, 0, 2)
    route = [(i, i + 1) for i in range(time_count - 1)]
    carried = lax.ppermute(edges[0:4:2].astype(jnp.bfloat16), "tm", route).astype(jnp.float32)
    scale = jnp.exp(-0.5 * log_var) * lax.rsqrt(season[0]) * valid_mask
    opening = ((edges[1:4:2] - ar_coef[None] * carried) * scale[None]).astype(jnp.bfloat16)
    innovation = lax.dynamic_update_slice_in_dim(innovation, opening[None], 0, 0)

    column_width = degree_count // time_count
    place = lax.axis_index("tm")
    columns = [misc[:, :, i * column_width : (i + 1) * column_width] for i in range(time_count)]
    moved = lax.all_to_all(jnp.stack(columns).astype(jnp.bfloat16), "tm", 0, 0, tiled=True).astype(jnp.float32)

    def own_columns(values):
        return lax.dynamic_slice_in_dim(values, place * column_width, column_width, 1)

    local_ar, local_var = own_columns(ar_coef), jnp.exp(-own_columns(log_var))
    first_days = day_of_year[0] + (jnp.arange(time_count, dtype=jnp.int32) - place) * day_count
    first_days = (first_days % 365).astype(jnp.float32)
    openness = 1.0 / (1.0 + 0.5 * jnp.cos(first_days * (2.0 * math.pi / 365.0)))
    first = moved[:, :, 1:4:2]
    before = jnp.concatenate([jnp.zeros_like(moved[:1, :, 0:4:2]), moved[:-1, :, 0:4:2]], axis=0)
    residual = first - local_ar[None, :, None] * before
    weighted = residual * openness[:, None, None, None]
    sum_coef = jnp.sum(moved[:, :, 4], axis=0) + jnp.sum(weighted * before, axis=(0, 2))
    sum_var = jnp.sum(moved[:, :, 5], axis=0) + jnp.sum(weighted * residual, axis=(0, 2))
    local_mask = own_columns(valid_mask)
    grad_coef = -local_mask * local_var * sum_coef / (2.0 * total_days)
    grad_var = local_mask * (total_days - 0.5 * local_var * sum_var) / (2.0 * total_days)
    return innovation, grad_coef, grad_var


def solution(mesh):
    in_specs = (P("tm", "band", None), P(), P("tm"), P("band", None), P("band", None))
    out_specs = (P("tm", None, "band", None), P("band", "tm"), P("band", "tm"))
    return jax.shard_map(
        per_device, mesh=mesh, in_specs=in_specs, out_specs=out_specs, check_vma=False
    )
```

profile of v0, /device:TPU:0, one launch (start us, length us, event | category | flops | bytes accessed | tf_op | source)
XLA Modules:
  0.0 359.8 jit_solution(9285817027101493547)
XLA Ops:
  0.7 0.8 reshape.400
  3.4 0.7 pad_maximum_fusion.10
  4.1 2.2 shard_map.76.table_ref
  6.2 16.4 %shard_map.77 = (bf16[88,32,128]{2,1,0:T(8,128)(2,1)}, bf16[88,32,128]{2,1,0:T(8,128)(2,1)}, bf16[88,32,128]{2,1,0:T(8,128)(2,1)}, bf16[88,32,128]{2,1,0:T(8,128)(2,1)}) custom-call(bf16[88,1440,128]{2,1,0:T(8,128)(2,1)} %bitcast.56, bf16[128,1440]{1,0:T(8,128)(2,1)} %shard_map.76.table_ref), custom_call_target="tpu_custom_call" | custom-call | tf_op jit(solution)/shard_map/pallas_call | solution.py:80
  22.6 3.0 collective-permute-start
  25.6 1.6 collective-permute-start.1
  27.9 0.7 pad_maximum_fusion.8
  28.6 0.8 pad_maximum_fusion.6
  29.4 2.9 shard_map.78.table_ref
  32.2 19.1 %shard_map.79 = (bf16[88,64,128]{2,1,0:T(8,128)(2,1)}, bf16[88,64,128]{2,1,0:T(8,128)(2,1)}, bf16[88,64,128]{2,1,0:T(8,128)(2,1)}, bf16[88,64,128]{2,1,0:T(8,128)(2,1)}) custom-call(bf16[88,1440,128]{2,1,0:T(8,128)(2,1)} %bitcast.57, bf16[256,1440]{1,0:T(8,128)(2,1)} %shard_map.78.table_ref), custom_call_target="tpu_custom_call" | custom-call | tf_op jit(solution)/shard_map/pallas_call | solution.py:80
  51.3 1.9 collective-permute-start.3
  53.2 1.6 collective-permute-start.4
  57.3 0.8 dynamic_slice.72
  58.3 0.7 multiply_add_fusion.2
  59.0 0.7 broadcast_in_dim.21.low_ref
  60.9 18.6 %shard_map.80.table_ref = bf16[24,400,352]{2,1,0:T(8,128)(2,1)} custom-call(f32[24,128]{1,0:T(8,128)} %broadcast_in_dim.21.low_ref, f32[24,384]{1,0:T(8,128)} %get-tuple-element.176.first_ref, f32[24,384]{1,0:T(8,128)} %get-tuple-element.175.second_ref, f32[24,384]{1,0:T(8,128)} %broadcast_in_dim.22.cos_ref, f32[24,384]{1,0:T(8,128)} %broadcast_in_dim.23.weight_ref), custom_call_target="tpu_custom_call" | custom-call | tf_op jit(solution)/shard_map/pallas_call | solution.py:193
  79.5 7.2 %shard_map.81 = (bf16[1552,256]{1,0:T(8,128)(2,1)}, bf16[1552,256]{1,0:T(8,128)(2,1)}) custom-call(s32[8]{0:T(128)} %get-tuple-element.67.low_ref, bf16[24,400,352]{2,1,0:T(8,128)(2,1)} %shard_map.80.table_ref, bf16[88,32,128]{2,1,0:T(8,128)(2,1)} %get-tuple-element.64.rest_0_, bf16[88,32,128]{2,1,0:T(8,128)(2,1)} %collective-permute-done.rest_1_, ...), custom_call_target="tpu_custom_call" | custom-call | tf_op jit(solution)/shard_map/pallas_call | solution.py:417
  86.7 3.0 collective-permute-start.6
  89.8 0.9 fusion.13
  90.7 0.7 pad_maximum_fusion.3
  91.4 0.7 pad_maximum_fusion.4
  92.1 0.8 pad_maximum_fusion.2
  92.9 3.6 %shard_map.82.table_ref = bf16[384,1440]{1,0:T(8,128)(2,1)} custom-call(f32[384,128]{1,0:T(8,128)} %bitcast.63, f32[384,128]{1,0:T(8,128)} %bitcast.62, f32[384,128]{1,0:T(8,128)} %bitcast.60, f32[384,128]{1,0:T(8,128)} %bitcast.61), custom_call_target="tpu_custom_call" | custom-call | tf_op jit(solution)/shard_map/pallas_call | solution.py:50
  96.5 21.8 %shard_map.83 = (bf16[88,32,128]{2,1,0:T(8,128)(2,1)}, bf16[88,32,128]{2,1,0:T(8,128)(2,1)}, bf16[88,32,128]{2,1,0:T(8,128)(2,1)}, bf16[88,32,128]{2,1,0:T(8,128...) custom-call(bf16[88,1440,128]{2,1,0:T(8,128)(2,1)} %bitcast.58, ...), custom_call_target="tpu_custom_call" | custom-call | tf_op jit(solution)/shard_map/pallas_call | solution.py:80
  118.4 0.7 multiply_add_fusion
  119.1 0.7 broadcast_in_dim.24.low_ref
  119.8 18.5 %shard_map.84.table_ref = bf16[24,400,352]{2,1,0:T(8,128)(2,1)} custom-call(f32[24,128]{1,0:T(8,128)} %broadcast_in_dim.24.low_ref, f32[24,384]{1,0:T(8,128)} %get-tuple-element.171.first_ref, f32[24,384]{1,0:T(8,128)} %get-tuple-element.170.second_ref, f32[24,384]{1,0:T(8,128)} %broadcast_in_dim.22.cos_ref, f32[24,384]{1,0:T(8,128)} %broadcast_in_dim.23.weight_ref), custom_call_target="tpu_custom_call" | custom-call | tf_op jit(solution)/shard_map/pallas_call | solution.py:193
  138.2 15.1 %collective-permute-done.5.rest_3_ = bf16[88,64,128]{2,1,0:T(8,128)(2,1)} collective-permute-done((bf16[88,64,128]{2,1,0:T(8,128)(2,1)}, bf16[88,64,128]{2,1,0:T(8,128)(2,1)}, u32[]{:S(2)}, u32[]{:S(2)}) %collective-permute-start.5) | collective-permute-done | bytes 1441824 | tf_op jit(solution)/shard_map/ppermute | solution.py:535
  153.4 2.7 collective-permute-start.12
  156.1 1.5 collective-permute-start.14
  159.2 7.4 %shard_map.87 = (bf16[1552,256]{1,0:T(8,128)(2,1)}, bf16[1552,256]{1,0:T(8,128)(2,1)}) custom-call(s32[8]{0:T(128)} %get-tuple-element.88.low_ref, bf16[24,400,352]{2,1,0:T(8,128)(2,1)} %shard_map.80.table_ref, bf16[88,64,128]{2,1,0:T(8,128)(2,1)} %get-tuple-element.66.rest_0_, bf16[88,64,128]{2,1,0:T(8,128)(2,1)} %copy-done, ...), custom_call_target="tpu_custom_call" | custom-call | tf_op jit(solution)/shard_map/pallas_call | solution.py:417
  167.0 2.5 collective-permute-start.9
  169.5 1.8 collective-permute-done.12.rest_1_
  171.4 23.5 %collective-permute-done.13.rest_2_ = bf16[88,32,128]{2,1,0:T(8,128)(2,1)} collective-permute-done((bf16[88,32,128]{2,1,0:T(8,128)(2,1)}, bf16[88,32,128]{2,1,0:T(8,128)(2,1)}, u32[]{:S(2)}, u32[]{:S(2)}) %collective-permute-start.13) | collective-permute-done | bytes 720928 | tf_op jit(solution)/shard_map/ppermute | solution.py:535
  194.9 12.3 %collective-permute-done.14.rest_3_ = bf16[88,32,128]{2,1,0:T(8,128)(2,1)} collective-permute-done((bf16[88,32,128]{2,1,0:T(8,128)(2,1)}, bf16[88,32,128]{2,1,0:T(8,128)(2,1)}, u32[]{:S(2)}, u32[]{:S(2)}) %collective-permute-start.14) | collective-permute-done | bytes 720928 | tf_op jit(solution)/shard_map/ppermute | solution.py:535
  207.2 1.9 collective-permute-start.15
  209.1 1.5 collective-permute-start.17
  210.8 0.9 select_maximum_fusion.in_ref
  211.7 11.4 %shard_map.85 = (f32[24,400,128]{2,1,0:T(8,128)}, f32[24,400,128]{2,1,0:T(8,128)}) custom-call(s32[24]{0:T(128)} %bitcast.75, f32[24,8,512]{2,1,0:T(8,128)} %select_maximum_fusion.in_ref), custom_call_target="tpu_custom_call" | custom-call | tf_op jit(solution)/shard_map/pallas_call | solution.py:298
  223.1 1.4 fusion.92
  224.5 7.5 %shard_map.86 = (bf16[1552,256]{1,0:T(8,128)(2,1)}, bf16[1552,256]{1,0:T(8,128)(2,1)}) custom-call(s32[8]{0:T(128)} %get-tuple-element.82.low_ref, bf16[24,400,352]{2,1,0:T(8,128)(2,1)} %shard_map.80.table_ref, bf16[88,64,128]{2,1,0:T(8,128)(2,1)} %get-tuple-element.66.rest_0_, bf16[88,64,128]{2,1,0:T(8,128)(2,1)} %copy-done, ...), custom_call_target="tpu_custom_call" | custom-call | tf_op jit(solution)/shard_map/pallas_call | solution.py:417
  232.0 4.6 %collective-permute-done.9.second_ref = bf16[1552,256]{1,0:T(8,128)(2,1)S(1)} collective-permute-done((bf16[1552,256]{1,0:T(8,128)(2,1)}, bf16[1552,256]{1,0:T(8,128)(2,1)S(1)}, u32[]{:S(2)}, u32[]{:S(2)}) %collective-permute-start.9) | collective-permute-done | bytes 794656 | tf_op jit(solution)/shard_map/ppermute | solution.py:552
  236.7 2.9 collective-permute-start.11
  239.6 0.7 fusion.91
  240.2 19.2 %shard_map.88 = (bf16[128,2,48,384]{3,2,1,0:T(8,128)(2,1)}, f32[16,8,384]{2,1,0:T(8,128)}) custom-call(s32[8]{0:T(128)} %get-tuple-element.183.low_ref, s32[8]{0:T(128)} %get-tuple-element.180.swap_ref, bf16[24,400,352]{2,1,0:T(8,128)(2,1)} %shard_map.84.table_ref, bf16[1552,256]{1,0:T(8,128)(2,1)} %collective-permute-done.6.first_ref, ...), custom_call_target="tpu_custom_call" | custom-call | tf_op jit(solution)/shard_map/pallas_call | solution.py:457
  259.5 0.9 copy-done.6
  260.4 0.9 copy-done.7
  261.3 9.6 %collective-permute-done.17.rest_3_ = bf16[88,32,128]{2,1,0:T(8,128)(2,1)S(1)} collective-permute-done((bf16[88,32,128]{2,1,0:T(8,128)(2,1)S(1)}, bf16[88,32,128]{2,1,0:T(8,128)(2,1)S(1)}, u32[]{:S(2)}, u32[]{:S(2)}) %collective-permute-start.17) | collective-permute-done | bytes 720928 | tf_op jit(solution)/shard_map/ppermute | solution.py:535
  270.8 0.9 copy-done.8
  272.0 3.2 collective-permute-start.20
  275.5 0.9 constant_dynamic-update-slice_fusion.2
  276.4 19.3 %shard_map.89 = (bf16[128,2,48,384]{3,2,1,0:T(8,128)(2,1)}, f32[16,8,384]{2,1,0:T(8,128)}) custom-call(s32[8]{0:T(128)} %get-tuple-element.182.low_ref, s32[8]{0:T(128)} %get-tuple-element.179.swap_ref, bf16[24,400,352]{2,1,0:T(8,128)(2,1)} %shard_map.84.table_ref, bf16[1552,256]{1,0:T(8,128)(2,1)} %copy-done.2, ...), custom_call_target="tpu_custom_call", output_to_operand_aliasing={{0}: (12, {})} | custom-call | tf_op jit(solution)/shard_map/pallas_call | solution.py:457
  295.7 0.9 constant_dynamic-update-slice_fusion.1
  296.6 9.1 %collective-permute-done.11.second_ref = bf16[1552,256]{1,0:T(8,128)(2,1)S(1)} collective-permute-done((bf16[1552,256]{1,0:T(8,128)(2,1)}, bf16[1552,256]{1,0:T(8,128)(2,1)S(1)}, u32[]{:S(2)}, u32[]{:S(2)}) %collective-permute-start.11) | collective-permute-done | bytes 794656 | tf_op jit(solution)/shard_map/ppermute | solution.py:552
  305.8 4.3 %collective-permute-done.19.rest_2_ = bf16[88,32,128]{2,1,0:T(8,128)(2,1)S(1)} collective-permute-done((bf16[88,32,128]{2,1,0:T(8,128)(2,1)}, bf16[88,32,128]{2,1,0:T(8,128)(2,1)S(1)}, u32[]{:S(2)}, u32[]{:S(2)}) %collective-permute-start.19) | collective-permute-done | bytes 720928 | tf_op jit(solution)/shard_map/ppermute | solution.py:535
  310.1 13.9 %collective-permute-done.20.rest_3_ = bf16[88,32,128]{2,1,0:T(8,128)(2,1)} collective-permute-done((bf16[88,32,128]{2,1,0:T(8,128)(2,1)}, bf16[88,32,128]{2,1,0:T(8,128)(2,1)}, u32[]{:S(2)}, u32[]{:S(2)}) %collective-permute-start.20) | collective-permute-done | bytes 720928 | tf_op jit(solution)/shard_map/ppermute | solution.py:535
  324.1 19.3 %shard_map.90 = (bf16[128,2,48,384]{3,2,1,0:T(8,128)(2,1)}, f32[16,8,384]{2,1,0:T(8,128)}) custom-call(s32[8]{0:T(128)} %get-tuple-element.184.low_ref, s32[8]{0:T(128)} %get-tuple-element.181.swap_ref, bf16[24,400,352]{2,1,0:T(8,128)(2,1)} %shard_map.84.table_ref, bf16[1552,256]{1,0:T(8,128)(2,1)} %copy-done.4, ...), custom_call_target="tpu_custom_call", output_to_operand_aliasing={{0}: (12, {})} | custom-call | tf_op jit(solution)/shard_map/pallas_call | solution.py:457
  343.4 0.9 constant_dynamic-update-slice_fusion
  345.0 0.7 slice.128
  345.7 1.3 collective-permute-start.21
  347.3 0.8 copy.17
  348.1 3.6 %all-to-all-start = ((bf16[4,48,6,96]{3,1,2,0:T(8,128)(2,1)}), bf16[4,48,6,96]{3,1,2,0:T(8,128)(2,1)S(1)}, u32[]{:S(2)}, u32[]{:S(2)}) async-start(bf16[4,48,6,96]{3,1,2,0:T(8,128)(2,1)} %copy.17), calls=%async_computation | async-start | bytes 589824 | tf_op jit(solution)/shard_map/all_to_all | solution.py:604
  352.4 5.6 %all-to-all-done = bf16[4,48,6,96]{3,1,2,0:T(8,128)(2,1)S(1)} async-done(((bf16[4,48,6,96]{3,1,2,0:T(8,128)(2,1)}), bf16[4,48,6,96]{3,1,2,0:T(8,128)(2,1)S(1)}, u32[]{:S(2)}, u32[]{:S(2)}) %all-to-all-start) | async-done | bytes 221216 | tf_op jit(solution)/shard_map/all_to_all | solution.py:604
  358.3 1.5 fusion.47
  (111 shorter events, 11.4 us)
Async XLA Ops:
  22.6 34.4 %collective-permute-start = (bf16[88,32,128]{2,1,0:T(8,128)(2,1)}, bf16[88,32,128]{2,1,0:T(8,128)(2,1)}, u32[]{:S(2)}, u32[]{:S(2)}) collective-permute-start(bf16[88,32,128]{2,1,0:T(8,128)(2,1)} %get-tuple-element.69), channel_id=1, source_target_pairs={{0,4},{4,0},{8,12},{12,8},{16,20},{20,16},{24,28},{28,24},{1,5},{5... | collective-permute-start | bytes 2162696 | tf_op jit(solution)/shard_map/ppermute | solution.py:535
  25.6 53.9 %collective-permute-start.1 = (bf16[88,32,128]{2,1,0:T(8,128)(2,1)}, bf16[88,32,128]{2,1,0:T(8,128)(2,1)}, u32[]{:S(2)}, u32[]{:S(2)}) collective-permute-start(bf16[88,32,128]{2,1,0:T(8,128)(2,1)} %get-tuple-element.70), channel_id=1, source_target_pairs={{0,8},{4,12},{8,0},{12,4},{16,24},{20,28},{24,16},{28,20},{1,9},{5... | collective-permute-start | bytes 2162696 | tf_op jit(solution)/shard_map/ppermute | solution.py:535
  27.2 52.4 %collective-permute-start.2 = (bf16[88,32,128]{2,1,0:T(8,128)(2,1)}, bf16[88,32,128]{2,1,0:T(8,128)(2,1)}, u32[]{:S(2)}, u32[]{:S(2)}) collective-permute-start(bf16[88,32,128]{2,1,0:T(8,128)(2,1)} %get-tuple-element.71), channel_id=1, source_target_pairs={{0,12},{4,8},{8,4},{12,0},{16,28},{20,24},{24,20},{28,16},{1,13},{... | collective-permute-start | bytes 2162696 | tf_op jit(solution)/shard_map/ppermute | solution.py:535
  32.2 24.9 %copy-start.17 = (s32[128]{0:T(128)S(1)}, s32[128]{0:T(128)}, u32[]{:S(2)}) copy-start(s32[128]{0:T(128)} %param.7) | copy-start | bytes 1540
  51.3 86.9 %collective-permute-start.3 = (bf16[88,64,128]{2,1,0:T(8,128)(2,1)}, bf16[88,64,128]{2,1,0:T(8,128)(2,1)S(1)}, u32[]{:S(2)}, u32[]{:S(2)}) collective-permute-start(bf16[88,64,128]{2,1,0:T(8,128)(2,1)} %get-tuple-element.83), channel_id=1, source_target_pairs={{0,4},{4,0},{8,12},{12,8},{16,20},{20,16},{24,28},{28,24},{1,5},{5... | collective-permute-start | bytes 4325384 | tf_op jit(solution)/shard_map/ppermute | solution.py:535
  53.2 85.0 %collective-permute-start.4 = (bf16[88,64,128]{2,1,0:T(8,128)(2,1)}, bf16[88,64,128]{2,1,0:T(8,128)(2,1)S(1)}, u32[]{:S(2)}, u32[]{:S(2)}) collective-permute-start(bf16[88,64,128]{2,1,0:T(8,128)(2,1)} %get-tuple-element.84), channel_id=1, source_target_pairs={{0,8},{4,12},{8,0},{12,4},{16,24},{20,28},{24,16},{28,20},{1,9},{5... | collective-permute-start | bytes 4325384 | tf_op jit(solution)/shard_map/ppermute | solution.py:535
  57.1 96.3 %collective-permute-start.5 = (bf16[88,64,128]{2,1,0:T(8,128)(2,1)}, bf16[88,64,128]{2,1,0:T(8,128)(2,1)}, u32[]{:S(2)}, u32[]{:S(2)}) collective-permute-start(bf16[88,64,128]{2,1,0:T(8,128)(2,1)} %get-tuple-element.85), channel_id=1, source_target_pairs={{0,12},{4,8},{8,4},{12,0},{16,28},{20,24},{24,20},{28,16},{1,13},{... | collective-permute-start | bytes 4325384 | tf_op jit(solution)/shard_map/ppermute | solution.py:535
  57.3 112.2 %copy-start.13 = (s32[1,24]{1,0:T(1,128)}, s32[1,24]{1,0:T(1,128)S(1)}, u32[]{:S(2)}) copy-start(s32[1,24]{1,0:T(1,128)S(1)} %slice.107) | copy-start | bytes 292
  86.7 79.8 %collective-permute-start.6 = (bf16[1552,256]{1,0:T(8,128)(2,1)}, bf16[1552,256]{1,0:T(8,128)(2,1)}, u32[]{:S(2)}, u32[]{:S(2)}) collective-permute-start(bf16[1552,256]{1,0:T(8,128)(2,1)} %get-tuple-element.72), channel_id=1, source_target_pairs={{0,16},{4,20},{8,24},{12,28},{16,0},{20,4},{24,8},{28,12},{1,17},{... | collective-permute-start | bytes 2383880 | tf_op jit(solution)/shard_map/ppermute | solution.py:552
  89.7 76.9 %collective-permute-start.7 = (bf16[1552,256]{1,0:T(8,128)(2,1)}, bf16[1552,256]{1,0:T(8,128)(2,1)}, u32[]{:S(2)}, u32[]{:S(2)}) collective-permute-start(bf16[1552,256]{1,0:T(8,128)(2,1)} %get-tuple-element.73), channel_id=1, source_target_pairs={{0,16},{4,20},{8,24},{12,28},{16,0},{20,4},{24,8},{28,12},{1,17},{... | collective-permute-start | bytes 2383880 | tf_op jit(solution)/shard_map/ppermute | solution.py:552
  118.2 40.0 %copy-start.11 = (f32[48,384]{1,0:T(8,128)S(1)}, f32[48,384]{1,0:T(8,128)}, u32[]{:S(2)}) copy-start(f32[48,384]{1,0:T(8,128)} %param.8) | copy-start | bytes 221188
  118.2 40.4 %copy-start.12 = (f32[48,384]{1,0:T(8,128)S(1)}, f32[48,384]{1,0:T(8,128)}, u32[]{:S(2)}) copy-start(f32[48,384]{1,0:T(8,128)} %param.9) | copy-start | bytes 221188
  138.2 20.9 %copy-start = (bf16[88,64,128]{2,1,0:T(8,128)(2,1)}, bf16[88,64,128]{2,1,0:T(8,128)(2,1)S(1)}, u32[]{:S(2)}) copy-start(bf16[88,64,128]{2,1,0:T(8,128)(2,1)S(1)} %collective-permute-done.3.rest_1_) | copy-start | bytes 4325380
  138.2 20.9 %copy-start.1 = (bf16[88,64,128]{2,1,0:T(8,128)(2,1)}, bf16[88,64,128]{2,1,0:T(8,128)(2,1)S(1)}, u32[]{:S(2)}) copy-start(bf16[88,64,128]{2,1,0:T(8,128)(2,1)S(1)} %collective-permute-done.4.rest_2_) | copy-start | bytes 4325380
  153.4 18.0 %collective-permute-start.12 = (bf16[88,32,128]{2,1,0:T(8,128)(2,1)}, bf16[88,32,128]{2,1,0:T(8,128)(2,1)}, u32[]{:S(2)}, u32[]{:S(2)}) collective-permute-start(bf16[88,32,128]{2,1,0:T(8,128)(2,1)} %get-tuple-element.108), channel_id=1, source_target_pairs={{0,4},{4,0},{8,12},{12,8},{16,20},{20,16},{24,28},{28,24},{1,5},{5... | collective-permute-start | bytes 2162696 | tf_op jit(solution)/shard_map/ppermute | solution.py:535
  156.1 38.8 %collective-permute-start.13 = (bf16[88,32,128]{2,1,0:T(8,128)(2,1)}, bf16[88,32,128]{2,1,0:T(8,128)(2,1)}, u32[]{:S(2)}, u32[]{:S(2)}) collective-permute-start(bf16[88,32,128]{2,1,0:T(8,128)(2,1)} %get-tuple-element.109), channel_id=1, source_target_pairs={{0,8},{4,12},{8,0},{12,4},{16,24},{20,28},{24,16},{28,20},{1,9},{5... | collective-permute-start | bytes 2162696 | tf_op jit(solution)/shard_map/ppermute | solution.py:535
  156.1 51.1 %collective-permute-start.14 = (bf16[88,32,128]{2,1,0:T(8,128)(2,1)}, bf16[88,32,128]{2,1,0:T(8,128)(2,1)}, u32[]{:S(2)}, u32[]{:S(2)}) collective-permute-start(bf16[88,32,128]{2,1,0:T(8,128)(2,1)} %get-tuple-element.110), channel_id=1, source_target_pairs={{0,12},{4,8},{8,4},{12,0},{16,28},{20,24},{24,20},{28,16},{1,13},{... | collective-permute-start | bytes 2162696 | tf_op jit(solution)/shard_map/ppermute | solution.py:535
  159.2 48.0 %copy-start.16 = (bf16[88,32,128]{2,1,0:T(8,128)(2,1)S(1)}, bf16[88,32,128]{2,1,0:T(8,128)(2,1)}, u32[]{:S(2)}) copy-start(bf16[88,32,128]{2,1,0:T(8,128)(2,1)} %get-tuple-element.112) | copy-start | bytes 2162692
  159.2 49.9 %copy-start.15 = (bf16[88,32,128]{2,1,0:T(8,128)(2,1)S(1)}, bf16[88,32,128]{2,1,0:T(8,128)(2,1)}, u32[]{:S(2)}) copy-start(bf16[88,32,128]{2,1,0:T(8,128)(2,1)} %get-tuple-element.113) | copy-start | bytes 2162692
  159.2 49.9 %copy-start.14 = (bf16[88,32,128]{2,1,0:T(8,128)(2,1)S(1)}, bf16[88,32,128]{2,1,0:T(8,128)(2,1)}, u32[]{:S(2)}) copy-start(bf16[88,32,128]{2,1,0:T(8,128)(2,1)} %get-tuple-element.114) | copy-start | bytes 2162692
  166.5 65.5 %collective-permute-start.8 = (bf16[1552,256]{1,0:T(8,128)(2,1)}, bf16[1552,256]{1,0:T(8,128)(2,1)S(1)}, u32[]{:S(2)}, u32[]{:S(2)}) collective-permute-start(bf16[1552,256]{1,0:T(8,128)(2,1)} %get-tuple-element.91), channel_id=1, source_target_pairs={{0,16},{4,20},{8,24},{12,28},{16,0},{20,4},{24,8},{28,12},{1,17},{... | collective-permute-start | bytes 2383880 | tf_op jit(solution)/shard_map/ppermute | solution.py:552
  167.0 69.7 %collective-permute-start.9 = (bf16[1552,256]{1,0:T(8,128)(2,1)}, bf16[1552,256]{1,0:T(8,128)(2,1)S(1)}, u32[]{:S(2)}, u32[]{:S(2)}) collective-permute-start(bf16[1552,256]{1,0:T(8,128)(2,1)} %get-tuple-element.92), channel_id=1, source_target_pairs={{0,16},{4,20},{8,24},{12,28},{16,0},{20,4},{24,8},{28,12},{1,17},{... | collective-permute-start | bytes 2383880 | tf_op jit(solution)/shard_map/ppermute | solution.py:552
  207.2 52.3 %collective-permute-start.15 = (bf16[88,32,128]{2,1,0:T(8,128)(2,1)S(1)}, bf16[88,32,128]{2,1,0:T(8,128)(2,1)S(1)}, u32[]{:S(2)}, u32[]{:S(2)}) collective-permute-start(bf16[88,32,128]{2,1,0:T(8,128)(2,1)S(1)} %copy-done.16), channel_id=1, source_target_pairs={{0,4},{4,0},{8,12},{12,8},{16,20},{20,16},{24,28},{28,24},{1,5},{5... | collective-permute-start | bytes 2162696 | tf_op jit(solution)/shard_map/ppermute | solution.py:535
  209.1 51.3 %collective-permute-start.16 = (bf16[88,32,128]{2,1,0:T(8,128)(2,1)S(1)}, bf16[88,32,128]{2,1,0:T(8,128)(2,1)S(1)}, u32[]{:S(2)}, u32[]{:S(2)}) collective-permute-start(bf16[88,32,128]{2,1,0:T(8,128)(2,1)S(1)} %copy-done.15), channel_id=1, source_target_pairs={{0,8},{4,12},{8,0},{12,4},{16,24},{20,28},{24,16},{28,20},{1,9},{5... | collective-permute-start | bytes 2162696 | tf_op jit(solution)/shard_map/ppermute | solution.py:535
  209.1 61.7 %collective-permute-start.17 = (bf16[88,32,128]{2,1,0:T(8,128)(2,1)S(1)}, bf16[88,32,128]{2,1,0:T(8,128)(2,1)S(1)}, u32[]{:S(2)}, u32[]{:S(2)}) collective-permute-start(bf16[88,32,128]{2,1,0:T(8,128)(2,1)S(1)} %copy-done.14), channel_id=1, source_target_pairs={{0,12},{4,8},{8,4},{12,0},{16,28},{20,24},{24,20},{28,16},{1,13},{... | collective-permute-start | bytes 2162696 | tf_op jit(solution)/shard_map/ppermute | solution.py:535
  232.0 27.5 %copy-start.2 = (bf16[1552,256]{1,0:T(8,128)(2,1)}, bf16[1552,256]{1,0:T(8,128)(2,1)S(1)}, u32[]{:S(2)}) copy-start(bf16[1552,256]{1,0:T(8,128)(2,1)S(1)} %collective-permute-done.8.first_ref) | copy-start | bytes 2383876
  236.7 22.8 %copy-start.3 = (bf16[1552,256]{1,0:T(8,128)(2,1)}, bf16[1552,256]{1,0:T(8,128)(2,1)S(1)}, u32[]{:S(2)}) copy-start(bf16[1552,256]{1,0:T(8,128)(2,1)S(1)} %collective-permute-done.9.second_ref) | copy-start | bytes 2383876
  236.7 60.0 %collective-permute-start.10 = (bf16[1552,256]{1,0:T(8,128)(2,1)}, bf16[1552,256]{1,0:T(8,128)(2,1)S(1)}, u32[]{:S(2)}, u32[]{:S(2)}) collective-permute-start(bf16[1552,256]{1,0:T(8,128)(2,1)} %get-tuple-element.93), channel_id=1, source_target_pairs={{0,16},{4,20},{8,24},{12,28},{16,0},{20,4},{24,8},{28,12},{1,17},{... | collective-permute-start | bytes 2383880 | tf_op jit(solution)/shard_map/ppermute | solution.py:552
  236.7 69.1 %collective-permute-start.11 = (bf16[1552,256]{1,0:T(8,128)(2,1)}, bf16[1552,256]{1,0:T(8,128)(2,1)S(1)}, u32[]{:S(2)}, u32[]{:S(2)}) collective-permute-start(bf16[1552,256]{1,0:T(8,128)(2,1)} %get-tuple-element.94), channel_id=1, source_target_pairs={{0,16},{4,20},{8,24},{12,28},{16,0},{20,4},{24,8},{28,12},{1,17},{... | collective-permute-start | bytes 2383880 | tf_op jit(solution)/shard_map/ppermute | solution.py:552
  259.5 0.9 copy-start.6
  260.4 0.9 copy-start.7
  270.8 0.9 copy-start.8
  271.7 34.1 %collective-permute-start.18 = (bf16[88,32,128]{2,1,0:T(8,128)(2,1)}, bf16[88,32,128]{2,1,0:T(8,128)(2,1)S(1)}, u32[]{:S(2)}, u32[]{:S(2)}) collective-permute-start(bf16[88,32,128]{2,1,0:T(8,128)(2,1)} %get-tuple-element.117), channel_id=1, source_target_pairs={{0,4},{4,0},{8,12},{12,8},{16,20},{20,16},{24,28},{28,24},{1,5},{5... | collective-permute-start | bytes 2162696 | tf_op jit(solution)/shard_map/ppermute | solution.py:535
  272.0 38.1 %collective-permute-start.19 = (bf16[88,32,128]{2,1,0:T(8,128)(2,1)}, bf16[88,32,128]{2,1,0:T(8,128)(2,1)S(1)}, u32[]{:S(2)}, u32[]{:S(2)}) collective-permute-start(bf16[88,32,128]{2,1,0:T(8,128)(2,1)} %get-tuple-element.118), channel_id=1, source_target_pairs={{0,8},{4,12},{8,0},{12,4},{16,24},{20,28},{24,16},{28,20},{1,9},{5... | collective-permute-start | bytes 2162696 | tf_op jit(solution)/shard_map/ppermute | solution.py:535
  272.0 52.0 %collective-permute-start.20 = (bf16[88,32,128]{2,1,0:T(8,128)(2,1)}, bf16[88,32,128]{2,1,0:T(8,128)(2,1)}, u32[]{:S(2)}, u32[]{:S(2)}) collective-permute-start(bf16[88,32,128]{2,1,0:T(8,128)(2,1)} %get-tuple-element.119), channel_id=1, source_target_pairs={{0,12},{4,8},{8,4},{12,0},{16,28},{20,24},{24,20},{28,16},{1,13},{... | collective-permute-start | bytes 2162696 | tf_op jit(solution)/shard_map/ppermute | solution.py:535
  296.6 27.4 %copy-start.4 = (bf16[1552,256]{1,0:T(8,128)(2,1)}, bf16[1552,256]{1,0:T(8,128)(2,1)S(1)}, u32[]{:S(2)}) copy-start(bf16[1552,256]{1,0:T(8,128)(2,1)S(1)} %collective-permute-done.10.first_ref) | copy-start | bytes 2383876
  305.8 18.3 %copy-start.5 = (bf16[1552,256]{1,0:T(8,128)(2,1)}, bf16[1552,256]{1,0:T(8,128)(2,1)S(1)}, u32[]{:S(2)}) copy-start(bf16[1552,256]{1,0:T(8,128)(2,1)S(1)} %collective-permute-done.11.second_ref) | copy-start | bytes 2383876
  305.8 18.3 %copy-start.9 = (bf16[88,32,128]{2,1,0:T(8,128)(2,1)}, bf16[88,32,128]{2,1,0:T(8,128)(2,1)S(1)}, u32[]{:S(2)}) copy-start(bf16[88,32,128]{2,1,0:T(8,128)(2,1)S(1)} %collective-permute-done.18.rest_1_) | copy-start | bytes 2162692
  310.1 14.0 %copy-start.10 = (bf16[88,32,128]{2,1,0:T(8,128)(2,1)}, bf16[88,32,128]{2,1,0:T(8,128)(2,1)S(1)}, u32[]{:S(2)}) copy-start(bf16[88,32,128]{2,1,0:T(8,128)(2,1)S(1)} %collective-permute-done.19.rest_2_) | copy-start | bytes 2162692
  345.7 6.0 %collective-permute-start.21 = (bf16[2,48,384]{2,0,1:T(2,128)(2,1)S(1)}, bf16[2,48,384]{2,0,1:T(2,128)(2,1)S(1)}, u32[]{:S(2)}, u32[]{:S(2)}) collective-permute-start(bf16[2,48,384]{2,0,1:T(2,128)(2,1)S(1)} %slice.128), channel_id=1, source_target_pairs={{0,1},{1,2},{2,3},{4,5},{5,6},{6,7},{8,9},{9,10},{10,11},{12,13},{... | collective-permute-start | bytes 221192 | tf_op jit(solution)/shard_map/ppermute | solution.py:596
  348.1 10.0 %all-to-all-start = ((bf16[4,48,6,96]{3,1,2,0:T(8,128)(2,1)}), bf16[4,48,6,96]{3,1,2,0:T(8,128)(2,1)S(1)}, u32[]{:S(2)}, u32[]{:S(2)}) async-start(bf16[4,48,6,96]{3,1,2,0:T(8,128)(2,1)} %copy.17), calls=%async_computation | async-start | bytes 589824 | tf_op jit(solution)/shard_map/all_to_all | solution.py:604
where the time goes:
time: 362 us; the launch traced here: 360 us
  Pallas kernels  194 us (54%)
  waiting for transfers between devices  100 us (28%)
  starting transfers between devices  33.1 us (9%)
  local copies, waits for them, and re-layouts  18.5 us (5%)
  other arithmetic  12.9 us (4%)
    ppermute x15, waiting for transfers between devices, exchange(): lax.ppermute(blocks[k], 'band', [(i, i ^ k) for i in range(band_count)])  80.6 us
    pallas_call x3, Pallas kernels, finish(): pl.pallas_call(functools.partial(finish_kernel, len(blocks)), grid=(1,),...  57.8 us
    pallas_call x3, Pallas kernels, longitude_sums(): pl.pallas_call(transform_kernel, grid=(lats // group,), in_specs=[pl.Bloc...  57.2 us
    pallas_call x2, Pallas kernels, packed_table(): pl.pallas_call(functools.partial(table_kernel, steps, lane_tiles, top), o...  37.1 us
    pallas_call x3, Pallas kernels, partial_sums(): pl.pallas_call(functools.partial(partial_kernel, degrees), grid=(1,), in_...  22 us
    ppermute x15, starting transfers between devices, exchange(): lax.ppermute(blocks[k], 'band', [(i, i ^ k) for i in range(band_count)])  19.3 us
    ppermute x6, waiting for transfers between devices, send_sums(): others.append([lax.ppermute(part, 'band', mirror) for part in sums])  13.8 us
    pallas_call x1, Pallas kernels, packed_columns(): pl.pallas_call(pack_kernel, in_specs=[pl.BlockSpec(memory_space=pltpu.SME...  11.4 us
  transfers between devices with their start and end apart: 23, of which 10 were waited for; matrix products, arithmetic and copies ran while one was open for 6% of the time, Pallas kernels for 43%

commit v1 on v0

--- a/solution.py
+++ b/solution.py
@@ -527,7 +527,8 @@
             table = table * mask.astype(jnp.bfloat16)
         return table
 
-    across, along = list(range(group // 2, group)), list(range(1, group // 2))
+    across = list(range(group // 2, group))
+    order = across[:0:-1] + list(range(1, group // 2)) + across[:1]
 
     def exchange(blocks, order):
         moved = [blocks[0]] + [None] * (group - 1)
@@ -536,11 +537,11 @@
         return moved
 
     blocks = longitude_sums(fields, table_of(far_waves, 0, 1), 2 * TILE)
-    far = [exchange(blocks, across + along)]
+    far = [exchange(blocks, order)]
     if chunks > 1:
         later = after(fields, blocks[0])
         blocks = longitude_sums(later, table_of(far_waves, 1, chunks - 1), (chunks - 1) * 2 * TILE)
-        far.append(exchange(blocks, across[:1] + along + across[1:]))
+        far.append(exchange(blocks, order))
     far_table = packed_table(after(far_low, blocks[0]), lats, lat_count, degree_count, steps)
 
     others = []
@@ -574,12 +575,13 @@
     later = (jnp.arange(day_count) > 0).astype(jnp.float32)
     season_rows = jnp.pad(jnp.stack([lax.rsqrt(season), later / season]), ((0, 6), (0, 0)))
 
-    own = [exchange(after(blocks[::chunks], (far[-1], own_table)), across + along)]
+    own = [exchange(after(blocks[::chunks], ([far[-1][k] for k in across], own_table)), order)]
     innovation = None
     misc = []
     for chunk in range(chunks):
         if chunk + 1 < chunks:
-            own.append(exchange(after(blocks[chunk + 1 :: chunks], (own[-1], misc[:chunk])), across + along))
+            crossed = own[-1]
+            own.append(exchange(after(blocks[chunk + 1 :: chunks], (crossed, misc[:chunk])), order))
         span = slice(chunk * TILE // 2, (chunk + 1) * TILE // 2)
         innovation, rows = finish(
             chunk, own_low[span], swap[span], own[chunk], own_table, others[chunk], columns, season_rows,

time: 362 us -> 362 us (level)
  no operation moved by 1% of the time
where the time goes in v1:
time: 362 us; the launch traced here: 360 us
  Pallas kernels  194 us (54%)
  waiting for transfers between devices  100 us (28%)
  starting transfers between devices  33.1 us (9%)
  local copies, waits for them, and re-layouts  18.5 us (5%)
  other arithmetic  12.9 us (4%)
    ppermute x15, waiting for transfers between devices, exchange(): lax.ppermute(blocks[k], 'band', [(i, i ^ k) for i in range(band_count)])  80.6 us
    pallas_call x3, Pallas kernels, finish(): pl.pallas_call(functools.partial(finish_kernel, len(blocks)), grid=(1,),...  57.8 us
    pallas_call x3, Pallas kernels, longitude_sums(): pl.pallas_call(transform_kernel, grid=(lats // group,), in_specs=[pl.Bloc...  57.2 us
    pallas_call x2, Pallas kernels, packed_table(): pl.pallas_call(functools.partial(table_kernel, steps, lane_tiles, top), o...  37.1 us
    pallas_call x3, Pallas kernels, partial_sums(): pl.pallas_call(functools.partial(partial_kernel, degrees), grid=(1,), in_...  22 us
    ppermute x15, starting transfers between devices, exchange(): lax.ppermute(blocks[k], 'band', [(i, i ^ k) for i in range(band_count)])  19.3 us
    ppermute x6, waiting for transfers between devices, send_sums(): others.append([lax.ppermute(part, 'band', mirror) for part in sums])  13.8 us
    pallas_call x1, Pallas kernels, packed_columns(): pl.pallas_call(pack_kernel, in_specs=[pl.BlockSpec(memory_space=pltpu.SME...  11.4 us
  transfers between devices with their start and end apart: 23, of which 10 were waited for; matrix products, arithmetic and copies ran while one was open for 6% of the time, Pallas kernels for 43%

profile of v1, /device:TPU:0, one launch (start us, length us, event | category | flops | bytes accessed | tf_op | source)
XLA Modules:
  0.0 359.8 jit_solution(1148137676718383885)
XLA Ops:
  0.7 0.8 reshape.400
  3.4 0.7 pad_maximum_fusion.10
  4.1 2.2 shard_map.76.table_ref
  6.2 16.4 %shard_map.77 = (bf16[88,32,128]{2,1,0:T(8,128)(2,1)}, bf16[88,32,128]{2,1,0:T(8,128)(2,1)}, bf16[88,32,128]{2,1,0:T(8,128)(2,1)}, bf16[88,32,128]{2,1,0:T(8,128)(2,1)}) custom-call(bf16[88,1440,128]{2,1,0:T(8,128)(2,1)} %bitcast.56, bf16[128,1440]{1,0:T(8,128)(2,1)} %shard_map.76.table_ref), custom_call_target="tpu_custom_call" | custom-call | tf_op jit(solution)/shard_map/pallas_call | solution.py:80
  22.6 3.0 collective-permute-start
  25.6 1.6 collective-permute-start.1
  27.9 0.7 pad_maximum_fusion.8
  28.6 0.8 pad_maximum_fusion.6
  29.4 2.9 shard_map.78.table_ref
  32.2 19.1 %shard_map.79 = (bf16[88,64,128]{2,1,0:T(8,128)(2,1)}, bf16[88,64,128]{2,1,0:T(8,128)(2,1)}, bf16[88,64,128]{2,1,0:T(8,128)(2,1)}, bf16[88,64,128]{2,1,0:T(8,128)(2,1)}) custom-call(bf16[88,1440,128]{2,1,0:T(8,128)(2,1)} %bitcast.57, bf16[256,1440]{1,0:T(8,128)(2,1)} %shard_map.78.table_ref), custom_call_target="tpu_custom_call" | custom-call | tf_op jit(solution)/shard_map/pallas_call | solution.py:80
  51.3 1.9 collective-permute-start.3
  53.2 1.6 collective-permute-start.4
  57.3 0.8 dynamic_slice.72
  58.3 0.7 multiply_add_fusion.2
  59.0 0.7 broadcast_in_dim.21.low_ref
  60.9 18.6 %shard_map.80.table_ref = bf16[24,400,352]{2,1,0:T(8,128)(2,1)} custom-call(f32[24,128]{1,0:T(8,128)} %broadcast_in_dim.21.low_ref, f32[24,384]{1,0:T(8,128)} %get-tuple-element.176.first_ref, f32[24,384]{1,0:T(8,128)} %get-tuple-element.175.second_ref, f32[24,384]{1,0:T(8,128)} %broadcast_in_dim.22.cos_ref, f32[24,384]{1,0:T(8,128)} %broadcast_in_dim.23.weight_ref), custom_call_target="tpu_custom_call" | custom-call | tf_op jit(solution)/shard_map/pallas_call | solution.py:193
  79.5 7.2 %shard_map.81 = (bf16[1552,256]{1,0:T(8,128)(2,1)}, bf16[1552,256]{1,0:T(8,128)(2,1)}) custom-call(s32[8]{0:T(128)} %get-tuple-element.67.low_ref, bf16[24,400,352]{2,1,0:T(8,128)(2,1)} %shard_map.80.table_ref, bf16[88,32,128]{2,1,0:T(8,128)(2,1)} %get-tuple-element.64.rest_0_, bf16[88,32,128]{2,1,0:T(8,128)(2,1)} %collective-permute-done.rest_1_, ...), custom_call_target="tpu_custom_call" | custom-call | tf_op jit(solution)/shard_map/pallas_call | solution.py:417
  86.7 3.0 collective-permute-start.6
  89.8 0.9 fusion.13
  90.7 0.7 pad_maximum_fusion.3
  91.4 0.7 pad_maximum_fusion.4
  92.1 0.8 pad_maximum_fusion.2
  92.9 3.6 %shard_map.82.table_ref = bf16[384,1440]{1,0:T(8,128)(2,1)} custom-call(f32[384,128]{1,0:T(8,128)} %bitcast.63, f32[384,128]{1,0:T(8,128)} %bitcast.62, f32[384,128]{1,0:T(8,128)} %bitcast.60, f32[384,128]{1,0:T(8,128)} %bitcast.61), custom_call_target="tpu_custom_call" | custom-call | tf_op jit(solution)/shard_map/pallas_call | solution.py:50
  96.5 21.8 %shard_map.83 = (bf16[88,32,128]{2,1,0:T(8,128)(2,1)}, bf16[88,32,128]{2,1,0:T(8,128)(2,1)}, bf16[88,32,128]{2,1,0:T(8,128)(2,1)}, bf16[88,32,128]{2,1,0:T(8,128...) custom-call(bf16[88,1440,128]{2,1,0:T(8,128)(2,1)} %bitcast.58, ...), custom_call_target="tpu_custom_call" | custom-call | tf_op jit(solution)/shard_map/pallas_call | solution.py:80
  118.4 0.7 multiply_add_fusion
  119.1 0.7 broadcast_in_dim.24.low_ref
  119.8 18.5 %shard_map.84.table_ref = bf16[24,400,352]{2,1,0:T(8,128)(2,1)} custom-call(f32[24,128]{1,0:T(8,128)} %broadcast_in_dim.24.low_ref, f32[24,384]{1,0:T(8,128)} %get-tuple-element.171.first_ref, f32[24,384]{1,0:T(8,128)} %get-tuple-element.170.second_ref, f32[24,384]{1,0:T(8,128)} %broadcast_in_dim.22.cos_ref, f32[24,384]{1,0:T(8,128)} %broadcast_in_dim.23.weight_ref), custom_call_target="tpu_custom_call" | custom-call | tf_op jit(solution)/shard_map/pallas_call | solution.py:193
  138.2 15.1 %collective-permute-done.5.rest_3_ = bf16[88,64,128]{2,1,0:T(8,128)(2,1)} collective-permute-done((bf16[88,64,128]{2,1,0:T(8,128)(2,1)}, bf16[88,64,128]{2,1,0:T(8,128)(2,1)}, u32[]{:S(2)}, u32[]{:S(2)}) %collective-permute-start.5) | collective-permute-done | bytes 1441824 | tf_op jit(solution)/shard_map/ppermute | solution.py:536
  153.4 2.7 collective-permute-start.12
  156.1 1.5 collective-permute-start.14
  159.2 7.4 %shard_map.87 = (bf16[1552,256]{1,0:T(8,128)(2,1)}, bf16[1552,256]{1,0:T(8,128)(2,1)}) custom-call(s32[8]{0:T(128)} %get-tuple-element.88.low_ref, bf16[24,400,352]{2,1,0:T(8,128)(2,1)} %shard_map.80.table_ref, bf16[88,64,128]{2,1,0:T(8,128)(2,1)} %get-tuple-element.66.rest_0_, bf16[88,64,128]{2,1,0:T(8,128)(2,1)} %copy-done, ...), custom_call_target="tpu_custom_call" | custom-call | tf_op jit(solution)/shard_map/pallas_call | solution.py:417
  167.1 2.5 collective-permute-start.9
  169.6 1.8 collective-permute-done.12.rest_1_
  171.4 23.5 %collective-permute-done.13.rest_2_ = bf16[88,32,128]{2,1,0:T(8,128)(2,1)} collective-permute-done((bf16[88,32,128]{2,1,0:T(8,128)(2,1)}, bf16[88,32,128]{2,1,0:T(8,128)(2,1)}, u32[]{:S(2)}, u32[]{:S(2)}) %collective-permute-start.13) | collective-permute-done | bytes 720928 | tf_op jit(solution)/shard_map/ppermute | solution.py:536
  194.9 12.3 %collective-permute-done.14.rest_3_ = bf16[88,32,128]{2,1,0:T(8,128)(2,1)} collective-permute-done((bf16[88,32,128]{2,1,0:T(8,128)(2,1)}, bf16[88,32,128]{2,1,0:T(8,128)(2,1)}, u32[]{:S(2)}, u32[]{:S(2)}) %collective-permute-start.14) | collective-permute-done | bytes 720928 | tf_op jit(solution)/shard_map/ppermute | solution.py:536
  207.2 1.9 collective-permute-start.15
  209.1 1.5 collective-permute-start.17
  210.8 0.9 select_maximum_fusion.in_ref
  211.7 11.4 %shard_map.85 = (f32[24,400,128]{2,1,0:T(8,128)}, f32[24,400,128]{2,1,0:T(8,128)}) custom-call(s32[24]{0:T(128)} %bitcast.75, f32[24,8,512]{2,1,0:T(8,128)} %select_maximum_fusion.in_ref), custom_call_target="tpu_custom_call" | custom-call | tf_op jit(solution)/shard_map/pallas_call | solution.py:298
  223.1 1.4 fusion.92
  224.5 7.5 %shard_map.86 = (bf16[1552,256]{1,0:T(8,128)(2,1)}, bf16[1552,256]{1,0:T(8,128)(2,1)}) custom-call(s32[8]{0:T(128)} %get-tuple-element.82.low_ref, bf16[24,400,352]{2,1,0:T(8,128)(2,1)} %shard_map.80.table_ref, bf16[88,64,128]{2,1,0:T(8,128)(2,1)} %get-tuple-element.66.rest_0_, bf16[88,64,128]{2,1,0:T(8,128)(2,1)} %copy-done, ...), custom_call_target="tpu_custom_call" | custom-call | tf_op jit(solution)/shard_map/pallas_call | solution.py:417
  232.0 4.7 %collective-permute-done.9.second_ref = bf16[1552,256]{1,0:T(8,128)(2,1)S(1)} collective-permute-done((bf16[1552,256]{1,0:T(8,128)(2,1)}, bf16[1552,256]{1,0:T(8,128)(2,1)S(1)}, u32[]{:S(2)}, u32[]{:S(2)}) %collective-permute-start.9) | collective-permute-done | bytes 794656 | tf_op jit(solution)/shard_map/ppermute | solution.py:553
  236.7 2.9 collective-permute-start.11
  239.6 0.7 fusion.91
  240.2 19.3 %shard_map.88 = (bf16[128,2,48,384]{3,2,1,0:T(8,128)(2,1)}, f32[16,8,384]{2,1,0:T(8,128)}) custom-call(s32[8]{0:T(128)} %get-tuple-element.183.low_ref, s32[8]{0:T(128)} %get-tuple-element.180.swap_ref, bf16[24,400,352]{2,1,0:T(8,128)(2,1)} %shard_map.84.table_ref, bf16[1552,256]{1,0:T(8,128)(2,1)} %collective-permute-done.6.first_ref, ...), custom_call_target="tpu_custom_call" | custom-call | tf_op jit(solution)/shard_map/pallas_call | solution.py:457
  259.5 0.9 copy-done.6
  260.4 0.9 copy-done.7
  261.3 9.6 %collective-permute-done.17.rest_3_ = bf16[88,32,128]{2,1,0:T(8,128)(2,1)S(1)} collective-permute-done((bf16[88,32,128]{2,1,0:T(8,128)(2,1)S(1)}, bf16[88,32,128]{2,1,0:T(8,128)(2,1)S(1)}, u32[]{:S(2)}, u32[]{:S(2)}) %collective-permute-start.17) | collective-permute-done | bytes 720928 | tf_op jit(solution)/shard_map/ppermute | solution.py:536
  270.8 0.9 copy-done.8
  272.0 3.2 collective-permute-start.20
  275.5 0.9 constant_dynamic-update-slice_fusion.2
  276.4 19.3 %shard_map.89 = (bf16[128,2,48,384]{3,2,1,0:T(8,128)(2,1)}, f32[16,8,384]{2,1,0:T(8,128)}) custom-call(s32[8]{0:T(128)} %get-tuple-element.182.low_ref, s32[8]{0:T(128)} %get-tuple-element.179.swap_ref, bf16[24,400,352]{2,1,0:T(8,128)(2,1)} %shard_map.84.table_ref, bf16[1552,256]{1,0:T(8,128)(2,1)} %copy-done.2, ...), custom_call_target="tpu_custom_call", output_to_operand_aliasing={{0}: (12, {})} | custom-call | tf_op jit(solution)/shard_map/pallas_call | solution.py:457
  295.7 0.9 constant_dynamic-update-slice_fusion.1
  296.6 9.1 %collective-permute-done.11.second_ref = bf16[1552,256]{1,0:T(8,128)(2,1)S(1)} collective-permute-done((bf16[1552,256]{1,0:T(8,128)(2,1)}, bf16[1552,256]{1,0:T(8,128)(2,1)S(1)}, u32[]{:S(2)}, u32[]{:S(2)}) %collective-permute-start.11) | collective-permute-done | bytes 794656 | tf_op jit(solution)/shard_map/ppermute | solution.py:553
  305.8 4.3 %collective-permute-done.19.rest_2_ = bf16[88,32,128]{2,1,0:T(8,128)(2,1)S(1)} collective-permute-done((bf16[88,32,128]{2,1,0:T(8,128)(2,1)}, bf16[88,32,128]{2,1,0:T(8,128)(2,1)S(1)}, u32[]{:S(2)}, u32[]{:S(2)}) %collective-permute-start.19) | collective-permute-done | bytes 720928 | tf_op jit(solution)/shard_map/ppermute | solution.py:536
  310.1 13.9 %collective-permute-done.20.rest_3_ = bf16[88,32,128]{2,1,0:T(8,128)(2,1)} collective-permute-done((bf16[88,32,128]{2,1,0:T(8,128)(2,1)}, bf16[88,32,128]{2,1,0:T(8,128)(2,1)}, u32[]{:S(2)}, u32[]{:S(2)}) %collective-permute-start.20) | collective-permute-done | bytes 720928 | tf_op jit(solution)/shard_map/ppermute | solution.py:536
  324.1 19.3 %shard_map.90 = (bf16[128,2,48,384]{3,2,1,0:T(8,128)(2,1)}, f32[16,8,384]{2,1,0:T(8,128)}) custom-call(s32[8]{0:T(128)} %get-tuple-element.184.low_ref, s32[8]{0:T(128)} %get-tuple-element.181.swap_ref, bf16[24,400,352]{2,1,0:T(8,128)(2,1)} %shard_map.84.table_ref, bf16[1552,256]{1,0:T(8,128)(2,1)} %copy-done.4, ...), custom_call_target="tpu_custom_call", output_to_operand_aliasing={{0}: (12, {})} | custom-call | tf_op jit(solution)/shard_map/pallas_call | solution.py:457
  343.4 0.9 constant_dynamic-update-slice_fusion
  345.0 0.7 slice.128
  345.7 1.3 collective-permute-start.21
  347.3 0.8 copy.17
  348.1 3.6 %all-to-all-start = ((bf16[4,48,6,96]{3,1,2,0:T(8,128)(2,1)}), bf16[4,48,6,96]{3,1,2,0:T(8,128)(2,1)S(1)}, u32[]{:S(2)}, u32[]{:S(2)}) async-start(bf16[4,48,6,96]{3,1,2,0:T(8,128)(2,1)} %copy.17), calls=%async_computation | async-start | bytes 589824 | tf_op jit(solution)/shard_map/all_to_all | solution.py:606
  352.4 5.6 %all-to-all-done = bf16[4,48,6,96]{3,1,2,0:T(8,128)(2,1)S(1)} async-done(((bf16[4,48,6,96]{3,1,2,0:T(8,128)(2,1)}), bf16[4,48,6,96]{3,1,2,0:T(8,128)(2,1)S(1)}, u32[]{:S(2)}, u32[]{:S(2)}) %all-to-all-start) | async-done | bytes 221216 | tf_op jit(solution)/shard_map/all_to_all | solution.py:606
  358.3 1.5 fusion.47
  (111 shorter events, 11.5 us)
Async XLA Ops:
  22.6 34.4 %collective-permute-start = (bf16[88,32,128]{2,1,0:T(8,128)(2,1)}, bf16[88,32,128]{2,1,0:T(8,128)(2,1)}, u32[]{:S(2)}, u32[]{:S(2)}) collective-permute-start(bf16[88,32,128]{2,1,0:T(8,128)(2,1)} %get-tuple-element.69), channel_id=1, source_target_pairs={{0,4},{4,0},{8,12},{12,8},{16,20},{20,16},{24,28},{28,24},{1,5},{5... | collective-permute-start | bytes 2162696 | tf_op jit(solution)/shard_map/ppermute | solution.py:536
  25.6 53.9 %collective-permute-start.1 = (bf16[88,32,128]{2,1,0:T(8,128)(2,1)}, bf16[88,32,128]{2,1,0:T(8,128)(2,1)}, u32[]{:S(2)}, u32[]{:S(2)}) collective-permute-start(bf16[88,32,128]{2,1,0:T(8,128)(2,1)} %get-tuple-element.70), channel_id=1, source_target_pairs={{0,8},{4,12},{8,0},{12,4},{16,24},{20,28},{24,16},{28,20},{1,9},{5... | collective-permute-start | bytes 2162696 | tf_op jit(solution)/shard_map/ppermute | solution.py:536
  27.2 52.4 %collective-permute-start.2 = (bf16[88,32,128]{2,1,0:T(8,128)(2,1)}, bf16[88,32,128]{2,1,0:T(8,128)(2,1)}, u32[]{:S(2)}, u32[]{:S(2)}) collective-permute-start(bf16[88,32,128]{2,1,0:T(8,128)(2,1)} %get-tuple-element.71), channel_id=1, source_target_pairs={{0,12},{4,8},{8,4},{12,0},{16,28},{20,24},{24,20},{28,16},{1,13},{... | collective-permute-start | bytes 2162696 | tf_op jit(solution)/shard_map/ppermute | solution.py:536
  32.2 24.9 %copy-start.17 = (s32[128]{0:T(128)S(1)}, s32[128]{0:T(128)}, u32[]{:S(2)}) copy-start(s32[128]{0:T(128)} %param.7) | copy-start | bytes 1540
  51.3 104.8 %collective-permute-start.3 = (bf16[88,64,128]{2,1,0:T(8,128)(2,1)}, bf16[88,64,128]{2,1,0:T(8,128)(2,1)S(1)}, u32[]{:S(2)}, u32[]{:S(2)}) collective-permute-start(bf16[88,64,128]{2,1,0:T(8,128)(2,1)} %get-tuple-element.83), channel_id=1, source_target_pairs={{0,4},{4,0},{8,12},{12,8},{16,20},{20,16},{24,28},{28,24},{1,5},{5... | collective-permute-start | bytes 4325384 | tf_op jit(solution)/shard_map/ppermute | solution.py:536
  53.2 85.0 %collective-permute-start.4 = (bf16[88,64,128]{2,1,0:T(8,128)(2,1)}, bf16[88,64,128]{2,1,0:T(8,128)(2,1)S(1)}, u32[]{:S(2)}, u32[]{:S(2)}) collective-permute-start(bf16[88,64,128]{2,1,0:T(8,128)(2,1)} %get-tuple-element.84), channel_id=1, source_target_pairs={{0,8},{4,12},{8,0},{12,4},{16,24},{20,28},{24,16},{28,20},{1,9},{5... | collective-permute-start | bytes 4325384 | tf_op jit(solution)/shard_map/ppermute | solution.py:536
  57.1 96.3 %collective-permute-start.5 = (bf16[88,64,128]{2,1,0:T(8,128)(2,1)}, bf16[88,64,128]{2,1,0:T(8,128)(2,1)}, u32[]{:S(2)}, u32[]{:S(2)}) collective-permute-start(bf16[88,64,128]{2,1,0:T(8,128)(2,1)} %get-tuple-element.85), channel_id=1, source_target_pairs={{0,12},{4,8},{8,4},{12,0},{16,28},{20,24},{24,20},{28,16},{1,13},{... | collective-permute-start | bytes 4325384 | tf_op jit(solution)/shard_map/ppermute | solution.py:536
  57.3 112.2 %copy-start.13 = (s32[1,24]{1,0:T(1,128)}, s32[1,24]{1,0:T(1,128)S(1)}, u32[]{:S(2)}) copy-start(s32[1,24]{1,0:T(1,128)S(1)} %slice.107) | copy-start | bytes 292
  86.7 79.8 %collective-permute-start.6 = (bf16[1552,256]{1,0:T(8,128)(2,1)}, bf16[1552,256]{1,0:T(8,128)(2,1)}, u32[]{:S(2)}, u32[]{:S(2)}) collective-permute-start(bf16[1552,256]{1,0:T(8,128)(2,1)} %get-tuple-element.72), channel_id=1, source_target_pairs={{0,16},{4,20},{8,24},{12,28},{16,0},{20,4},{24,8},{28,12},{1,17},{... | collective-permute-start | bytes 2383880 | tf_op jit(solution)/shard_map/ppermute | solution.py:553
  89.7 76.9 %collective-permute-start.7 = (bf16[1552,256]{1,0:T(8,128)(2,1)}, bf16[1552,256]{1,0:T(8,128)(2,1)}, u32[]{:S(2)}, u32[]{:S(2)}) collective-permute-start(bf16[1552,256]{1,0:T(8,128)(2,1)} %get-tuple-element.73), channel_id=1, source_target_pairs={{0,16},{4,20},{8,24},{12,28},{16,0},{20,4},{24,8},{28,12},{1,17},{... | collective-permute-start | bytes 2383880 | tf_op jit(solution)/shard_map/ppermute | solution.py:553
  118.2 40.0 %copy-start.11 = (f32[48,384]{1,0:T(8,128)S(1)}, f32[48,384]{1,0:T(8,128)}, u32[]{:S(2)}) copy-start(f32[48,384]{1,0:T(8,128)} %param.8) | copy-start | bytes 221188
  118.2 40.4 %copy-start.12 = (f32[48,384]{1,0:T(8,128)S(1)}, f32[48,384]{1,0:T(8,128)}, u32[]{:S(2)}) copy-start(f32[48,384]{1,0:T(8,128)} %param.9) | copy-start | bytes 221188
  138.2 20.9 %copy-start.1 = (bf16[88,64,128]{2,1,0:T(8,128)(2,1)}, bf16[88,64,128]{2,1,0:T(8,128)(2,1)S(1)}, u32[]{:S(2)}) copy-start(bf16[88,64,128]{2,1,0:T(8,128)(2,1)S(1)} %collective-permute-done.4.rest_2_) | copy-start | bytes 4325380
  153.4 18.0 %collective-permute-start.12 = (bf16[88,32,128]{2,1,0:T(8,128)(2,1)}, bf16[88,32,128]{2,1,0:T(8,128)(2,1)}, u32[]{:S(2)}, u32[]{:S(2)}) collective-permute-start(bf16[88,32,128]{2,1,0:T(8,128)(2,1)} %get-tuple-element.108), channel_id=1, source_target_pairs={{0,4},{4,0},{8,12},{12,8},{16,20},{20,16},{24,28},{28,24},{1,5},{5... | collective-permute-start | bytes 2162696 | tf_op jit(solution)/shard_map/ppermute | solution.py:536
  156.1 38.8 %collective-permute-start.13 = (bf16[88,32,128]{2,1,0:T(8,128)(2,1)}, bf16[88,32,128]{2,1,0:T(8,128)(2,1)}, u32[]{:S(2)}, u32[]{:S(2)}) collective-permute-start(bf16[88,32,128]{2,1,0:T(8,128)(2,1)} %get-tuple-element.109), channel_id=1, source_target_pairs={{0,8},{4,12},{8,0},{12,4},{16,24},{20,28},{24,16},{28,20},{1,9},{5... | collective-permute-start | bytes 2162696 | tf_op jit(solution)/shard_map/ppermute | solution.py:536
  156.1 3.0 copy-start
  156.1 51.0 %collective-permute-start.14 = (bf16[88,32,128]{2,1,0:T(8,128)(2,1)}, bf16[88,32,128]{2,1,0:T(8,128)(2,1)}, u32[]{:S(2)}, u32[]{:S(2)}) collective-permute-start(bf16[88,32,128]{2,1,0:T(8,128)(2,1)} %get-tuple-element.110), channel_id=1, source_target_pairs={{0,12},{4,8},{8,4},{12,0},{16,28},{20,24},{24,20},{28,16},{1,13},{... | collective-permute-start | bytes 2162696 | tf_op jit(solution)/shard_map/ppermute | solution.py:536
  159.2 48.0 %copy-start.16 = (bf16[88,32,128]{2,1,0:T(8,128)(2,1)S(1)}, bf16[88,32,128]{2,1,0:T(8,128)(2,1)}, u32[]{:S(2)}) copy-start(bf16[88,32,128]{2,1,0:T(8,128)(2,1)} %get-tuple-element.112) | copy-start | bytes 2162692
  159.2 49.9 %copy-start.15 = (bf16[88,32,128]{2,1,0:T(8,128)(2,1)S(1)}, bf16[88,32,128]{2,1,0:T(8,128)(2,1)}, u32[]{:S(2)}) copy-start(bf16[88,32,128]{2,1,0:T(8,128)(2,1)} %get-tuple-element.113) | copy-start | bytes 2162692
  159.2 49.9 %copy-start.14 = (bf16[88,32,128]{2,1,0:T(8,128)(2,1)S(1)}, bf16[88,32,128]{2,1,0:T(8,128)(2,1)}, u32[]{:S(2)}) copy-start(bf16[88,32,128]{2,1,0:T(8,128)(2,1)} %get-tuple-element.114) | copy-start | bytes 2162692
  166.6 65.5 %collective-permute-start.8 = (bf16[1552,256]{1,0:T(8,128)(2,1)}, bf16[1552,256]{1,0:T(8,128)(2,1)S(1)}, u32[]{:S(2)}, u32[]{:S(2)}) collective-permute-start(bf16[1552,256]{1,0:T(8,128)(2,1)} %get-tuple-element.91), channel_id=1, source_target_pairs={{0,16},{4,20},{8,24},{12,28},{16,0},{20,4},{24,8},{28,12},{1,17},{... | collective-permute-start | bytes 2383880 | tf_op jit(solution)/shard_map/ppermute | solution.py:553
  167.1 69.6 %collective-permute-start.9 = (bf16[1552,256]{1,0:T(8,128)(2,1)}, bf16[1552,256]{1,0:T(8,128)(2,1)S(1)}, u32[]{:S(2)}, u32[]{:S(2)}) collective-permute-start(bf16[1552,256]{1,0:T(8,128)(2,1)} %get-tuple-element.92), channel_id=1, source_target_pairs={{0,16},{4,20},{8,24},{12,28},{16,0},{20,4},{24,8},{28,12},{1,17},{... | collective-permute-start | bytes 2383880 | tf_op jit(solution)/shard_map/ppermute | solution.py:553
  207.2 52.4 %collective-permute-start.15 = (bf16[88,32,128]{2,1,0:T(8,128)(2,1)S(1)}, bf16[88,32,128]{2,1,0:T(8,128)(2,1)S(1)}, u32[]{:S(2)}, u32[]{:S(2)}) collective-permute-start(bf16[88,32,128]{2,1,0:T(8,128)(2,1)S(1)} %copy-done.16), channel_id=1, source_target_pairs={{0,4},{4,0},{8,12},{12,8},{16,20},{20,16},{24,28},{28,24},{1,5},{5... | collective-permute-start | bytes 2162696 | tf_op jit(solution)/shard_map/ppermute | solution.py:536
  209.1 51.3 %collective-permute-start.16 = (bf16[88,32,128]{2,1,0:T(8,128)(2,1)S(1)}, bf16[88,32,128]{2,1,0:T(8,128)(2,1)S(1)}, u32[]{:S(2)}, u32[]{:S(2)}) collective-permute-start(bf16[88,32,128]{2,1,0:T(8,128)(2,1)S(1)} %copy-done.15), channel_id=1, source_target_pairs={{0,8},{4,12},{8,0},{12,4},{16,24},{20,28},{24,16},{28,20},{1,9},{5... | collective-permute-start | bytes 2162696 | tf_op jit(solution)/shard_map/ppermute | solution.py:536
  209.1 61.7 %collective-permute-start.17 = (bf16[88,32,128]{2,1,0:T(8,128)(2,1)S(1)}, bf16[88,32,128]{2,1,0:T(8,128)(2,1)S(1)}, u32[]{:S(2)}, u32[]{:S(2)}) collective-permute-start(bf16[88,32,128]{2,1,0:T(8,128)(2,1)S(1)} %copy-done.14), channel_id=1, source_target_pairs={{0,12},{4,8},{8,4},{12,0},{16,28},{20,24},{24,20},{28,16},{1,13},{... | collective-permute-start | bytes 2162696 | tf_op jit(solution)/shard_map/ppermute | solution.py:536
  232.0 27.5 %copy-start.2 = (bf16[1552,256]{1,0:T(8,128)(2,1)}, bf16[1552,256]{1,0:T(8,128)(2,1)S(1)}, u32[]{:S(2)}) copy-start(bf16[1552,256]{1,0:T(8,128)(2,1)S(1)} %collective-permute-done.8.first_ref) | copy-start | bytes 2383876
  236.7 22.8 %copy-start.3 = (bf16[1552,256]{1,0:T(8,128)(2,1)}, bf16[1552,256]{1,0:T(8,128)(2,1)S(1)}, u32[]{:S(2)}) copy-start(bf16[1552,256]{1,0:T(8,128)(2,1)S(1)} %collective-permute-done.9.second_ref) | copy-start | bytes 2383876
  236.7 60.0 %collective-permute-start.10 = (bf16[1552,256]{1,0:T(8,128)(2,1)}, bf16[1552,256]{1,0:T(8,128)(2,1)S(1)}, u32[]{:S(2)}, u32[]{:S(2)}) collective-permute-start(bf16[1552,256]{1,0:T(8,128)(2,1)} %get-tuple-element.93), channel_id=1, source_target_pairs={{0,16},{4,20},{8,24},{12,28},{16,0},{20,4},{24,8},{28,12},{1,17},{... | collective-permute-start | bytes 2383880 | tf_op jit(solution)/shard_map/ppermute | solution.py:553
  236.7 69.1 %collective-permute-start.11 = (bf16[1552,256]{1,0:T(8,128)(2,1)}, bf16[1552,256]{1,0:T(8,128)(2,1)S(1)}, u32[]{:S(2)}, u32[]{:S(2)}) collective-permute-start(bf16[1552,256]{1,0:T(8,128)(2,1)} %get-tuple-element.94), channel_id=1, source_target_pairs={{0,16},{4,20},{8,24},{12,28},{16,0},{20,4},{24,8},{28,12},{1,17},{... | collective-permute-start | bytes 2383880 | tf_op jit(solution)/shard_map/ppermute | solution.py:553
  259.5 0.9 copy-start.6
  260.4 0.9 copy-start.7
  270.8 0.9 copy-start.8
  271.7 34.1 %collective-permute-start.18 = (bf16[88,32,128]{2,1,0:T(8,128)(2,1)}, bf16[88,32,128]{2,1,0:T(8,128)(2,1)S(1)}, u32[]{:S(2)}, u32[]{:S(2)}) collective-permute-start(bf16[88,32,128]{2,1,0:T(8,128)(2,1)} %get-tuple-element.117), channel_id=1, source_target_pairs={{0,4},{4,0},{8,12},{12,8},{16,20},{20,16},{24,28},{28,24},{1,5},{5... | collective-permute-start | bytes 2162696 | tf_op jit(solution)/shard_map/ppermute | solution.py:536
  272.0 38.1 %collective-permute-start.19 = (bf16[88,32,128]{2,1,0:T(8,128)(2,1)}, bf16[88,32,128]{2,1,0:T(8,128)(2,1)S(1)}, u32[]{:S(2)}, u32[]{:S(2)}) collective-permute-start(bf16[88,32,128]{2,1,0:T(8,128)(2,1)} %get-tuple-element.118), channel_id=1, source_target_pairs={{0,8},{4,12},{8,0},{12,4},{16,24},{20,28},{24,16},{28,20},{1,9},{5... | collective-permute-start | bytes 2162696 | tf_op jit(solution)/shard_map/ppermute | solution.py:536
  272.0 52.0 %collective-permute-start.20 = (bf16[88,32,128]{2,1,0:T(8,128)(2,1)}, bf16[88,32,128]{2,1,0:T(8,128)(2,1)}, u32[]{:S(2)}, u32[]{:S(2)}) collective-permute-start(bf16[88,32,128]{2,1,0:T(8,128)(2,1)} %get-tuple-element.119), channel_id=1, source_target_pairs={{0,12},{4,8},{8,4},{12,0},{16,28},{20,24},{24,20},{28,16},{1,13},{... | collective-permute-start | bytes 2162696 | tf_op jit(solution)/shard_map/ppermute | solution.py:536
  296.6 27.4 %copy-start.4 = (bf16[1552,256]{1,0:T(8,128)(2,1)}, bf16[1552,256]{1,0:T(8,128)(2,1)S(1)}, u32[]{:S(2)}) copy-start(bf16[1552,256]{1,0:T(8,128)(2,1)S(1)} %collective-permute-done.10.first_ref) | copy-start | bytes 2383876
  305.8 18.3 %copy-start.5 = (bf16[1552,256]{1,0:T(8,128)(2,1)}, bf16[1552,256]{1,0:T(8,128)(2,1)S(1)}, u32[]{:S(2)}) copy-start(bf16[1552,256]{1,0:T(8,128)(2,1)S(1)} %collective-permute-done.11.second_ref) | copy-start | bytes 2383876
  305.8 18.3 %copy-start.9 = (bf16[88,32,128]{2,1,0:T(8,128)(2,1)}, bf16[88,32,128]{2,1,0:T(8,128)(2,1)S(1)}, u32[]{:S(2)}) copy-start(bf16[88,32,128]{2,1,0:T(8,128)(2,1)S(1)} %collective-permute-done.18.rest_1_) | copy-start | bytes 2162692
  310.1 14.0 %copy-start.10 = (bf16[88,32,128]{2,1,0:T(8,128)(2,1)}, bf16[88,32,128]{2,1,0:T(8,128)(2,1)S(1)}, u32[]{:S(2)}) copy-start(bf16[88,32,128]{2,1,0:T(8,128)(2,1)S(1)} %collective-permute-done.19.rest_2_) | copy-start | bytes 2162692
  345.7 6.0 %collective-permute-start.21 = (bf16[2,48,384]{2,0,1:T(2,128)(2,1)S(1)}, bf16[2,48,384]{2,0,1:T(2,128)(2,1)S(1)}, u32[]{:S(2)}, u32[]{:S(2)}) collective-permute-start(bf16[2,48,384]{2,0,1:T(2,128)(2,1)S(1)} %slice.128), channel_id=1, source_target_pairs={{0,1},{1,2},{2,3},{4,5},{5,6},{6,7},{8,9},{9,10},{10,11},{12,13},{... | collective-permute-start | bytes 221192 | tf_op jit(solution)/shard_map/ppermute | solution.py:598
  348.1 10.0 %all-to-all-start = ((bf16[4,48,6,96]{3,1,2,0:T(8,128)(2,1)}), bf16[4,48,6,96]{3,1,2,0:T(8,128)(2,1)S(1)}, u32[]{:S(2)}, u32[]{:S(2)}) async-start(bf16[4,48,6,96]{3,1,2,0:T(8,128)(2,1)} %copy.17), calls=%async_computation | async-start | bytes 589824 | tf_op jit(solution)/shard_map/all_to_all | solution.py:606

commit v2 on v1

--- a/solution.py
+++ b/solution.py
@@ -136,7 +136,7 @@
                 advanced = factor * (cosines[t] * current[t] - last_inverse * lagged[t])
                 lagged[t] = current[t]
                 current[t] = jnp.where(fresh, 1.0, advanced)
-                rows_ref[t, pl.ds(step, pairs, stride=TILE), :] = current[t]
+                rows_ref[t, pl.ds(step, pairs, stride=PITCH), :] = current[t]
             last_inverse = inverse
         renewed = (low_next >= begin) & (low_next < begin + float(TILE))
         for t in tiles:
@@ -149,7 +149,7 @@
                 span = slice(t * LANES, min((t + 1) * LANES, lat_count))
                 width = span.stop - span.start
                 here = slice(t * LANES, (t + 1) * LANES)
-                values = rows_ref[t, pair * TILE : (pair + 1) * TILE, :]
+                values = rows_ref[t, pair * PITCH : pair * PITCH + TILE, :]
                 one = jnp.where(before, scale_ref[0, pair : pair + 1, here], scale_ref[2, pair : pair + 1, here])
                 two = jnp.where(before, scale_ref[1, pair : pair + 1, here], scale_ref[3, pair : pair + 1, here])
                 values = (values * one * two).astype(jnp.bfloat16)
@@ -194,7 +194,7 @@
         functools.partial(table_kernel, steps, lane_tiles, top),
         out_shape=jax.ShapeDtypeStruct((pair_count, steps, lat_half), jnp.bfloat16),
         scratch_shapes=[
-            pltpu.VMEM((lane_tiles, pair_count * TILE, LANES), jnp.float32),
+            pltpu.VMEM((lane_tiles, pair_count * PITCH, LANES), jnp.float32),
             pltpu.VMEM((4, pair_count, width), jnp.float32),
         ],
         compiler_params=pltpu.CompilerParams(vmem_limit_bytes=VMEM_LIMIT),

time: 362 us -> 359 us (level)
  Pallas kernels: 194 us -> 183 us
  waiting for transfers between devices: 100 us -> 109 us
    ppermute x15, waiting for transfers between devices: 80.6 us -> 91.9 us  [exchange(): lax.ppermute(blocks[k], 'band', [(i, i ^ k) for i in range(band_count)])]
    pallas_call x2, Pallas kernels: 37.1 us -> 25.8 us  [packed_table(): pl.pallas_call(functools.partial(table_kernel, steps, lane_tiles, top), o...]
  transfers between devices with their start and end apart: 23 -> 23, of which waited for: 10 -> 10; matrix products, arithmetic and copies ran while one was open for 6% -> 6% of each run, Pallas kernels for 43% -> 41%
where the time goes in v2:
time: 359 us; the launch traced here: 357 us
  Pallas kernels  183 us (51%)
  waiting for transfers between devices  109 us (30%)
  starting transfers between devices  32.7 us (9%)
  local copies, waits for them, and re-layouts  18.5 us (5%)
  other arithmetic  12.9 us (4%)
    ppermute x15, waiting for transfers between devices, exchange(): lax.ppermute(blocks[k], 'band', [(i, i ^ k) for i in range(band_count)])  91.9 us
    pallas_call x3, Pallas kernels, finish(): pl.pallas_call(functools.partial(finish_kernel, len(blocks)), grid=(1,),...  57.8 us
    pallas_call x3, Pallas kernels, longitude_sums(): pl.pallas_call(transform_kernel, grid=(lats // group,), in_specs=[pl.Bloc...  57.2 us
    pallas_call x2, Pallas kernels, packed_table(): pl.pallas_call(functools.partial(table_kernel, steps, lane_tiles, top), o...  25.8 us
    pallas_call x3, Pallas kernels, partial_sums(): pl.pallas_call(functools.partial(partial_kernel, degrees), grid=(1,), in_...  22 us
    ppermute x15, starting transfers between devices, exchange(): lax.ppermute(blocks[k], 'band', [(i, i ^ k) for i in range(band_count)])  18.8 us
    ppermute x6, waiting for transfers between devices, send_sums(): others.append([lax.ppermute(part, 'band', mirror) for part in sums])  11.8 us
    pallas_call x1, Pallas kernels, packed_columns(): pl.pallas_call(pack_kernel, in_specs=[pl.BlockSpec(memory_space=pltpu.SME...  11.4 us
  transfers between devices with their start and end apart: 23, of which 10 were waited for; matrix products, arithmetic and copies ran while one was open for 6% of the time, Pallas kernels for 41%

profile of v2, /device:TPU:0, one launch (start us, length us, event | category | flops | bytes accessed | tf_op | source)
XLA Modules:
  0.0 357.5 jit_solution(1686224001474861825)
XLA Ops:
  0.7 0.8 reshape.400
  3.4 0.7 pad_maximum_fusion.10
  4.1 2.2 shard_map.76.table_ref
  6.2 16.4 %shard_map.77 = (bf16[88,32,128]{2,1,0:T(8,128)(2,1)}, bf16[88,32,128]{2,1,0:T(8,128)(2,1)}, bf16[88,32,128]{2,1,0:T(8,128)(2,1)}, bf16[88,32,128]{2,1,0:T(8,128)(2,1)}) custom-call(bf16[88,1440,128]{2,1,0:T(8,128)(2,1)} %bitcast.56, bf16[128,1440]{1,0:T(8,128)(2,1)} %shard_map.76.table_ref), custom_call_target="tpu_custom_call" | custom-call | tf_op jit(solution)/shard_map/pallas_call | solution.py:80
  22.6 3.0 collective-permute-start
  25.6 1.6 collective-permute-start.1
  27.9 0.7 pad_maximum_fusion.8
  28.6 0.8 pad_maximum_fusion.6
  29.4 2.9 shard_map.78.table_ref
  32.2 19.1 %shard_map.79 = (bf16[88,64,128]{2,1,0:T(8,128)(2,1)}, bf16[88,64,128]{2,1,0:T(8,128)(2,1)}, bf16[88,64,128]{2,1,0:T(8,128)(2,1)}, bf16[88,64,128]{2,1,0:T(8,128)(2,1)}) custom-call(bf16[88,1440,128]{2,1,0:T(8,128)(2,1)} %bitcast.57, bf16[256,1440]{1,0:T(8,128)(2,1)} %shard_map.78.table_ref), custom_call_target="tpu_custom_call" | custom-call | tf_op jit(solution)/shard_map/pallas_call | solution.py:80
  51.3 1.9 collective-permute-start.3
  53.2 1.6 collective-permute-start.4
  57.3 0.8 dynamic_slice.72
  58.3 0.7 multiply_add_fusion.2
  59.0 0.7 broadcast_in_dim.21.low_ref
  60.9 13.0 %shard_map.80.table_ref = bf16[24,400,352]{2,1,0:T(8,128)(2,1)} custom-call(f32[24,128]{1,0:T(8,128)} %broadcast_in_dim.21.low_ref, f32[24,384]{1,0:T(8,128)} %get-tuple-element.176.first_ref, f32[24,384]{1,0:T(8,128)} %get-tuple-element.175.second_ref, f32[24,384]{1,0:T(8,128)} %broadcast_in_dim.22.cos_ref, f32[24,384]{1,0:T(8,128)} %broadcast_in_dim.23.weight_ref), custom_call_target="tpu_custom_call" | custom-call | tf_op jit(solution)/shard_map/pallas_call | solution.py:193
  73.9 7.2 %shard_map.81 = (bf16[1552,256]{1,0:T(8,128)(2,1)}, bf16[1552,256]{1,0:T(8,128)(2,1)}) custom-call(s32[8]{0:T(128)} %get-tuple-element.67.low_ref, bf16[24,400,352]{2,1,0:T(8,128)(2,1)} %shard_map.80.table_ref, bf16[88,32,128]{2,1,0:T(8,128)(2,1)} %get-tuple-element.64.rest_0_, bf16[88,32,128]{2,1,0:T(8,128)(2,1)} %collective-permute-done.rest_1_, ...), custom_call_target="tpu_custom_call" | custom-call | tf_op jit(solution)/shard_map/pallas_call | solution.py:417
  81.1 3.0 collective-permute-start.6
  84.2 0.9 fusion.13
  85.1 0.7 pad_maximum_fusion.3
  85.8 0.7 pad_maximum_fusion.4
  86.5 0.8 pad_maximum_fusion.2
  87.2 3.6 %shard_map.82.table_ref = bf16[384,1440]{1,0:T(8,128)(2,1)} custom-call(f32[384,128]{1,0:T(8,128)} %bitcast.63, f32[384,128]{1,0:T(8,128)} %bitcast.62, f32[384,128]{1,0:T(8,128)} %bitcast.60, f32[384,128]{1,0:T(8,128)} %bitcast.61), custom_call_target="tpu_custom_call" | custom-call | tf_op jit(solution)/shard_map/pallas_call | solution.py:50
  90.8 21.8 %shard_map.83 = (bf16[88,32,128]{2,1,0:T(8,128)(2,1)}, bf16[88,32,128]{2,1,0:T(8,128)(2,1)}, bf16[88,32,128]{2,1,0:T(8,128)(2,1)}, bf16[88,32,128]{2,1,0:T(8,128...) custom-call(bf16[88,1440,128]{2,1,0:T(8,128)(2,1)} %bitcast.58, ...), custom_call_target="tpu_custom_call" | custom-call | tf_op jit(solution)/shard_map/pallas_call | solution.py:80
  112.8 0.7 multiply_add_fusion
  113.5 0.7 broadcast_in_dim.24.low_ref
  114.1 12.9 %shard_map.84.table_ref = bf16[24,400,352]{2,1,0:T(8,128)(2,1)} custom-call(f32[24,128]{1,0:T(8,128)} %broadcast_in_dim.24.low_ref, f32[24,384]{1,0:T(8,128)} %get-tuple-element.171.first_ref, f32[24,384]{1,0:T(8,128)} %get-tuple-element.170.second_ref, f32[24,384]{1,0:T(8,128)} %broadcast_in_dim.22.cos_ref, f32[24,384]{1,0:T(8,128)} %broadcast_in_dim.23.weight_ref), custom_call_target="tpu_custom_call" | custom-call | tf_op jit(solution)/shard_map/pallas_call | solution.py:193
  127.0 27.6 %collective-permute-done.5.rest_3_ = bf16[88,64,128]{2,1,0:T(8,128)(2,1)} collective-permute-done((bf16[88,64,128]{2,1,0:T(8,128)(2,1)}, bf16[88,64,128]{2,1,0:T(8,128)(2,1)}, u32[]{:S(2)}, u32[]{:S(2)}) %collective-permute-start.5) | collective-permute-done | bytes 1441824 | tf_op jit(solution)/shard_map/ppermute | solution.py:536
  154.6 1.7 collective-permute-start.12
  156.3 1.8 collective-permute-start.14
  159.7 7.3 %shard_map.87 = (bf16[1552,256]{1,0:T(8,128)(2,1)}, bf16[1552,256]{1,0:T(8,128)(2,1)}) custom-call(s32[8]{0:T(128)} %get-tuple-element.88.low_ref, bf16[24,400,352]{2,1,0:T(8,128)(2,1)} %shard_map.80.table_ref, bf16[88,64,128]{2,1,0:T(8,128)(2,1)} %get-tuple-element.66.rest_0_, bf16[88,64,128]{2,1,0:T(8,128)(2,1)} %copy-done, ...), custom_call_target="tpu_custom_call" | custom-call | tf_op jit(solution)/shard_map/pallas_call | solution.py:417
  167.1 2.5 collective-permute-start.8
  170.1 1.8 collective-permute-done.12.rest_1_
  171.9 25.0 %collective-permute-done.13.rest_2_ = bf16[88,32,128]{2,1,0:T(8,128)(2,1)} collective-permute-done((bf16[88,32,128]{2,1,0:T(8,128)(2,1)}, bf16[88,32,128]{2,1,0:T(8,128)(2,1)}, u32[]{:S(2)}, u32[]{:S(2)}) %collective-permute-start.13) | collective-permute-done | bytes 720928 | tf_op jit(solution)/shard_map/ppermute | solution.py:536
  197.0 12.0 %collective-permute-done.14.rest_3_ = bf16[88,32,128]{2,1,0:T(8,128)(2,1)} collective-permute-done((bf16[88,32,128]{2,1,0:T(8,128)(2,1)}, bf16[88,32,128]{2,1,0:T(8,128)(2,1)}, u32[]{:S(2)}, u32[]{:S(2)}) %collective-permute-start.14) | collective-permute-done | bytes 720928 | tf_op jit(solution)/shard_map/ppermute | solution.py:536
  209.0 2.2 collective-permute-start.15
  211.2 1.5 collective-permute-start.17
  212.9 0.9 select_maximum_fusion.in_ref
  213.8 11.4 %shard_map.85 = (f32[24,400,128]{2,1,0:T(8,128)}, f32[24,400,128]{2,1,0:T(8,128)}) custom-call(s32[24]{0:T(128)} %bitcast.75, f32[24,8,512]{2,1,0:T(8,128)} %select_maximum_fusion.in_ref), custom_call_target="tpu_custom_call" | custom-call | tf_op jit(solution)/shard_map/pallas_call | solution.py:298
  225.2 1.4 fusion.92
  226.6 7.5 %shard_map.86 = (bf16[1552,256]{1,0:T(8,128)(2,1)}, bf16[1552,256]{1,0:T(8,128)(2,1)}) custom-call(s32[8]{0:T(128)} %get-tuple-element.82.low_ref, bf16[24,400,352]{2,1,0:T(8,128)(2,1)} %shard_map.80.table_ref, bf16[88,64,128]{2,1,0:T(8,128)(2,1)} %get-tuple-element.66.rest_0_, bf16[88,64,128]{2,1,0:T(8,128)(2,1)} %copy-done, ...), custom_call_target="tpu_custom_call" | custom-call | tf_op jit(solution)/shard_map/pallas_call | solution.py:417
  234.1 3.1 collective-permute-done.9.second_ref
  237.2 2.9 collective-permute-start.11
  240.8 19.3 %shard_map.88 = (bf16[128,2,48,384]{3,2,1,0:T(8,128)(2,1)}, f32[16,8,384]{2,1,0:T(8,128)}) custom-call(s32[8]{0:T(128)} %get-tuple-element.183.low_ref, s32[8]{0:T(128)} %get-tuple-element.180.swap_ref, bf16[24,400,352]{2,1,0:T(8,128)(2,1)} %shard_map.84.table_ref, bf16[1552,256]{1,0:T(8,128)(2,1)} %collective-permute-done.6.first_ref, ...), custom_call_target="tpu_custom_call" | custom-call | tf_op jit(solution)/shard_map/pallas_call | solution.py:457
  260.1 0.9 copy-done.6
  261.0 0.9 copy-done.7
  261.8 10.0 %collective-permute-done.17.rest_3_ = bf16[88,32,128]{2,1,0:T(8,128)(2,1)S(1)} collective-permute-done((bf16[88,32,128]{2,1,0:T(8,128)(2,1)S(1)}, bf16[88,32,128]{2,1,0:T(8,128)(2,1)S(1)}, u32[]{:S(2)}, u32[]{:S(2)}) %collective-permute-start.17) | collective-permute-done | bytes 720928 | tf_op jit(solution)/shard_map/ppermute | solution.py:536
  271.9 0.9 copy-done.8
  272.8 1.4 collective-permute-start.18
  274.1 2.1 collective-permute-start.20
  276.5 0.9 constant_dynamic-update-slice_fusion.2
  277.5 19.3 %shard_map.89 = (bf16[128,2,48,384]{3,2,1,0:T(8,128)(2,1)}, f32[16,8,384]{2,1,0:T(8,128)}) custom-call(s32[8]{0:T(128)} %get-tuple-element.182.low_ref, s32[8]{0:T(128)} %get-tuple-element.179.swap_ref, bf16[24,400,352]{2,1,0:T(8,128)(2,1)} %shard_map.84.table_ref, bf16[1552,256]{1,0:T(8,128)(2,1)} %copy-done.2, ...), custom_call_target="tpu_custom_call", output_to_operand_aliasing={{0}: (12, {})} | custom-call | tf_op jit(solution)/shard_map/pallas_call | solution.py:457
  296.7 0.9 constant_dynamic-update-slice_fusion.1
  297.7 8.7 %collective-permute-done.11.second_ref = bf16[1552,256]{1,0:T(8,128)(2,1)S(1)} collective-permute-done((bf16[1552,256]{1,0:T(8,128)(2,1)}, bf16[1552,256]{1,0:T(8,128)(2,1)S(1)}, u32[]{:S(2)}, u32[]{:S(2)}) %collective-permute-start.11) | collective-permute-done | bytes 794656 | tf_op jit(solution)/shard_map/ppermute | solution.py:553
  306.4 3.9 %collective-permute-done.19.rest_2_ = bf16[88,32,128]{2,1,0:T(8,128)(2,1)S(1)} collective-permute-done((bf16[88,32,128]{2,1,0:T(8,128)(2,1)}, bf16[88,32,128]{2,1,0:T(8,128)(2,1)S(1)}, u32[]{:S(2)}, u32[]{:S(2)}) %collective-permute-start.19) | collective-permute-done | bytes 720928 | tf_op jit(solution)/shard_map/ppermute | solution.py:536
  310.3 11.4 %collective-permute-done.20.rest_3_ = bf16[88,32,128]{2,1,0:T(8,128)(2,1)} collective-permute-done((bf16[88,32,128]{2,1,0:T(8,128)(2,1)}, bf16[88,32,128]{2,1,0:T(8,128)(2,1)}, u32[]{:S(2)}, u32[]{:S(2)}) %collective-permute-start.20) | collective-permute-done | bytes 720928 | tf_op jit(solution)/shard_map/ppermute | solution.py:536
  321.8 19.3 %shard_map.90 = (bf16[128,2,48,384]{3,2,1,0:T(8,128)(2,1)}, f32[16,8,384]{2,1,0:T(8,128)}) custom-call(s32[8]{0:T(128)} %get-tuple-element.184.low_ref, s32[8]{0:T(128)} %get-tuple-element.181.swap_ref, bf16[24,400,352]{2,1,0:T(8,128)(2,1)} %shard_map.84.table_ref, bf16[1552,256]{1,0:T(8,128)(2,1)} %copy-done.4, ...), custom_call_target="tpu_custom_call", output_to_operand_aliasing={{0}: (12, {})} | custom-call | tf_op jit(solution)/shard_map/pallas_call | solution.py:457
  341.0 0.9 constant_dynamic-update-slice_fusion
  342.7 0.7 slice.128
  343.4 1.3 collective-permute-start.21
  345.0 0.8 copy.17
  345.7 3.6 %all-to-all-start = ((bf16[4,48,6,96]{3,1,2,0:T(8,128)(2,1)}), bf16[4,48,6,96]{3,1,2,0:T(8,128)(2,1)S(1)}, u32[]{:S(2)}, u32[]{:S(2)}) async-start(bf16[4,48,6,96]{3,1,2,0:T(8,128)(2,1)} %copy.17), calls=%async_computation | async-start | bytes 589824 | tf_op jit(solution)/shard_map/all_to_all | solution.py:606
  350.1 5.6 %all-to-all-done = bf16[4,48,6,96]{3,1,2,0:T(8,128)(2,1)S(1)} async-done(((bf16[4,48,6,96]{3,1,2,0:T(8,128)(2,1)}), bf16[4,48,6,96]{3,1,2,0:T(8,128)(2,1)S(1)}, u32[]{:S(2)}, u32[]{:S(2)}) %all-to-all-start) | async-done | bytes 221216 | tf_op jit(solution)/shard_map/all_to_all | solution.py:606
  355.9 1.5 fusion.47
  (111 shorter events, 11.8 us)
Async XLA Ops:
  22.6 34.4 %collective-permute-start = (bf16[88,32,128]{2,1,0:T(8,128)(2,1)}, bf16[88,32,128]{2,1,0:T(8,128)(2,1)}, u32[]{:S(2)}, u32[]{:S(2)}) collective-permute-start(bf16[88,32,128]{2,1,0:T(8,128)(2,1)} %get-tuple-element.69), channel_id=1, source_target_pairs={{0,4},{4,0},{8,12},{12,8},{16,20},{20,16},{24,28},{28,24},{1,5},{5... | collective-permute-start | bytes 2162696 | tf_op jit(solution)/shard_map/ppermute | solution.py:536
  25.6 48.3 %collective-permute-start.1 = (bf16[88,32,128]{2,1,0:T(8,128)(2,1)}, bf16[88,32,128]{2,1,0:T(8,128)(2,1)}, u32[]{:S(2)}, u32[]{:S(2)}) collective-permute-start(bf16[88,32,128]{2,1,0:T(8,128)(2,1)} %get-tuple-element.70), channel_id=1, source_target_pairs={{0,8},{4,12},{8,0},{12,4},{16,24},{20,28},{24,16},{28,20},{1,9},{5... | collective-permute-start | bytes 2162696 | tf_op jit(solution)/shard_map/ppermute | solution.py:536
  27.2 46.8 %collective-permute-start.2 = (bf16[88,32,128]{2,1,0:T(8,128)(2,1)}, bf16[88,32,128]{2,1,0:T(8,128)(2,1)}, u32[]{:S(2)}, u32[]{:S(2)}) collective-permute-start(bf16[88,32,128]{2,1,0:T(8,128)(2,1)} %get-tuple-element.71), channel_id=1, source_target_pairs={{0,12},{4,8},{8,4},{12,0},{16,28},{20,24},{24,20},{28,16},{1,13},{... | collective-permute-start | bytes 2162696 | tf_op jit(solution)/shard_map/ppermute | solution.py:536
  32.2 24.9 %copy-start.17 = (s32[128]{0:T(128)S(1)}, s32[128]{0:T(128)}, u32[]{:S(2)}) copy-start(s32[128]{0:T(128)} %param.7) | copy-start | bytes 1540
  51.3 105.0 %collective-permute-start.3 = (bf16[88,64,128]{2,1,0:T(8,128)(2,1)}, bf16[88,64,128]{2,1,0:T(8,128)(2,1)S(1)}, u32[]{:S(2)}, u32[]{:S(2)}) collective-permute-start(bf16[88,64,128]{2,1,0:T(8,128)(2,1)} %get-tuple-element.83), channel_id=1, source_target_pairs={{0,4},{4,0},{8,12},{12,8},{16,20},{20,16},{24,28},{28,24},{1,5},{5... | collective-permute-start | bytes 4325384 | tf_op jit(solution)/shard_map/ppermute | solution.py:536
  53.2 73.8 %collective-permute-start.4 = (bf16[88,64,128]{2,1,0:T(8,128)(2,1)}, bf16[88,64,128]{2,1,0:T(8,128)(2,1)S(1)}, u32[]{:S(2)}, u32[]{:S(2)}) collective-permute-start(bf16[88,64,128]{2,1,0:T(8,128)(2,1)} %get-tuple-element.84), channel_id=1, source_target_pairs={{0,8},{4,12},{8,0},{12,4},{16,24},{20,28},{24,16},{28,20},{1,9},{5... | collective-permute-start | bytes 4325384 | tf_op jit(solution)/shard_map/ppermute | solution.py:536
  57.1 97.6 %collective-permute-start.5 = (bf16[88,64,128]{2,1,0:T(8,128)(2,1)}, bf16[88,64,128]{2,1,0:T(8,128)(2,1)}, u32[]{:S(2)}, u32[]{:S(2)}) collective-permute-start(bf16[88,64,128]{2,1,0:T(8,128)(2,1)} %get-tuple-element.85), channel_id=1, source_target_pairs={{0,12},{4,8},{8,4},{12,0},{16,28},{20,24},{24,20},{28,16},{1,13},{... | collective-permute-start | bytes 4325384 | tf_op jit(solution)/shard_map/ppermute | solution.py:536
  57.3 112.8 %copy-start.13 = (s32[1,24]{1,0:T(1,128)}, s32[1,24]{1,0:T(1,128)S(1)}, u32[]{:S(2)}) copy-start(s32[1,24]{1,0:T(1,128)S(1)} %slice.107) | copy-start | bytes 292
  81.1 86.0 %collective-permute-start.6 = (bf16[1552,256]{1,0:T(8,128)(2,1)}, bf16[1552,256]{1,0:T(8,128)(2,1)}, u32[]{:S(2)}, u32[]{:S(2)}) collective-permute-start(bf16[1552,256]{1,0:T(8,128)(2,1)} %get-tuple-element.72), channel_id=1, source_target_pairs={{0,16},{4,20},{8,24},{12,28},{16,0},{20,4},{24,8},{28,12},{1,17},{... | collective-permute-start | bytes 2383880 | tf_op jit(solution)/shard_map/ppermute | solution.py:553
  84.0 83.0 %collective-permute-start.7 = (bf16[1552,256]{1,0:T(8,128)(2,1)}, bf16[1552,256]{1,0:T(8,128)(2,1)}, u32[]{:S(2)}, u32[]{:S(2)}) collective-permute-start(bf16[1552,256]{1,0:T(8,128)(2,1)} %get-tuple-element.73), channel_id=1, source_target_pairs={{0,16},{4,20},{8,24},{12,28},{16,0},{20,4},{24,8},{28,12},{1,17},{... | collective-permute-start | bytes 2383880 | tf_op jit(solution)/shard_map/ppermute | solution.py:553
  112.6 46.1 %copy-start.11 = (f32[48,384]{1,0:T(8,128)S(1)}, f32[48,384]{1,0:T(8,128)}, u32[]{:S(2)}) copy-start(f32[48,384]{1,0:T(8,128)} %param.8) | copy-start | bytes 221188
  112.6 46.5 %copy-start.12 = (f32[48,384]{1,0:T(8,128)S(1)}, f32[48,384]{1,0:T(8,128)}, u32[]{:S(2)}) copy-start(f32[48,384]{1,0:T(8,128)} %param.9) | copy-start | bytes 221188
  127.0 32.7 %copy-start.1 = (bf16[88,64,128]{2,1,0:T(8,128)(2,1)}, bf16[88,64,128]{2,1,0:T(8,128)(2,1)S(1)}, u32[]{:S(2)}) copy-start(bf16[88,64,128]{2,1,0:T(8,128)(2,1)S(1)} %collective-permute-done.4.rest_2_) | copy-start | bytes 4325380
  154.6 17.3 %collective-permute-start.12 = (bf16[88,32,128]{2,1,0:T(8,128)(2,1)}, bf16[88,32,128]{2,1,0:T(8,128)(2,1)}, u32[]{:S(2)}, u32[]{:S(2)}) collective-permute-start(bf16[88,32,128]{2,1,0:T(8,128)(2,1)} %get-tuple-element.108), channel_id=1, source_target_pairs={{0,4},{4,0},{8,12},{12,8},{16,20},{20,16},{24,28},{28,24},{1,5},{5... | collective-permute-start | bytes 2162696 | tf_op jit(solution)/shard_map/ppermute | solution.py:536
  156.3 40.7 %collective-permute-start.13 = (bf16[88,32,128]{2,1,0:T(8,128)(2,1)}, bf16[88,32,128]{2,1,0:T(8,128)(2,1)}, u32[]{:S(2)}, u32[]{:S(2)}) collective-permute-start(bf16[88,32,128]{2,1,0:T(8,128)(2,1)} %get-tuple-element.109), channel_id=1, source_target_pairs={{0,8},{4,12},{8,0},{12,4},{16,24},{20,28},{24,16},{28,20},{1,9},{5... | collective-permute-start | bytes 2162696 | tf_op jit(solution)/shard_map/ppermute | solution.py:536
  156.3 3.4 copy-start
  156.3 52.7 %collective-permute-start.14 = (bf16[88,32,128]{2,1,0:T(8,128)(2,1)}, bf16[88,32,128]{2,1,0:T(8,128)(2,1)}, u32[]{:S(2)}, u32[]{:S(2)}) collective-permute-start(bf16[88,32,128]{2,1,0:T(8,128)(2,1)} %get-tuple-element.110), channel_id=1, source_target_pairs={{0,12},{4,8},{8,4},{12,0},{16,28},{20,24},{24,20},{28,16},{1,13},{... | collective-permute-start | bytes 2162696 | tf_op jit(solution)/shard_map/ppermute | solution.py:536
  159.7 49.3 %copy-start.16 = (bf16[88,32,128]{2,1,0:T(8,128)(2,1)S(1)}, bf16[88,32,128]{2,1,0:T(8,128)(2,1)}, u32[]{:S(2)}) copy-start(bf16[88,32,128]{2,1,0:T(8,128)(2,1)} %get-tuple-element.112) | copy-start | bytes 2162692
  159.7 51.5 %copy-start.15 = (bf16[88,32,128]{2,1,0:T(8,128)(2,1)S(1)}, bf16[88,32,128]{2,1,0:T(8,128)(2,1)}, u32[]{:S(2)}) copy-start(bf16[88,32,128]{2,1,0:T(8,128)(2,1)} %get-tuple-element.113) | copy-start | bytes 2162692
  159.7 51.5 %copy-start.14 = (bf16[88,32,128]{2,1,0:T(8,128)(2,1)S(1)}, bf16[88,32,128]{2,1,0:T(8,128)(2,1)}, u32[]{:S(2)}) copy-start(bf16[88,32,128]{2,1,0:T(8,128)(2,1)} %get-tuple-element.114) | copy-start | bytes 2162692
  167.1 67.0 %collective-permute-start.8 = (bf16[1552,256]{1,0:T(8,128)(2,1)}, bf16[1552,256]{1,0:T(8,128)(2,1)S(1)}, u32[]{:S(2)}, u32[]{:S(2)}) collective-permute-start(bf16[1552,256]{1,0:T(8,128)(2,1)} %get-tuple-element.91), channel_id=1, source_target_pairs={{0,16},{4,20},{8,24},{12,28},{16,0},{20,4},{24,8},{28,12},{1,17},{... | collective-permute-start | bytes 2383880 | tf_op jit(solution)/shard_map/ppermute | solution.py:553
  169.6 67.7 %collective-permute-start.9 = (bf16[1552,256]{1,0:T(8,128)(2,1)}, bf16[1552,256]{1,0:T(8,128)(2,1)S(1)}, u32[]{:S(2)}, u32[]{:S(2)}) collective-permute-start(bf16[1552,256]{1,0:T(8,128)(2,1)} %get-tuple-element.92), channel_id=1, source_target_pairs={{0,16},{4,20},{8,24},{12,28},{16,0},{20,4},{24,8},{28,12},{1,17},{... | collective-permute-start | bytes 2383880 | tf_op jit(solution)/shard_map/ppermute | solution.py:553
  209.0 51.1 %collective-permute-start.15 = (bf16[88,32,128]{2,1,0:T(8,128)(2,1)S(1)}, bf16[88,32,128]{2,1,0:T(8,128)(2,1)S(1)}, u32[]{:S(2)}, u32[]{:S(2)}) collective-permute-start(bf16[88,32,128]{2,1,0:T(8,128)(2,1)S(1)} %copy-done.16), channel_id=1, source_target_pairs={{0,4},{4,0},{8,12},{12,8},{16,20},{20,16},{24,28},{28,24},{1,5},{5... | collective-permute-start | bytes 2162696 | tf_op jit(solution)/shard_map/ppermute | solution.py:536
  211.2 49.7 %collective-permute-start.16 = (bf16[88,32,128]{2,1,0:T(8,128)(2,1)S(1)}, bf16[88,32,128]{2,1,0:T(8,128)(2,1)S(1)}, u32[]{:S(2)}, u32[]{:S(2)}) collective-permute-start(bf16[88,32,128]{2,1,0:T(8,128)(2,1)S(1)} %copy-done.15), channel_id=1, source_target_pairs={{0,8},{4,12},{8,0},{12,4},{16,24},{20,28},{24,16},{28,20},{1,9},{5... | collective-permute-start | bytes 2162696 | tf_op jit(solution)/shard_map/ppermute | solution.py:536
  211.2 60.6 %collective-permute-start.17 = (bf16[88,32,128]{2,1,0:T(8,128)(2,1)S(1)}, bf16[88,32,128]{2,1,0:T(8,128)(2,1)S(1)}, u32[]{:S(2)}, u32[]{:S(2)}) collective-permute-start(bf16[88,32,128]{2,1,0:T(8,128)(2,1)S(1)} %copy-done.14), channel_id=1, source_target_pairs={{0,12},{4,8},{8,4},{12,0},{16,28},{20,24},{24,20},{28,16},{1,13},{... | collective-permute-start | bytes 2162696 | tf_op jit(solution)/shard_map/ppermute | solution.py:536
  234.1 26.0 %copy-start.2 = (bf16[1552,256]{1,0:T(8,128)(2,1)}, bf16[1552,256]{1,0:T(8,128)(2,1)S(1)}, u32[]{:S(2)}) copy-start(bf16[1552,256]{1,0:T(8,128)(2,1)S(1)} %collective-permute-done.8.first_ref) | copy-start | bytes 2383876
  237.2 22.8 %copy-start.3 = (bf16[1552,256]{1,0:T(8,128)(2,1)}, bf16[1552,256]{1,0:T(8,128)(2,1)S(1)}, u32[]{:S(2)}) copy-start(bf16[1552,256]{1,0:T(8,128)(2,1)S(1)} %collective-permute-done.9.second_ref) | copy-start | bytes 2383876
  237.2 60.4 %collective-permute-start.10 = (bf16[1552,256]{1,0:T(8,128)(2,1)}, bf16[1552,256]{1,0:T(8,128)(2,1)S(1)}, u32[]{:S(2)}, u32[]{:S(2)}) collective-permute-start(bf16[1552,256]{1,0:T(8,128)(2,1)} %get-tuple-element.93), channel_id=1, source_target_pairs={{0,16},{4,20},{8,24},{12,28},{16,0},{20,4},{24,8},{28,12},{1,17},{... | collective-permute-start | bytes 2383880 | tf_op jit(solution)/shard_map/ppermute | solution.py:553
  237.2 69.2 %collective-permute-start.11 = (bf16[1552,256]{1,0:T(8,128)(2,1)}, bf16[1552,256]{1,0:T(8,128)(2,1)S(1)}, u32[]{:S(2)}, u32[]{:S(2)}) collective-permute-start(bf16[1552,256]{1,0:T(8,128)(2,1)} %get-tuple-element.94), channel_id=1, source_target_pairs={{0,16},{4,20},{8,24},{12,28},{16,0},{20,4},{24,8},{28,12},{1,17},{... | collective-permute-start | bytes 2383880 | tf_op jit(solution)/shard_map/ppermute | solution.py:553
  260.1 0.9 copy-start.6
  261.0 0.9 copy-start.7
  271.9 0.9 copy-start.8
  272.8 33.6 %collective-permute-start.18 = (bf16[88,32,128]{2,1,0:T(8,128)(2,1)}, bf16[88,32,128]{2,1,0:T(8,128)(2,1)S(1)}, u32[]{:S(2)}, u32[]{:S(2)}) collective-permute-start(bf16[88,32,128]{2,1,0:T(8,128)(2,1)} %get-tuple-element.117), channel_id=1, source_target_pairs={{0,4},{4,0},{8,12},{12,8},{16,20},{20,16},{24,28},{28,24},{1,5},{5... | collective-permute-start | bytes 2162696 | tf_op jit(solution)/shard_map/ppermute | solution.py:536
  274.1 36.2 %collective-permute-start.19 = (bf16[88,32,128]{2,1,0:T(8,128)(2,1)}, bf16[88,32,128]{2,1,0:T(8,128)(2,1)S(1)}, u32[]{:S(2)}, u32[]{:S(2)}) collective-permute-start(bf16[88,32,128]{2,1,0:T(8,128)(2,1)} %get-tuple-element.118), channel_id=1, source_target_pairs={{0,8},{4,12},{8,0},{12,4},{16,24},{20,28},{24,16},{28,20},{1,9},{5... | collective-permute-start | bytes 2162696 | tf_op jit(solution)/shard_map/ppermute | solution.py:536
  274.1 47.6 %collective-permute-start.20 = (bf16[88,32,128]{2,1,0:T(8,128)(2,1)}, bf16[88,32,128]{2,1,0:T(8,128)(2,1)}, u32[]{:S(2)}, u32[]{:S(2)}) collective-permute-start(bf16[88,32,128]{2,1,0:T(8,128)(2,1)} %get-tuple-element.119), channel_id=1, source_target_pairs={{0,12},{4,8},{8,4},{12,0},{16,28},{20,24},{24,20},{28,16},{1,13},{... | collective-permute-start | bytes 2162696 | tf_op jit(solution)/shard_map/ppermute | solution.py:536
  297.7 24.1 %copy-start.4 = (bf16[1552,256]{1,0:T(8,128)(2,1)}, bf16[1552,256]{1,0:T(8,128)(2,1)S(1)}, u32[]{:S(2)}) copy-start(bf16[1552,256]{1,0:T(8,128)(2,1)S(1)} %collective-permute-done.10.first_ref) | copy-start | bytes 2383876
  306.4 15.3 %copy-start.5 = (bf16[1552,256]{1,0:T(8,128)(2,1)}, bf16[1552,256]{1,0:T(8,128)(2,1)S(1)}, u32[]{:S(2)}) copy-start(bf16[1552,256]{1,0:T(8,128)(2,1)S(1)} %collective-permute-done.11.second_ref) | copy-start | bytes 2383876
  306.4 15.3 %copy-start.9 = (bf16[88,32,128]{2,1,0:T(8,128)(2,1)}, bf16[88,32,128]{2,1,0:T(8,128)(2,1)S(1)}, u32[]{:S(2)}) copy-start(bf16[88,32,128]{2,1,0:T(8,128)(2,1)S(1)} %collective-permute-done.18.rest_1_) | copy-start | bytes 2162692
  310.3 11.4 %copy-start.10 = (bf16[88,32,128]{2,1,0:T(8,128)(2,1)}, bf16[88,32,128]{2,1,0:T(8,128)(2,1)S(1)}, u32[]{:S(2)}) copy-start(bf16[88,32,128]{2,1,0:T(8,128)(2,1)S(1)} %collective-permute-done.19.rest_2_) | copy-start | bytes 2162692
  343.4 6.0 %collective-permute-start.21 = (bf16[2,48,384]{2,0,1:T(2,128)(2,1)S(1)}, bf16[2,48,384]{2,0,1:T(2,128)(2,1)S(1)}, u32[]{:S(2)}, u32[]{:S(2)}) collective-permute-start(bf16[2,48,384]{2,0,1:T(2,128)(2,1)S(1)} %slice.128), channel_id=1, source_target_pairs={{0,1},{1,2},{2,3},{4,5},{5,6},{6,7},{8,9},{9,10},{10,11},{12,13},{... | collective-permute-start | bytes 221192 | tf_op jit(solution)/shard_map/ppermute | solution.py:598
  345.7 10.0 %all-to-all-start = ((bf16[4,48,6,96]{3,1,2,0:T(8,128)(2,1)}), bf16[4,48,6,96]{3,1,2,0:T(8,128)(2,1)S(1)}, u32[]{:S(2)}, u32[]{:S(2)}) async-start(bf16[4,48,6,96]{3,1,2,0:T(8,128)(2,1)} %copy.17), calls=%async_computation | async-start | bytes 589824 | tf_op jit(solution)/shard_map/all_to_all | solution.py:606

commit v3 on v2

--- a/solution.py
+++ b/solution.py
@@ -304,7 +304,7 @@
 
 
 def finish_kernel(sources, low_ref, swap_ref, table_ref, first_ref, second_ref, ar_ref, half_ref, season_ref, *rest):
-    out_ref, misc_ref, flat_ref, slot_ref, turned_ref, innovation_ref, stacked_ref = rest[-7:]
+    out_ref, misc_ref, edge_ref, send_ref, flat_ref, slot_ref, turned_ref, innovation_ref, stacked_ref = rest[-9:]
     steps = table_ref.shape[1]
     days = out_ref.shape[0]
     degrees = out_ref.shape[3]
@@ -388,7 +388,12 @@
                     ]
             stacked = stacked_ref[part_of, 2 * days :, :]
             placed = jnp.where(degree[:TILE] >= start, pltpu.roll(stacked, shift, 1)[:, :degrees], 0.0)
-            misc_ref[slot] = placed[:8] + placed[8:]
+            placed = placed[:8] + placed[8:]
+            misc_ref[slot] = placed
+            edge_ref[slot] = placed.astype(jnp.bfloat16)
+            columns = send_ref.shape[3]
+            for peer in range(send_ref.shape[0]):
+                send_ref[peer, slot] = placed[:, peer * columns : (peer + 1) * columns].astype(jnp.bfloat16)
 
     by_halves(one)
 
@@ -433,7 +438,7 @@
     )(low, table, *blocks)
 
 
-def finish(chunk, low, swap, blocks, table, other, columns, season, held, slot_total, degrees):
+def finish(chunk, low, swap, blocks, table, other, columns, season, held, slot_total, degrees, time_count):
     lats, rows, days = blocks[0].shape
     steps, lat_half = table.shape[1:]
     pairs = TILE // 2
@@ -461,10 +466,14 @@
         out_specs=[
             pl.BlockSpec((days, 2, TILE, degrees), lambda i: (0, 0, chunk, 0)),
             leading((TILE, 8, degrees), 0),
+            leading((TILE, 8, degrees), 0),
+            leading((time_count, TILE, 8, degrees // time_count), 0),
         ],
         out_shape=[
             jax.ShapeDtypeStruct((days, 2, slot_total, degrees), jnp.bfloat16),
             jax.ShapeDtypeStruct((TILE, 8, degrees), jnp.float32),
+            jax.ShapeDtypeStruct((TILE, 8, degrees), jnp.bfloat16),
+            jax.ShapeDtypeStruct((time_count, TILE, 8, degrees // time_count), jnp.bfloat16),
         ],
         input_output_aliases=aliases,
         scratch_shapes=[
@@ -577,34 +586,34 @@
 
     own = [exchange(after(blocks[::chunks], ([far[-1][k] for k in across], own_table)), order)]
     innovation = None
-    misc = []
+    misc, carried, moved = [], [], []
+    route = [(i, i + 1) for i in range(time_count - 1)]
     for chunk in range(chunks):
         if chunk + 1 < chunks:
             crossed = own[-1]
             own.append(exchange(after(blocks[chunk + 1 :: chunks], (crossed, misc[:chunk])), order))
         span = slice(chunk * TILE // 2, (chunk + 1) * TILE // 2)
-        innovation, rows = finish(
-            chunk, own_low[span], swap[span], own[chunk], own_table, others[chunk], columns, season_rows,
-            innovation, slot_pad, degree_count,
+        innovation, rows, edges, sent = finish(
+            chunk, after(own_low[span], others[1:2]), swap[span], own[chunk], own_table, others[chunk], columns, season_rows,
+            innovation, slot_pad, degree_count, time_count,
         )
         misc.append(rows)
+        carried.append(edges)
+        moved.append(sent)
     innovation = innovation[:, :, :slot_count]
-    misc = jnp.concatenate(misc, axis=0)[:slot_count, :6]
+    carried = lax.ppermute(jnp.concatenate(carried, axis=0), "tm", route)
+    moved = lax.all_to_all(jnp.concatenate(moved, axis=1), "tm", 0, 0, tiled=True)
 
     degree_list = jnp.arange(degree_count, dtype=jnp.int32)
     valid_mask = (degree_list[None, :] >= slot_waves[:, None]).astype(jnp.float32)
-    edges = misc.transpose(1, 0, 2)
-    route = [(i, i + 1) for i in range(time_count - 1)]
-    carried = lax.ppermute(edges[0:4:2].astype(jnp.bfloat16), "tm", route).astype(jnp.float32)
+    first_day = jnp.stack([jnp.concatenate([rows[:, i] for rows in misc])[:slot_count] for i in (1, 3)])
+    last_day = jnp.stack([carried[:slot_count, i] for i in (0, 2)]).astype(jnp.float32)
     scale = jnp.exp(-0.5 * log_var) * lax.rsqrt(season[0]) * valid_mask
-    opening = ((edges[1:4:2] - ar_coef[None] * carried) * scale[None]).astype(jnp.bfloat16)
+    opening = ((first_day - ar_coef[None] * last_day) * scale[None]).astype(jnp.bfloat16)
     innovation = lax.dynamic_update_slice_in_dim(innovation, opening[None], 0, 0)
 
     column_width = degree_count // time_count
     place = lax.axis_index("tm")
-    columns = [misc[:, :, i * column_width : (i + 1) * column_width] for i in range(time_count)]
-    moved = lax.all_to_all(jnp.stack(columns).astype(jnp.bfloat16), "tm", 0, 0, tiled=True).astype(jnp.float32)
-
     def own_columns(values):
         return lax.dynamic_slice_in_dim(values, place * column_width, column_width, 1)
 
@@ -612,6 +621,7 @@
     first_days = day_of_year[0] + (jnp.arange(time_count, dtype=jnp.int32) - place) * day_count
     first_days = (first_days % 365).astype(jnp.float32)
     openness = 1.0 / (1.0 + 0.5 * jnp.cos(first_days * (2.0 * math.pi / 365.0)))
+    moved = moved[:, :slot_count].astype(jnp.float32)
     first = moved[:, :, 1:4:2]
     before = jnp.concatenate([jnp.zeros_like(moved[:1, :, 0:4:2]), moved[:-1, :, 0:4:2]], axis=0)
     residual = first - local_ar[None, :, None] * before

time: 359 us -> 364 us (1.014)
  other arithmetic: 12.9 us -> 16.6 us
  transfers between devices with their start and end apart: 23 -> 23, of which waited for: 10 -> 10; matrix products, arithmetic and copies ran while one was open for 6% -> 7% of each run, Pallas kernels for 41% -> 40%
where the time goes in v3:
time: 364 us; the launch traced here: 362 us
  Pallas kernels  183 us (50%)
  waiting for transfers between devices  112 us (31%)
  starting transfers between devices  32.6 us (9%)
  local copies, waits for them, and re-layouts  16.7 us (5%)
  other arithmetic  16.6 us (5%)
    ppermute x15, waiting for transfers between devices, exchange(): lax.ppermute(blocks[k], 'band', [(i, i ^ k) for i in range(band_count)])  92.5 us
    pallas_call x3, Pallas kernels, finish(): pl.pallas_call(functools.partial(finish_kernel, len(blocks)), grid=(1,),...  58 us
    pallas_call x3, Pallas kernels, longitude_sums(): pl.pallas_call(transform_kernel, grid=(lats // group,), in_specs=[pl.Bloc...  57.2 us
    pallas_call x2, Pallas kernels, packed_table(): pl.pallas_call(functools.partial(table_kernel, steps, lane_tiles, top), o...  25.8 us
    pallas_call x3, Pallas kernels, partial_sums(): pl.pallas_call(functools.partial(partial_kernel, degrees), grid=(1,), in_...  21.9 us
    ppermute x15, starting transfers between devices, exchange(): lax.ppermute(blocks[k], 'band', [(i, i ^ k) for i in range(band_count)])  18.8 us
    ppermute x6, waiting for transfers between devices, send_sums(): others.append([lax.ppermute(part, 'band', mirror) for part in sums])  11.9 us
    pallas_call x1, Pallas kernels, packed_columns(): pl.pallas_call(pack_kernel, in_specs=[pl.BlockSpec(memory_space=pltpu.SME...  11.3 us
  transfers between devices with their start and end apart: 23, of which 10 were waited for; matrix products, arithmetic and copies ran while one was open for 7% of the time, Pallas kernels for 40%

profile of v3, /device:TPU:0, one launch (start us, length us, event | category | flops | bytes accessed | tf_op | source)
XLA Modules:
  0.0 362.1 jit_solution(10485239930234118051)
XLA Ops:
  0.7 0.8 reshape.471
  3.4 0.7 pad_maximum_fusion.11
  4.1 2.2 shard_map.76.table_ref
  6.3 16.4 %shard_map.77 = (bf16[88,32,128]{2,1,0:T(8,128)(2,1)}, bf16[88,32,128]{2,1,0:T(8,128)(2,1)}, bf16[88,32,128]{2,1,0:T(8,128)(2,1)}, bf16[88,32,128]{2,1,0:T(8,128)(2,1)}) custom-call(bf16[88,1440,128]{2,1,0:T(8,128)(2,1)} %bitcast.65, bf16[128,1440]{1,0:T(8,128)(2,1)} %shard_map.76.table_ref), custom_call_target="tpu_custom_call" | custom-call | tf_op jit(solution)/shard_map/pallas_call | solution.py:80
  22.6 3.0 collective-permute-start
  25.6 1.6 collective-permute-start.1
  28.0 0.7 pad_maximum_fusion.9
  28.6 0.8 pad_maximum_fusion.7
  29.4 2.9 shard_map.78.table_ref
  32.3 19.1 %shard_map.79 = (bf16[88,64,128]{2,1,0:T(8,128)(2,1)}, bf16[88,64,128]{2,1,0:T(8,128)(2,1)}, bf16[88,64,128]{2,1,0:T(8,128)(2,1)}, bf16[88,64,128]{2,1,0:T(8,128)(2,1)}) custom-call(bf16[88,1440,128]{2,1,0:T(8,128)(2,1)} %bitcast.66, bf16[256,1440]{1,0:T(8,128)(2,1)} %shard_map.78.table_ref), custom_call_target="tpu_custom_call" | custom-call | tf_op jit(solution)/shard_map/pallas_call | solution.py:80
  51.3 1.9 collective-permute-start.3
  53.3 1.6 collective-permute-start.4
  57.4 0.8 dynamic_slice.72
  58.3 0.7 multiply_add_fusion.2
  61.0 13.0 %shard_map.80.table_ref = bf16[24,400,352]{2,1,0:T(8,128)(2,1)} custom-call(f32[24,128]{1,0:T(8,128)} %broadcast_in_dim.19.low_ref, f32[24,384]{1,0:T(8,128)} %get-tuple-element.196.first_ref, f32[24,384]{1,0:T(8,128)} %get-tuple-element.195.second_ref, f32[24,384]{1,0:T(8,128)} %broadcast_in_dim.20.cos_ref, f32[24,384]{1,0:T(8,128)} %broadcast_in_dim.21.weight_ref), custom_call_target="tpu_custom_call" | custom-call | tf_op jit(solution)/shard_map/pallas_call | solution.py:193
  74.0 7.2 %shard_map.81 = (bf16[1552,256]{1,0:T(8,128)(2,1)}, bf16[1552,256]{1,0:T(8,128)(2,1)}) custom-call(s32[8]{0:T(128)} %get-tuple-element.76.low_ref, bf16[24,400,352]{2,1,0:T(8,128)(2,1)} %shard_map.80.table_ref, bf16[88,32,128]{2,1,0:T(8,128)(2,1)} %get-tuple-element.73.rest_0_, bf16[88,32,128]{2,1,0:T(8,128)(2,1)} %collective-permute-done.rest_1_, ...), custom_call_target="tpu_custom_call" | custom-call | tf_op jit(solution)/shard_map/pallas_call | solution.py:422
  81.2 3.0 collective-permute-start.6
  84.2 0.9 fusion.14
  85.1 0.7 pad_maximum_fusion.4
  85.8 0.7 pad_maximum_fusion.5
  86.5 0.8 pad_maximum_fusion.3
  87.3 3.6 shard_map.82.table_ref
  90.9 21.7 %shard_map.83 = (bf16[88,32,128]{2,1,0:T(8,128)(2,1)}, bf16[88,32,128]{2,1,0:T(8,128)(2,1)}, bf16[88,32,128]{2,1,0:T(8,128)(2,1)}, bf16[88,32,128]{2,1,0:T(8,128...) custom-call(bf16[88,1440,128]{2,1,0:T(8,128)(2,1)} %bitcast.67, ...), custom_call_target="tpu_custom_call" | custom-call | tf_op jit(solution)/shard_map/pallas_call | solution.py:80
  112.8 0.7 multiply_add_fusion
  113.6 0.7 broadcast_in_dim.22.low_ref
  114.2 12.8 %shard_map.84.table_ref = bf16[24,400,352]{2,1,0:T(8,128)(2,1)} custom-call(f32[24,128]{1,0:T(8,128)} %broadcast_in_dim.22.low_ref, f32[24,384]{1,0:T(8,128)} %get-tuple-element.191.first_ref, f32[24,384]{1,0:T(8,128)} %get-tuple-element.190.second_ref, f32[24,384]{1,0:T(8,128)} %broadcast_in_dim.20.cos_ref, f32[24,384]{1,0:T(8,128)} %broadcast_in_dim.21.weight_ref), custom_call_target="tpu_custom_call" | custom-call | tf_op jit(solution)/shard_map/pallas_call | solution.py:193
  127.1 27.6 %collective-permute-done.5.rest_3_ = bf16[88,64,128]{2,1,0:T(8,128)(2,1)} collective-permute-done((bf16[88,64,128]{2,1,0:T(8,128)(2,1)}, bf16[88,64,128]{2,1,0:T(8,128)(2,1)}, u32[]{:S(2)}, u32[]{:S(2)}) %collective-permute-start.5) | collective-permute-done | bytes 1441824 | tf_op jit(solution)/shard_map/ppermute | solution.py:545
  154.6 1.7 collective-permute-start.12
  156.3 1.8 collective-permute-start.14
  159.8 7.3 %shard_map.85 = (bf16[1552,256]{1,0:T(8,128)(2,1)}, bf16[1552,256]{1,0:T(8,128)(2,1)}) custom-call(s32[8]{0:T(128)} %get-tuple-element.88.low_ref, bf16[24,400,352]{2,1,0:T(8,128)(2,1)} %shard_map.80.table_ref, bf16[88,64,128]{2,1,0:T(8,128)(2,1)} %get-tuple-element.75.rest_0_, bf16[88,64,128]{2,1,0:T(8,128)(2,1)} %copy-done, ...), custom_call_target="tpu_custom_call" | custom-call | tf_op jit(solution)/shard_map/pallas_call | solution.py:422
  167.1 2.5 collective-permute-start.8
  170.1 1.9 collective-permute-done.12.rest_1_
  172.0 25.1 %collective-permute-done.13.rest_2_ = bf16[88,32,128]{2,1,0:T(8,128)(2,1)} collective-permute-done((bf16[88,32,128]{2,1,0:T(8,128)(2,1)}, bf16[88,32,128]{2,1,0:T(8,128)(2,1)}, u32[]{:S(2)}, u32[]{:S(2)}) %collective-permute-start.13) | collective-permute-done | bytes 720928 | tf_op jit(solution)/shard_map/ppermute | solution.py:545
  197.0 12.0 %collective-permute-done.14.rest_3_ = bf16[88,32,128]{2,1,0:T(8,128)(2,1)} collective-permute-done((bf16[88,32,128]{2,1,0:T(8,128)(2,1)}, bf16[88,32,128]{2,1,0:T(8,128)(2,1)}, u32[]{:S(2)}, u32[]{:S(2)}) %collective-permute-start.14) | collective-permute-done | bytes 720928 | tf_op jit(solution)/shard_map/ppermute | solution.py:545
  209.0 2.2 collective-permute-start.15
  211.3 1.5 collective-permute-start.17
  212.9 0.9 select_maximum_fusion.in_ref
  213.8 11.3 %shard_map.86 = (f32[24,400,128]{2,1,0:T(8,128)}, f32[24,400,128]{2,1,0:T(8,128)}) custom-call(s32[24]{0:T(128)} %bitcast.87, f32[24,8,512]{2,1,0:T(8,128)} %select_maximum_fusion.in_ref), custom_call_target="tpu_custom_call" | custom-call | tf_op jit(solution)/shard_map/pallas_call | solution.py:298
  226.5 7.4 %shard_map.87 = (bf16[1552,256]{1,0:T(8,128)(2,1)}, bf16[1552,256]{1,0:T(8,128)(2,1)}) custom-call(s32[8]{0:T(128)} %get-tuple-element.100.low_ref, bf16[24,400,352]{2,1,0:T(8,128)(2,1)} %shard_map.80.table_ref, bf16[88,64,128]{2,1,0:T(8,128)(2,1)} %get-tuple-element.75.rest_0_, bf16[88,64,128]{2,1,0:T(8,128)(2,1)} %copy-done, ...), custom_call_target="tpu_custom_call" | custom-call | tf_op jit(solution)/shard_map/pallas_call | solution.py:422
  233.9 3.3 collective-permute-done.9.second_ref
  237.2 2.9 collective-permute-start.11
  240.2 19.3 %shard_map.88 = (bf16[128,2,48,384]{3,2,1,0:T(8,128)(2,1)}, f32[16,8,384]{2,1,0:T(8,128)}, bf16[16,8,384]{2,1,0:T(8,128)(2,1)}, bf16[4,16,8,96]{3,2,1,0:T(8,128)(2,1)}) custom-call(s32[8]{0:T(128)} %get-tuple-element.125.low_ref, s32[8]{0:T(128)} %get-tuple-element.200.swap_ref, bf16[24,400,352]{2,1,0:T(8,128)(2,1)} %shard_map.84.table_ref, ...), custom_call_target="tpu_custom_call" | custom-call | tf_op jit(solution)/shard_map/pallas_call | solution.py:462
  259.5 0.9 copy-done.6
  260.3 0.9 copy-done.7
  261.2 10.7 %collective-permute-done.17.rest_3_ = bf16[88,32,128]{2,1,0:T(8,128)(2,1)S(1)} collective-permute-done((bf16[88,32,128]{2,1,0:T(8,128)(2,1)S(1)}, bf16[88,32,128]{2,1,0:T(8,128)(2,1)S(1)}, u32[]{:S(2)}, u32[]{:S(2)}) %collective-permute-start.17) | collective-permute-done | bytes 720928 | tf_op jit(solution)/shard_map/ppermute | solution.py:545
  271.9 0.9 copy-done.8
  272.7 1.4 collective-permute-start.18
  274.2 2.0 collective-permute-start.20
  276.5 1.0 copy.25
  277.5 19.3 %shard_map.89 = (bf16[128,2,48,384]{3,2,1,0:T(8,128)(2,1)}, f32[16,8,384]{2,1,0:T(8,128)}, bf16[16,8,384]{2,1,0:T(8,128)(2,1)}, bf16[4,16,8,96]{3,2,1,0:T(8,128)(2,1)}) custom-call(s32[8]{0:T(128)} %get-tuple-element.131.low_ref, s32[8]{0:T(128)} %get-tuple-element.199.swap_ref, ...), custom_call_target="tpu_custom_call", output_to_operand_aliasing={{0}: (12, {})} | custom-call | tf_op jit(solution)/shard_map/pallas_call | solution.py:462
  296.8 1.0 copy.26
  297.8 8.6 %collective-permute-done.11.second_ref = bf16[1552,256]{1,0:T(8,128)(2,1)S(1)} collective-permute-done((bf16[1552,256]{1,0:T(8,128)(2,1)}, bf16[1552,256]{1,0:T(8,128)(2,1)S(1)}, u32[]{:S(2)}, u32[]{:S(2)}) %collective-permute-start.11) | collective-permute-done | bytes 794656 | tf_op jit(solution)/shard_map/ppermute | solution.py:562
  306.4 4.0 %collective-permute-done.19.rest_2_ = bf16[88,32,128]{2,1,0:T(8,128)(2,1)S(1)} collective-permute-done((bf16[88,32,128]{2,1,0:T(8,128)(2,1)}, bf16[88,32,128]{2,1,0:T(8,128)(2,1)S(1)}, u32[]{:S(2)}, u32[]{:S(2)}) %collective-permute-start.19) | collective-permute-done | bytes 720928 | tf_op jit(solution)/shard_map/ppermute | solution.py:545
  310.4 11.3 %collective-permute-done.20.rest_3_ = bf16[88,32,128]{2,1,0:T(8,128)(2,1)} collective-permute-done((bf16[88,32,128]{2,1,0:T(8,128)(2,1)}, bf16[88,32,128]{2,1,0:T(8,128)(2,1)}, u32[]{:S(2)}, u32[]{:S(2)}) %collective-permute-start.20) | collective-permute-done | bytes 720928 | tf_op jit(solution)/shard_map/ppermute | solution.py:545
  321.8 19.4 %shard_map.90 = (bf16[128,2,48,384]{3,2,1,0:T(8,128)(2,1)}, f32[16,8,384]{2,1,0:T(8,128)}, bf16[16,8,384]{2,1,0:T(8,128)(2,1)}, bf16[4,16,8,96]{3,2,1,0:T(8,128)(2,1)}) custom-call(s32[8]{0:T(128)} %get-tuple-element.96.low_ref, s32[8]{0:T(128)} %get-tuple-element.201.swap_ref, ...), custom_call_target="tpu_custom_call", output_to_operand_aliasing={{0}: (12, {})} | custom-call | tf_op jit(solution)/shard_map/pallas_call | solution.py:462
  341.1 0.9 slice.125
  342.1 1.0 copy.27
  343.1 0.9 pad_maximum_fusion.1
  344.0 1.3 collective-permute-start.21
  345.4 1.7 pad_maximum_fusion
  347.1 3.6 %all-to-all-start = ((bf16[4,48,8,96]{3,2,1,0:T(8,128)(2,1)}), bf16[4,48,8,96]{3,2,1,0:T(8,128)(2,1)S(1)}, u32[]{:S(2)}, u32[]{:S(2)}) async-start(bf16[4,48,8,96]{3,2,1,0:T(8,128)(2,1)} %pad_maximum_fusion), calls=%async_computation | async-start | bytes 786432 | tf_op jit(solution)/shard_map/all_to_all | solution.py:605
  350.8 7.4 %all-to-all-done = bf16[4,48,8,96]{3,2,1,0:T(8,128)(2,1)S(1)} async-done(((bf16[4,48,8,96]{3,2,1,0:T(8,128)(2,1)}), bf16[4,48,8,96]{3,2,1,0:T(8,128)(2,1)S(1)}, u32[]{:S(2)}, u32[]{:S(2)}) %all-to-all-start) | async-done | bytes 294944 | tf_op jit(solution)/shard_map/all_to_all | solution.py:605
  359.8 1.5 fusion.48
  361.4 0.7 fusion.18
  (123 shorter events, 12.9 us)
Async XLA Ops:
  22.6 34.5 %collective-permute-start = (bf16[88,32,128]{2,1,0:T(8,128)(2,1)}, bf16[88,32,128]{2,1,0:T(8,128)(2,1)}, u32[]{:S(2)}, u32[]{:S(2)}) collective-permute-start(bf16[88,32,128]{2,1,0:T(8,128)(2,1)} %get-tuple-element.78), channel_id=1, source_target_pairs={{0,4},{4,0},{8,12},{12,8},{16,20},{20,16},{24,28},{28,24},{1,5},{5... | collective-permute-start | bytes 2162696 | tf_op jit(solution)/shard_map/ppermute | solution.py:545
  25.6 48.4 %collective-permute-start.1 = (bf16[88,32,128]{2,1,0:T(8,128)(2,1)}, bf16[88,32,128]{2,1,0:T(8,128)(2,1)}, u32[]{:S(2)}, u32[]{:S(2)}) collective-permute-start(bf16[88,32,128]{2,1,0:T(8,128)(2,1)} %get-tuple-element.79), channel_id=1, source_target_pairs={{0,8},{4,12},{8,0},{12,4},{16,24},{20,28},{24,16},{28,20},{1,9},{5... | collective-permute-start | bytes 2162696 | tf_op jit(solution)/shard_map/ppermute | solution.py:545
  27.2 46.8 %collective-permute-start.2 = (bf16[88,32,128]{2,1,0:T(8,128)(2,1)}, bf16[88,32,128]{2,1,0:T(8,128)(2,1)}, u32[]{:S(2)}, u32[]{:S(2)}) collective-permute-start(bf16[88,32,128]{2,1,0:T(8,128)(2,1)} %get-tuple-element.80), channel_id=1, source_target_pairs={{0,12},{4,8},{8,4},{12,0},{16,28},{20,24},{24,20},{28,16},{1,13},{... | collective-permute-start | bytes 2162696 | tf_op jit(solution)/shard_map/ppermute | solution.py:545
  32.3 24.9 %copy-start.21 = (s32[128]{0:T(128)S(1)}, s32[128]{0:T(128)}, u32[]{:S(2)}) copy-start(s32[128]{0:T(128)} %param.7) | copy-start | bytes 1540
  51.3 105.0 %collective-permute-start.3 = (bf16[88,64,128]{2,1,0:T(8,128)(2,1)}, bf16[88,64,128]{2,1,0:T(8,128)(2,1)S(1)}, u32[]{:S(2)}, u32[]{:S(2)}) collective-permute-start(bf16[88,64,128]{2,1,0:T(8,128)(2,1)} %get-tuple-element.89), channel_id=1, source_target_pairs={{0,4},{4,0},{8,12},{12,8},{16,20},{20,16},{24,28},{28,24},{1,5},{5... | collective-permute-start | bytes 4325384 | tf_op jit(solution)/shard_map/ppermute | solution.py:545
  53.3 73.8 %collective-permute-start.4 = (bf16[88,64,128]{2,1,0:T(8,128)(2,1)}, bf16[88,64,128]{2,1,0:T(8,128)(2,1)S(1)}, u32[]{:S(2)}, u32[]{:S(2)}) collective-permute-start(bf16[88,64,128]{2,1,0:T(8,128)(2,1)} %get-tuple-element.90), channel_id=1, source_target_pairs={{0,8},{4,12},{8,0},{12,4},{16,24},{20,28},{24,16},{28,20},{1,9},{5... | collective-permute-start | bytes 4325384 | tf_op jit(solution)/shard_map/ppermute | solution.py:545
  57.1 97.5 %collective-permute-start.5 = (bf16[88,64,128]{2,1,0:T(8,128)(2,1)}, bf16[88,64,128]{2,1,0:T(8,128)(2,1)}, u32[]{:S(2)}, u32[]{:S(2)}) collective-permute-start(bf16[88,64,128]{2,1,0:T(8,128)(2,1)} %get-tuple-element.91), channel_id=1, source_target_pairs={{0,12},{4,8},{8,4},{12,0},{16,28},{20,24},{24,20},{28,16},{1,13},{... | collective-permute-start | bytes 4325384 | tf_op jit(solution)/shard_map/ppermute | solution.py:545
  57.4 102.3 %copy-start.17 = (s32[1,24]{1,0:T(1,128)}, s32[1,24]{1,0:T(1,128)S(1)}, u32[]{:S(2)}) copy-start(s32[1,24]{1,0:T(1,128)S(1)} %slice.101) | copy-start | bytes 292
  81.2 85.9 %collective-permute-start.6 = (bf16[1552,256]{1,0:T(8,128)(2,1)}, bf16[1552,256]{1,0:T(8,128)(2,1)}, u32[]{:S(2)}, u32[]{:S(2)}) collective-permute-start(bf16[1552,256]{1,0:T(8,128)(2,1)} %get-tuple-element.81), channel_id=1, source_target_pairs={{0,16},{4,20},{8,24},{12,28},{16,0},{20,4},{24,8},{28,12},{1,17},{... | collective-permute-start | bytes 2383880 | tf_op jit(solution)/shard_map/ppermute | solution.py:562
  84.1 83.0 %collective-permute-start.7 = (bf16[1552,256]{1,0:T(8,128)(2,1)}, bf16[1552,256]{1,0:T(8,128)(2,1)}, u32[]{:S(2)}, u32[]{:S(2)}) collective-permute-start(bf16[1552,256]{1,0:T(8,128)(2,1)} %get-tuple-element.82), channel_id=1, source_target_pairs={{0,16},{4,20},{8,24},{12,28},{16,0},{20,4},{24,8},{28,12},{1,17},{... | collective-permute-start | bytes 2383880 | tf_op jit(solution)/shard_map/ppermute | solution.py:562
  112.7 46.1 %copy-start.11 = (f32[48,384]{1,0:T(8,128)S(1)}, f32[48,384]{1,0:T(8,128)}, u32[]{:S(2)}) copy-start(f32[48,384]{1,0:T(8,128)} %param.8) | copy-start | bytes 221188
  112.7 46.5 %copy-start.12 = (f32[48,384]{1,0:T(8,128)S(1)}, f32[48,384]{1,0:T(8,128)}, u32[]{:S(2)}) copy-start(f32[48,384]{1,0:T(8,128)} %param.9) | copy-start | bytes 221188
  127.1 32.6 %copy-start.1 = (bf16[88,64,128]{2,1,0:T(8,128)(2,1)}, bf16[88,64,128]{2,1,0:T(8,128)(2,1)S(1)}, u32[]{:S(2)}) copy-start(bf16[88,64,128]{2,1,0:T(8,128)(2,1)S(1)} %collective-permute-done.4.rest_2_) | copy-start | bytes 4325380
  154.6 17.3 %collective-permute-start.12 = (bf16[88,32,128]{2,1,0:T(8,128)(2,1)}, bf16[88,32,128]{2,1,0:T(8,128)(2,1)}, u32[]{:S(2)}, u32[]{:S(2)}) collective-permute-start(bf16[88,32,128]{2,1,0:T(8,128)(2,1)} %get-tuple-element.118), channel_id=1, source_target_pairs={{0,4},{4,0},{8,12},{12,8},{16,20},{20,16},{24,28},{28,24},{1,5},{5... | collective-permute-start | bytes 2162696 | tf_op jit(solution)/shard_map/ppermute | solution.py:545
  156.3 40.7 %collective-permute-start.13 = (bf16[88,32,128]{2,1,0:T(8,128)(2,1)}, bf16[88,32,128]{2,1,0:T(8,128)(2,1)}, u32[]{:S(2)}, u32[]{:S(2)}) collective-permute-start(bf16[88,32,128]{2,1,0:T(8,128)(2,1)} %get-tuple-element.119), channel_id=1, source_target_pairs={{0,8},{4,12},{8,0},{12,4},{16,24},{20,28},{24,16},{28,20},{1,9},{5... | collective-permute-start | bytes 2162696 | tf_op jit(solution)/shard_map/ppermute | solution.py:545
  156.3 3.4 copy-start
  156.3 52.7 %collective-permute-start.14 = (bf16[88,32,128]{2,1,0:T(8,128)(2,1)}, bf16[88,32,128]{2,1,0:T(8,128)(2,1)}, u32[]{:S(2)}, u32[]{:S(2)}) collective-permute-start(bf16[88,32,128]{2,1,0:T(8,128)(2,1)} %get-tuple-element.120), channel_id=1, source_target_pairs={{0,12},{4,8},{8,4},{12,0},{16,28},{20,24},{24,20},{28,16},{1,13},{... | collective-permute-start | bytes 2162696 | tf_op jit(solution)/shard_map/ppermute | solution.py:545
  159.7 51.5 %copy-start.20 = (bf16[88,32,128]{2,1,0:T(8,128)(2,1)S(1)}, bf16[88,32,128]{2,1,0:T(8,128)(2,1)}, u32[]{:S(2)}) copy-start(bf16[88,32,128]{2,1,0:T(8,128)(2,1)} %get-tuple-element.123) | copy-start | bytes 2162692
  159.8 51.5 %copy-start.19 = (bf16[88,32,128]{2,1,0:T(8,128)(2,1)S(1)}, bf16[88,32,128]{2,1,0:T(8,128)(2,1)}, u32[]{:S(2)}) copy-start(bf16[88,32,128]{2,1,0:T(8,128)(2,1)} %get-tuple-element.124) | copy-start | bytes 2162692
  159.8 65.4 %copy-start.18 = (s32[1,24]{1,0:T(1,128)S(1)}, s32[1,24]{1,0:T(1,128)}, u32[]{:S(2)}) copy-start(s32[1,24]{1,0:T(1,128)} %copy-done.17) | copy-start | bytes 292
  167.1 66.8 %collective-permute-start.8 = (bf16[1552,256]{1,0:T(8,128)(2,1)}, bf16[1552,256]{1,0:T(8,128)(2,1)S(1)}, u32[]{:S(2)}, u32[]{:S(2)}) collective-permute-start(bf16[1552,256]{1,0:T(8,128)(2,1)} %get-tuple-element.94), channel_id=1, source_target_pairs={{0,16},{4,20},{8,24},{12,28},{16,0},{20,4},{24,8},{28,12},{1,17},{... | collective-permute-start | bytes 2383880 | tf_op jit(solution)/shard_map/ppermute | solution.py:562
  169.6 67.6 %collective-permute-start.9 = (bf16[1552,256]{1,0:T(8,128)(2,1)}, bf16[1552,256]{1,0:T(8,128)(2,1)S(1)}, u32[]{:S(2)}, u32[]{:S(2)}) collective-permute-start(bf16[1552,256]{1,0:T(8,128)(2,1)} %get-tuple-element.95), channel_id=1, source_target_pairs={{0,16},{4,20},{8,24},{12,28},{16,0},{20,4},{24,8},{28,12},{1,17},{... | collective-permute-start | bytes 2383880 | tf_op jit(solution)/shard_map/ppermute | solution.py:562
  209.0 50.4 %collective-permute-start.15 = (bf16[88,32,128]{2,1,0:T(8,128)(2,1)}, bf16[88,32,128]{2,1,0:T(8,128)(2,1)S(1)}, u32[]{:S(2)}, u32[]{:S(2)}) collective-permute-start(bf16[88,32,128]{2,1,0:T(8,128)(2,1)} %get-tuple-element.122), channel_id=1, source_target_pairs={{0,4},{4,0},{8,12},{12,8},{16,20},{20,16},{24,28},{28,24},{1,5},{5... | collective-permute-start | bytes 2162696 | tf_op jit(solution)/shard_map/ppermute | solution.py:545
  211.3 49.1 %collective-permute-start.16 = (bf16[88,32,128]{2,1,0:T(8,128)(2,1)S(1)}, bf16[88,32,128]{2,1,0:T(8,128)(2,1)S(1)}, u32[]{:S(2)}, u32[]{:S(2)}) collective-permute-start(bf16[88,32,128]{2,1,0:T(8,128)(2,1)S(1)} %copy-done.20), channel_id=1, source_target_pairs={{0,8},{4,12},{8,0},{12,4},{16,24},{20,28},{24,16},{28,20},{1,9},{5... | collective-permute-start | bytes 2162696 | tf_op jit(solution)/shard_map/ppermute | solution.py:545
  211.3 60.6 %collective-permute-start.17 = (bf16[88,32,128]{2,1,0:T(8,128)(2,1)S(1)}, bf16[88,32,128]{2,1,0:T(8,128)(2,1)S(1)}, u32[]{:S(2)}, u32[]{:S(2)}) collective-permute-start(bf16[88,32,128]{2,1,0:T(8,128)(2,1)S(1)} %copy-done.19), channel_id=1, source_target_pairs={{0,12},{4,8},{8,4},{12,0},{16,28},{20,24},{24,20},{28,16},{1,13},{... | collective-permute-start | bytes 2162696 | tf_op jit(solution)/shard_map/ppermute | solution.py:545
  233.9 25.5 %copy-start.2 = (bf16[1552,256]{1,0:T(8,128)(2,1)}, bf16[1552,256]{1,0:T(8,128)(2,1)S(1)}, u32[]{:S(2)}) copy-start(bf16[1552,256]{1,0:T(8,128)(2,1)S(1)} %collective-permute-done.8.first_ref) | copy-start | bytes 2383876
  237.2 22.2 %copy-start.3 = (bf16[1552,256]{1,0:T(8,128)(2,1)}, bf16[1552,256]{1,0:T(8,128)(2,1)S(1)}, u32[]{:S(2)}) copy-start(bf16[1552,256]{1,0:T(8,128)(2,1)S(1)} %collective-permute-done.9.second_ref) | copy-start | bytes 2383876
  237.2 60.5 %collective-permute-start.10 = (bf16[1552,256]{1,0:T(8,128)(2,1)}, bf16[1552,256]{1,0:T(8,128)(2,1)S(1)}, u32[]{:S(2)}, u32[]{:S(2)}) collective-permute-start(bf16[1552,256]{1,0:T(8,128)(2,1)} %get-tuple-element.103), channel_id=1, source_target_pairs={{0,16},{4,20},{8,24},{12,28},{16,0},{20,4},{24,8},{28,12},{1,17},{... | collective-permute-start | bytes 2383880 | tf_op jit(solution)/shard_map/ppermute | solution.py:562
  237.2 69.1 %collective-permute-start.11 = (bf16[1552,256]{1,0:T(8,128)(2,1)}, bf16[1552,256]{1,0:T(8,128)(2,1)S(1)}, u32[]{:S(2)}, u32[]{:S(2)}) collective-permute-start(bf16[1552,256]{1,0:T(8,128)(2,1)} %get-tuple-element.104), channel_id=1, source_target_pairs={{0,16},{4,20},{8,24},{12,28},{16,0},{20,4},{24,8},{28,12},{1,17},{... | collective-permute-start | bytes 2383880 | tf_op jit(solution)/shard_map/ppermute | solution.py:562
  259.5 0.9 copy-start.6
  260.3 0.9 copy-start.7
  271.9 0.9 copy-start.8
  272.7 33.6 %collective-permute-start.18 = (bf16[88,32,128]{2,1,0:T(8,128)(2,1)}, bf16[88,32,128]{2,1,0:T(8,128)(2,1)S(1)}, u32[]{:S(2)}, u32[]{:S(2)}) collective-permute-start(bf16[88,32,128]{2,1,0:T(8,128)(2,1)} %get-tuple-element.128), channel_id=1, source_target_pairs={{0,4},{4,0},{8,12},{12,8},{16,20},{20,16},{24,28},{28,24},{1,5},{5... | collective-permute-start | bytes 2162696 | tf_op jit(solution)/shard_map/ppermute | solution.py:545
  274.2 36.2 %collective-permute-start.19 = (bf16[88,32,128]{2,1,0:T(8,128)(2,1)}, bf16[88,32,128]{2,1,0:T(8,128)(2,1)S(1)}, u32[]{:S(2)}, u32[]{:S(2)}) collective-permute-start(bf16[88,32,128]{2,1,0:T(8,128)(2,1)} %get-tuple-element.129), channel_id=1, source_target_pairs={{0,8},{4,12},{8,0},{12,4},{16,24},{20,28},{24,16},{28,20},{1,9},{5... | collective-permute-start | bytes 2162696 | tf_op jit(solution)/shard_map/ppermute | solution.py:545
  274.2 47.5 %collective-permute-start.20 = (bf16[88,32,128]{2,1,0:T(8,128)(2,1)}, bf16[88,32,128]{2,1,0:T(8,128)(2,1)}, u32[]{:S(2)}, u32[]{:S(2)}) collective-permute-start(bf16[88,32,128]{2,1,0:T(8,128)(2,1)} %get-tuple-element.130), channel_id=1, source_target_pairs={{0,12},{4,8},{8,4},{12,0},{16,28},{20,24},{24,20},{28,16},{1,13},{... | collective-permute-start | bytes 2162696 | tf_op jit(solution)/shard_map/ppermute | solution.py:545
  297.8 23.9 %copy-start.4 = (bf16[1552,256]{1,0:T(8,128)(2,1)}, bf16[1552,256]{1,0:T(8,128)(2,1)S(1)}, u32[]{:S(2)}) copy-start(bf16[1552,256]{1,0:T(8,128)(2,1)S(1)} %collective-permute-done.10.first_ref) | copy-start | bytes 2383876
  306.4 15.3 %copy-start.5 = (bf16[1552,256]{1,0:T(8,128)(2,1)}, bf16[1552,256]{1,0:T(8,128)(2,1)S(1)}, u32[]{:S(2)}) copy-start(bf16[1552,256]{1,0:T(8,128)(2,1)S(1)} %collective-permute-done.11.second_ref) | copy-start | bytes 2383876
  306.4 15.3 %copy-start.9 = (bf16[88,32,128]{2,1,0:T(8,128)(2,1)}, bf16[88,32,128]{2,1,0:T(8,128)(2,1)S(1)}, u32[]{:S(2)}) copy-start(bf16[88,32,128]{2,1,0:T(8,128)(2,1)S(1)} %collective-permute-done.18.rest_1_) | copy-start | bytes 2162692
  310.4 11.4 %copy-start.10 = (bf16[88,32,128]{2,1,0:T(8,128)(2,1)}, bf16[88,32,128]{2,1,0:T(8,128)(2,1)S(1)}, u32[]{:S(2)}) copy-start(bf16[88,32,128]{2,1,0:T(8,128)(2,1)S(1)} %collective-permute-done.19.rest_2_) | copy-start | bytes 2162692
  321.7 21.4 %copy-start.15 = (bf16[16,8,384]{2,1,0:T(8,128)(2,1)S(1)}, bf16[16,8,384]{2,1,0:T(8,128)(2,1)}, u32[]{:S(2)}) copy-start(bf16[16,8,384]{2,1,0:T(8,128)(2,1)} %get-tuple-element.137) | copy-start | bytes 294916
  321.7 21.4 %copy-start.16 = (bf16[16,8,384]{2,1,0:T(8,128)(2,1)S(1)}, bf16[16,8,384]{2,1,0:T(8,128)(2,1)}, u32[]{:S(2)}) copy-start(bf16[16,8,384]{2,1,0:T(8,128)(2,1)} %get-tuple-element.138) | copy-start | bytes 294916
  321.7 23.6 %copy-start.13 = (bf16[4,16,8,96]{3,2,1,0:T(8,128)(2,1)S(1)}, bf16[4,16,8,96]{3,2,1,0:T(8,128)(2,1)}, u32[]{:S(2)}) copy-start(bf16[4,16,8,96]{3,2,1,0:T(8,128)(2,1)} %get-tuple-element.140) | copy-start | bytes 294916
  321.8 23.6 %copy-start.14 = (bf16[4,16,8,96]{3,2,1,0:T(8,128)(2,1)S(1)}, bf16[4,16,8,96]{3,2,1,0:T(8,128)(2,1)}, u32[]{:S(2)}) copy-start(bf16[4,16,8,96]{3,2,1,0:T(8,128)(2,1)} %get-tuple-element.141) | copy-start | bytes 294916
  344.0 17.3 %collective-permute-start.21 = (bf16[48,8,384]{2,1,0:T(8,128)(2,1)S(1)}, bf16[48,8,384]{2,1,0:T(8,128)(2,1)S(1)}, u32[]{:S(2)}, u32[]{:S(2)}) collective-permute-start(bf16[48,8,384]{2,1,0:T(8,128)(2,1)S(1)} %pad_maximum_fusion.1), channel_id=1, source_target_pairs={{0,1},{1,2},{2,3},{4,5},{5,6},{6,7},{8,9},{9,10},{10,11},{12,13},{... | collective-permute-start | bytes 884744 | tf_op jit(solution)/shard_map/ppermute | solution.py:604
  347.1 11.1 %all-to-all-start = ((bf16[4,48,8,96]{3,2,1,0:T(8,128)(2,1)}), bf16[4,48,8,96]{3,2,1,0:T(8,128)(2,1)S(1)}, u32[]{:S(2)}, u32[]{:S(2)}) async-start(bf16[4,48,8,96]{3,2,1,0:T(8,128)(2,1)} %pad_maximum_fusion), calls=%async_computation | async-start | bytes 786432 | tf_op jit(solution)/shard_map/all_to_all | solution.py:605

commit v4 on v2

--- a/solution.py
+++ b/solution.py
@@ -74,7 +74,7 @@
 
 def longitude_sums(fields, table, block_rows):
     lats, lon_count, days = fields.shape
-    group = 8 if lats % 8 == 0 else 2
+    group = 22 if lats % 22 == 0 else 2
     rows = table.shape[0]
     blocks = rows // block_rows
     return pl.pallas_call(

time: 359 us -> 355 us (0.989)
  Pallas kernels: 183 us -> 175 us
  waiting for transfers between devices: 109 us -> 114 us
    pallas_call x3, Pallas kernels: 57.2 us -> 49.1 us  [longitude_sums(): pl.pallas_call(transform_kernel, grid=(lats // group,), in_specs=[pl.Bloc...]
    ppermute x15, waiting for transfers between devices: 91.9 us -> 96.8 us  [exchange(): lax.ppermute(blocks[k], 'band', [(i, i ^ k) for i in range(band_count)])]
  transfers between devices with their start and end apart: 23 -> 23, of which waited for: 10 -> 11; matrix products, arithmetic and copies ran while one was open for 6% -> 6% of each run, Pallas kernels for 41% -> 39%
where the time goes in v4:
time: 355 us
  Pallas kernels  175 us (49%)
  waiting for transfers between devices  114 us (32%)
  starting transfers between devices  32.7 us (9%)
  local copies, waits for them, and re-layouts  18.5 us (5%)
  other arithmetic  12.9 us (4%)
    ppermute x15, waiting for transfers between devices, exchange(): lax.ppermute(blocks[k], 'band', [(i, i ^ k) for i in range(band_count)])  96.8 us
    pallas_call x3, Pallas kernels, finish(): pl.pallas_call(functools.partial(finish_kernel, len(blocks)), grid=(1,),...  58 us
    pallas_call x3, Pallas kernels, longitude_sums(): pl.pallas_call(transform_kernel, grid=(lats // group,), in_specs=[pl.Bloc...  49.1 us
    pallas_call x2, Pallas kernels, packed_table(): pl.pallas_call(functools.partial(table_kernel, steps, lane_tiles, top), o...  26 us
    pallas_call x3, Pallas kernels, partial_sums(): pl.pallas_call(functools.partial(partial_kernel, degrees), grid=(1,), in_...  21.8 us
    ppermute x15, starting transfers between devices, exchange(): lax.ppermute(blocks[k], 'band', [(i, i ^ k) for i in range(band_count)])  18.9 us
    ppermute x6, waiting for transfers between devices, send_sums(): others.append([lax.ppermute(part, 'band', mirror) for part in sums])  11.9 us
    pallas_call x1, Pallas kernels, packed_columns(): pl.pallas_call(pack_kernel, in_specs=[pl.BlockSpec(memory_space=pltpu.SME...  11.4 us
  transfers between devices with their start and end apart: 23, of which 11 were waited for; matrix products, arithmetic and copies ran while one was open for 6% of the time, Pallas kernels for 39%

profile of v4, /device:TPU:0, one launch (start us, length us, event | category | flops | bytes accessed | tf_op | source)
XLA Modules:
  0.0 354.6 jit_solution(1273893606394585309)
XLA Ops:
  0.7 0.8 reshape.400
  3.4 0.7 pad_maximum_fusion.10
  4.1 2.2 shard_map.76.table_ref
  6.2 13.3 %shard_map.77 = (bf16[88,32,128]{2,1,0:T(8,128)(2,1)}, bf16[88,32,128]{2,1,0:T(8,128)(2,1)}, bf16[88,32,128]{2,1,0:T(8,128)(2,1)}, bf16[88,32,128]{2,1,0:T(8,128)(2,1)}) custom-call(bf16[88,1440,128]{2,1,0:T(8,128)(2,1)} %bitcast.56, bf16[128,1440]{1,0:T(8,128)(2,1)} %shard_map.76.table_ref), custom_call_target="tpu_custom_call" | custom-call | tf_op jit(solution)/shard_map/pallas_call | solution.py:80
  19.5 3.0 collective-permute-start
  22.5 1.6 collective-permute-start.1
  24.9 0.7 pad_maximum_fusion.8
  25.5 0.8 pad_maximum_fusion.6
  26.3 2.9 shard_map.78.table_ref
  29.2 16.2 %shard_map.79 = (bf16[88,64,128]{2,1,0:T(8,128)(2,1)}, bf16[88,64,128]{2,1,0:T(8,128)(2,1)}, bf16[88,64,128]{2,1,0:T(8,128)(2,1)}, bf16[88,64,128]{2,1,0:T(8,128)(2,1)}) custom-call(bf16[88,1440,128]{2,1,0:T(8,128)(2,1)} %bitcast.57, bf16[256,1440]{1,0:T(8,128)(2,1)} %shard_map.78.table_ref), custom_call_target="tpu_custom_call" | custom-call | tf_op jit(solution)/shard_map/pallas_call | solution.py:80
  45.4 1.9 collective-permute-start.3
  47.3 1.6 collective-permute-start.4
  51.4 0.8 dynamic_slice.72
  52.4 0.7 multiply_add_fusion.2
  55.0 13.0 %shard_map.80.table_ref = bf16[24,400,352]{2,1,0:T(8,128)(2,1)} custom-call(f32[24,128]{1,0:T(8,128)} %broadcast_in_dim.21.low_ref, f32[24,384]{1,0:T(8,128)} %get-tuple-element.176.first_ref, f32[24,384]{1,0:T(8,128)} %get-tuple-element.175.second_ref, f32[24,384]{1,0:T(8,128)} %broadcast_in_dim.22.cos_ref, f32[24,384]{1,0:T(8,128)} %broadcast_in_dim.23.weight_ref), custom_call_target="tpu_custom_call" | custom-call | tf_op jit(solution)/shard_map/pallas_call | solution.py:193
  68.0 7.2 %shard_map.81 = (bf16[1552,256]{1,0:T(8,128)(2,1)}, bf16[1552,256]{1,0:T(8,128)(2,1)}) custom-call(s32[8]{0:T(128)} %get-tuple-element.67.low_ref, bf16[24,400,352]{2,1,0:T(8,128)(2,1)} %shard_map.80.table_ref, bf16[88,32,128]{2,1,0:T(8,128)(2,1)} %get-tuple-element.64.rest_0_, bf16[88,32,128]{2,1,0:T(8,128)(2,1)} %collective-permute-done.rest_1_, ...), custom_call_target="tpu_custom_call" | custom-call | tf_op jit(solution)/shard_map/pallas_call | solution.py:417
  75.2 3.0 collective-permute-start.6
  78.2 0.9 fusion.13
  79.1 0.7 pad_maximum_fusion.3
  79.8 0.7 pad_maximum_fusion.4
  80.5 0.8 pad_maximum_fusion.2
  81.3 3.6 %shard_map.82.table_ref = bf16[384,1440]{1,0:T(8,128)(2,1)} custom-call(f32[384,128]{1,0:T(8,128)} %bitcast.63, f32[384,128]{1,0:T(8,128)} %bitcast.62, f32[384,128]{1,0:T(8,128)} %bitcast.60, f32[384,128]{1,0:T(8,128)} %bitcast.61), custom_call_target="tpu_custom_call" | custom-call | tf_op jit(solution)/shard_map/pallas_call | solution.py:50
  84.9 19.6 %shard_map.83 = (bf16[88,32,128]{2,1,0:T(8,128)(2,1)}, bf16[88,32,128]{2,1,0:T(8,128)(2,1)}, bf16[88,32,128]{2,1,0:T(8,128)(2,1)}, bf16[88,32,128]{2,1,0:T(8,128...) custom-call(bf16[88,1440,128]{2,1,0:T(8,128)(2,1)} %bitcast.58, ...), custom_call_target="tpu_custom_call" | custom-call | tf_op jit(solution)/shard_map/pallas_call | solution.py:80
  104.7 0.7 multiply_add_fusion
  105.4 0.7 broadcast_in_dim.24.low_ref
  106.1 13.0 %shard_map.84.table_ref = bf16[24,400,352]{2,1,0:T(8,128)(2,1)} custom-call(f32[24,128]{1,0:T(8,128)} %broadcast_in_dim.24.low_ref, f32[24,384]{1,0:T(8,128)} %get-tuple-element.171.first_ref, f32[24,384]{1,0:T(8,128)} %get-tuple-element.170.second_ref, f32[24,384]{1,0:T(8,128)} %broadcast_in_dim.22.cos_ref, f32[24,384]{1,0:T(8,128)} %broadcast_in_dim.23.weight_ref), custom_call_target="tpu_custom_call" | custom-call | tf_op jit(solution)/shard_map/pallas_call | solution.py:193
  119.1 3.1 collective-permute-done.4.rest_2_
  122.2 29.3 %collective-permute-done.5.rest_3_ = bf16[88,64,128]{2,1,0:T(8,128)(2,1)} collective-permute-done((bf16[88,64,128]{2,1,0:T(8,128)(2,1)}, bf16[88,64,128]{2,1,0:T(8,128)(2,1)}, u32[]{:S(2)}, u32[]{:S(2)}) %collective-permute-start.5) | collective-permute-done | bytes 1441824 | tf_op jit(solution)/shard_map/ppermute | solution.py:536
  151.5 1.7 collective-permute-start.12
  153.2 1.8 collective-permute-start.14
  156.6 7.3 %shard_map.87 = (bf16[1552,256]{1,0:T(8,128)(2,1)}, bf16[1552,256]{1,0:T(8,128)(2,1)}) custom-call(s32[8]{0:T(128)} %get-tuple-element.88.low_ref, bf16[24,400,352]{2,1,0:T(8,128)(2,1)} %shard_map.80.table_ref, bf16[88,64,128]{2,1,0:T(8,128)(2,1)} %get-tuple-element.66.rest_0_, bf16[88,64,128]{2,1,0:T(8,128)(2,1)} %copy-done, ...), custom_call_target="tpu_custom_call" | custom-call | tf_op jit(solution)/shard_map/pallas_call | solution.py:417
  164.0 2.5 collective-permute-start.8
  167.0 1.8 collective-permute-done.12.rest_1_
  168.8 25.1 %collective-permute-done.13.rest_2_ = bf16[88,32,128]{2,1,0:T(8,128)(2,1)} collective-permute-done((bf16[88,32,128]{2,1,0:T(8,128)(2,1)}, bf16[88,32,128]{2,1,0:T(8,128)(2,1)}, u32[]{:S(2)}, u32[]{:S(2)}) %collective-permute-start.13) | collective-permute-done | bytes 720928 | tf_op jit(solution)/shard_map/ppermute | solution.py:536
  193.9 12.0 %collective-permute-done.14.rest_3_ = bf16[88,32,128]{2,1,0:T(8,128)(2,1)} collective-permute-done((bf16[88,32,128]{2,1,0:T(8,128)(2,1)}, bf16[88,32,128]{2,1,0:T(8,128)(2,1)}, u32[]{:S(2)}, u32[]{:S(2)}) %collective-permute-start.14) | collective-permute-done | bytes 720928 | tf_op jit(solution)/shard_map/ppermute | solution.py:536
  205.9 2.3 collective-permute-start.15
  208.2 1.5 collective-permute-start.17
  209.9 0.9 select_maximum_fusion.in_ref
  210.8 11.4 %shard_map.85 = (f32[24,400,128]{2,1,0:T(8,128)}, f32[24,400,128]{2,1,0:T(8,128)}) custom-call(s32[24]{0:T(128)} %bitcast.75, f32[24,8,512]{2,1,0:T(8,128)} %select_maximum_fusion.in_ref), custom_call_target="tpu_custom_call" | custom-call | tf_op jit(solution)/shard_map/pallas_call | solution.py:298
  222.2 1.4 fusion.92
  223.6 7.3 %shard_map.86 = (bf16[1552,256]{1,0:T(8,128)(2,1)}, bf16[1552,256]{1,0:T(8,128)(2,1)}) custom-call(s32[8]{0:T(128)} %get-tuple-element.82.low_ref, bf16[24,400,352]{2,1,0:T(8,128)(2,1)} %shard_map.80.table_ref, bf16[88,64,128]{2,1,0:T(8,128)(2,1)} %get-tuple-element.66.rest_0_, bf16[88,64,128]{2,1,0:T(8,128)(2,1)} %copy-done, ...), custom_call_target="tpu_custom_call" | custom-call | tf_op jit(solution)/shard_map/pallas_call | solution.py:417
  230.9 3.2 collective-permute-done.9.second_ref
  234.2 2.9 collective-permute-start.11
  237.7 19.2 %shard_map.88 = (bf16[128,2,48,384]{3,2,1,0:T(8,128)(2,1)}, f32[16,8,384]{2,1,0:T(8,128)}) custom-call(s32[8]{0:T(128)} %get-tuple-element.183.low_ref, s32[8]{0:T(128)} %get-tuple-element.180.swap_ref, bf16[24,400,352]{2,1,0:T(8,128)(2,1)} %shard_map.84.table_ref, bf16[1552,256]{1,0:T(8,128)(2,1)} %collective-permute-done.6.first_ref, ...), custom_call_target="tpu_custom_call" | custom-call | tf_op jit(solution)/shard_map/pallas_call | solution.py:457
  257.0 0.9 copy-done.6
  257.9 0.9 copy-done.7
  258.7 10.1 %collective-permute-done.17.rest_3_ = bf16[88,32,128]{2,1,0:T(8,128)(2,1)S(1)} collective-permute-done((bf16[88,32,128]{2,1,0:T(8,128)(2,1)S(1)}, bf16[88,32,128]{2,1,0:T(8,128)(2,1)S(1)}, u32[]{:S(2)}, u32[]{:S(2)}) %collective-permute-start.17) | collective-permute-done | bytes 720928 | tf_op jit(solution)/shard_map/ppermute | solution.py:536
  268.8 0.9 copy-done.8
  269.7 1.4 collective-permute-start.18
  271.1 2.1 collective-permute-start.20
  273.5 0.9 constant_dynamic-update-slice_fusion.2
  274.4 19.3 %shard_map.89 = (bf16[128,2,48,384]{3,2,1,0:T(8,128)(2,1)}, f32[16,8,384]{2,1,0:T(8,128)}) custom-call(s32[8]{0:T(128)} %get-tuple-element.182.low_ref, s32[8]{0:T(128)} %get-tuple-element.179.swap_ref, bf16[24,400,352]{2,1,0:T(8,128)(2,1)} %shard_map.84.table_ref, bf16[1552,256]{1,0:T(8,128)(2,1)} %copy-done.2, ...), custom_call_target="tpu_custom_call", output_to_operand_aliasing={{0}: (12, {})} | custom-call | tf_op jit(solution)/shard_map/pallas_call | solution.py:457
  293.7 0.9 constant_dynamic-update-slice_fusion.1
  294.6 8.6 %collective-permute-done.11.second_ref = bf16[1552,256]{1,0:T(8,128)(2,1)S(1)} collective-permute-done((bf16[1552,256]{1,0:T(8,128)(2,1)}, bf16[1552,256]{1,0:T(8,128)(2,1)S(1)}, u32[]{:S(2)}, u32[]{:S(2)}) %collective-permute-start.11) | collective-permute-done | bytes 794656 | tf_op jit(solution)/shard_map/ppermute | solution.py:553
  303.3 3.9 %collective-permute-done.19.rest_2_ = bf16[88,32,128]{2,1,0:T(8,128)(2,1)S(1)} collective-permute-done((bf16[88,32,128]{2,1,0:T(8,128)(2,1)}, bf16[88,32,128]{2,1,0:T(8,128)(2,1)S(1)}, u32[]{:S(2)}, u32[]{:S(2)}) %collective-permute-start.19) | collective-permute-done | bytes 720928 | tf_op jit(solution)/shard_map/ppermute | solution.py:536
  307.2 11.4 %collective-permute-done.20.rest_3_ = bf16[88,32,128]{2,1,0:T(8,128)(2,1)} collective-permute-done((bf16[88,32,128]{2,1,0:T(8,128)(2,1)}, bf16[88,32,128]{2,1,0:T(8,128)(2,1)}, u32[]{:S(2)}, u32[]{:S(2)}) %collective-permute-start.20) | collective-permute-done | bytes 720928 | tf_op jit(solution)/shard_map/ppermute | solution.py:536
  318.7 19.5 %shard_map.90 = (bf16[128,2,48,384]{3,2,1,0:T(8,128)(2,1)}, f32[16,8,384]{2,1,0:T(8,128)}) custom-call(s32[8]{0:T(128)} %get-tuple-element.184.low_ref, s32[8]{0:T(128)} %get-tuple-element.181.swap_ref, bf16[24,400,352]{2,1,0:T(8,128)(2,1)} %shard_map.84.table_ref, bf16[1552,256]{1,0:T(8,128)(2,1)} %copy-done.4, ...), custom_call_target="tpu_custom_call", output_to_operand_aliasing={{0}: (12, {})} | custom-call | tf_op jit(solution)/shard_map/pallas_call | solution.py:457
  338.2 0.9 constant_dynamic-update-slice_fusion
  339.8 0.7 slice.128
  340.5 1.3 collective-permute-start.21
  342.1 0.8 copy.17
  342.9 3.6 %all-to-all-start = ((bf16[4,48,6,96]{3,1,2,0:T(8,128)(2,1)}), bf16[4,48,6,96]{3,1,2,0:T(8,128)(2,1)S(1)}, u32[]{:S(2)}, u32[]{:S(2)}) async-start(bf16[4,48,6,96]{3,1,2,0:T(8,128)(2,1)} %copy.17), calls=%async_computation | async-start | bytes 589824 | tf_op jit(solution)/shard_map/all_to_all | solution.py:606
  347.3 5.6 %all-to-all-done = bf16[4,48,6,96]{3,1,2,0:T(8,128)(2,1)S(1)} async-done(((bf16[4,48,6,96]{3,1,2,0:T(8,128)(2,1)}), bf16[4,48,6,96]{3,1,2,0:T(8,128)(2,1)S(1)}, u32[]{:S(2)}, u32[]{:S(2)}) %all-to-all-start) | async-done | bytes 221216 | tf_op jit(solution)/shard_map/all_to_all | solution.py:606
  353.1 1.5 fusion.47
  (111 shorter events, 12.4 us)
Async XLA Ops:
  19.5 31.6 %collective-permute-start = (bf16[88,32,128]{2,1,0:T(8,128)(2,1)}, bf16[88,32,128]{2,1,0:T(8,128)(2,1)}, u32[]{:S(2)}, u32[]{:S(2)}) collective-permute-start(bf16[88,32,128]{2,1,0:T(8,128)(2,1)} %get-tuple-element.69), channel_id=1, source_target_pairs={{0,4},{4,0},{8,12},{12,8},{16,20},{20,16},{24,28},{28,24},{1,5},{5... | collective-permute-start | bytes 2162696 | tf_op jit(solution)/shard_map/ppermute | solution.py:536
  22.5 45.5 %collective-permute-start.1 = (bf16[88,32,128]{2,1,0:T(8,128)(2,1)}, bf16[88,32,128]{2,1,0:T(8,128)(2,1)}, u32[]{:S(2)}, u32[]{:S(2)}) collective-permute-start(bf16[88,32,128]{2,1,0:T(8,128)(2,1)} %get-tuple-element.70), channel_id=1, source_target_pairs={{0,8},{4,12},{8,0},{12,4},{16,24},{20,28},{24,16},{28,20},{1,9},{5... | collective-permute-start | bytes 2162696 | tf_op jit(solution)/shard_map/ppermute | solution.py:536
  24.1 43.9 %collective-permute-start.2 = (bf16[88,32,128]{2,1,0:T(8,128)(2,1)}, bf16[88,32,128]{2,1,0:T(8,128)(2,1)}, u32[]{:S(2)}, u32[]{:S(2)}) collective-permute-start(bf16[88,32,128]{2,1,0:T(8,128)(2,1)} %get-tuple-element.71), channel_id=1, source_target_pairs={{0,12},{4,8},{8,4},{12,0},{16,28},{20,24},{24,20},{28,16},{1,13},{... | collective-permute-start | bytes 2162696 | tf_op jit(solution)/shard_map/ppermute | solution.py:536
  29.2 22.0 %copy-start.17 = (s32[128]{0:T(128)S(1)}, s32[128]{0:T(128)}, u32[]{:S(2)}) copy-start(s32[128]{0:T(128)} %param.7) | copy-start | bytes 1540
  45.4 107.9 %collective-permute-start.3 = (bf16[88,64,128]{2,1,0:T(8,128)(2,1)}, bf16[88,64,128]{2,1,0:T(8,128)(2,1)S(1)}, u32[]{:S(2)}, u32[]{:S(2)}) collective-permute-start(bf16[88,64,128]{2,1,0:T(8,128)(2,1)} %get-tuple-element.83), channel_id=1, source_target_pairs={{0,4},{4,0},{8,12},{12,8},{16,20},{20,16},{24,28},{28,24},{1,5},{5... | collective-permute-start | bytes 4325384 | tf_op jit(solution)/shard_map/ppermute | solution.py:536
  47.3 74.9 %collective-permute-start.4 = (bf16[88,64,128]{2,1,0:T(8,128)(2,1)}, bf16[88,64,128]{2,1,0:T(8,128)(2,1)S(1)}, u32[]{:S(2)}, u32[]{:S(2)}) collective-permute-start(bf16[88,64,128]{2,1,0:T(8,128)(2,1)} %get-tuple-element.84), channel_id=1, source_target_pairs={{0,8},{4,12},{8,0},{12,4},{16,24},{20,28},{24,16},{28,20},{1,9},{5... | collective-permute-start | bytes 4325384 | tf_op jit(solution)/shard_map/ppermute | solution.py:536
  51.1 100.4 %collective-permute-start.5 = (bf16[88,64,128]{2,1,0:T(8,128)(2,1)}, bf16[88,64,128]{2,1,0:T(8,128)(2,1)}, u32[]{:S(2)}, u32[]{:S(2)}) collective-permute-start(bf16[88,64,128]{2,1,0:T(8,128)(2,1)} %get-tuple-element.85), channel_id=1, source_target_pairs={{0,12},{4,8},{8,4},{12,0},{16,28},{20,24},{24,20},{28,16},{1,13},{... | collective-permute-start | bytes 4325384 | tf_op jit(solution)/shard_map/ppermute | solution.py:536
  51.4 115.6 %copy-start.13 = (s32[1,24]{1,0:T(1,128)}, s32[1,24]{1,0:T(1,128)S(1)}, u32[]{:S(2)}) copy-start(s32[1,24]{1,0:T(1,128)S(1)} %slice.107) | copy-start | bytes 292
  75.2 88.8 %collective-permute-start.6 = (bf16[1552,256]{1,0:T(8,128)(2,1)}, bf16[1552,256]{1,0:T(8,128)(2,1)}, u32[]{:S(2)}, u32[]{:S(2)}) collective-permute-start(bf16[1552,256]{1,0:T(8,128)(2,1)} %get-tuple-element.72), channel_id=1, source_target_pairs={{0,16},{4,20},{8,24},{12,28},{16,0},{20,4},{24,8},{28,12},{1,17},{... | collective-permute-start | bytes 2383880 | tf_op jit(solution)/shard_map/ppermute | solution.py:553
  78.1 85.9 %collective-permute-start.7 = (bf16[1552,256]{1,0:T(8,128)(2,1)}, bf16[1552,256]{1,0:T(8,128)(2,1)}, u32[]{:S(2)}, u32[]{:S(2)}) collective-permute-start(bf16[1552,256]{1,0:T(8,128)(2,1)} %get-tuple-element.73), channel_id=1, source_target_pairs={{0,16},{4,20},{8,24},{12,28},{16,0},{20,4},{24,8},{28,12},{1,17},{... | collective-permute-start | bytes 2383880 | tf_op jit(solution)/shard_map/ppermute | solution.py:553
  104.6 51.1 %copy-start.11 = (f32[48,384]{1,0:T(8,128)S(1)}, f32[48,384]{1,0:T(8,128)}, u32[]{:S(2)}) copy-start(f32[48,384]{1,0:T(8,128)} %param.8) | copy-start | bytes 221188
  104.6 51.5 %copy-start.12 = (f32[48,384]{1,0:T(8,128)S(1)}, f32[48,384]{1,0:T(8,128)}, u32[]{:S(2)}) copy-start(f32[48,384]{1,0:T(8,128)} %param.9) | copy-start | bytes 221188
  122.2 34.4 %copy-start.1 = (bf16[88,64,128]{2,1,0:T(8,128)(2,1)}, bf16[88,64,128]{2,1,0:T(8,128)(2,1)S(1)}, u32[]{:S(2)}) copy-start(bf16[88,64,128]{2,1,0:T(8,128)(2,1)S(1)} %collective-permute-done.4.rest_2_) | copy-start | bytes 4325380
  151.5 17.3 %collective-permute-start.12 = (bf16[88,32,128]{2,1,0:T(8,128)(2,1)}, bf16[88,32,128]{2,1,0:T(8,128)(2,1)}, u32[]{:S(2)}, u32[]{:S(2)}) collective-permute-start(bf16[88,32,128]{2,1,0:T(8,128)(2,1)} %get-tuple-element.108), channel_id=1, source_target_pairs={{0,4},{4,0},{8,12},{12,8},{16,20},{20,16},{24,28},{28,24},{1,5},{5... | collective-permute-start | bytes 2162696 | tf_op jit(solution)/shard_map/ppermute | solution.py:536
  153.2 40.7 %collective-permute-start.13 = (bf16[88,32,128]{2,1,0:T(8,128)(2,1)}, bf16[88,32,128]{2,1,0:T(8,128)(2,1)}, u32[]{:S(2)}, u32[]{:S(2)}) collective-permute-start(bf16[88,32,128]{2,1,0:T(8,128)(2,1)} %get-tuple-element.109), channel_id=1, source_target_pairs={{0,8},{4,12},{8,0},{12,4},{16,24},{20,28},{24,16},{28,20},{1,9},{5... | collective-permute-start | bytes 2162696 | tf_op jit(solution)/shard_map/ppermute | solution.py:536
  153.2 3.4 copy-start
  153.2 52.7 %collective-permute-start.14 = (bf16[88,32,128]{2,1,0:T(8,128)(2,1)}, bf16[88,32,128]{2,1,0:T(8,128)(2,1)}, u32[]{:S(2)}, u32[]{:S(2)}) collective-permute-start(bf16[88,32,128]{2,1,0:T(8,128)(2,1)} %get-tuple-element.110), channel_id=1, source_target_pairs={{0,12},{4,8},{8,4},{12,0},{16,28},{20,24},{24,20},{28,16},{1,13},{... | collective-permute-start | bytes 2162696 | tf_op jit(solution)/shard_map/ppermute | solution.py:536
  156.6 49.3 %copy-start.16 = (bf16[88,32,128]{2,1,0:T(8,128)(2,1)S(1)}, bf16[88,32,128]{2,1,0:T(8,128)(2,1)}, u32[]{:S(2)}) copy-start(bf16[88,32,128]{2,1,0:T(8,128)(2,1)} %get-tuple-element.112) | copy-start | bytes 2162692
  156.6 51.6 %copy-start.15 = (bf16[88,32,128]{2,1,0:T(8,128)(2,1)S(1)}, bf16[88,32,128]{2,1,0:T(8,128)(2,1)}, u32[]{:S(2)}) copy-start(bf16[88,32,128]{2,1,0:T(8,128)(2,1)} %get-tuple-element.113) | copy-start | bytes 2162692
  156.6 51.6 %copy-start.14 = (bf16[88,32,128]{2,1,0:T(8,128)(2,1)S(1)}, bf16[88,32,128]{2,1,0:T(8,128)(2,1)}, u32[]{:S(2)}) copy-start(bf16[88,32,128]{2,1,0:T(8,128)(2,1)} %get-tuple-element.114) | copy-start | bytes 2162692
  164.0 66.9 %collective-permute-start.8 = (bf16[1552,256]{1,0:T(8,128)(2,1)}, bf16[1552,256]{1,0:T(8,128)(2,1)S(1)}, u32[]{:S(2)}, u32[]{:S(2)}) collective-permute-start(bf16[1552,256]{1,0:T(8,128)(2,1)} %get-tuple-element.91), channel_id=1, source_target_pairs={{0,16},{4,20},{8,24},{12,28},{16,0},{20,4},{24,8},{28,12},{1,17},{... | collective-permute-start | bytes 2383880 | tf_op jit(solution)/shard_map/ppermute | solution.py:553
  166.5 67.6 %collective-permute-start.9 = (bf16[1552,256]{1,0:T(8,128)(2,1)}, bf16[1552,256]{1,0:T(8,128)(2,1)S(1)}, u32[]{:S(2)}, u32[]{:S(2)}) collective-permute-start(bf16[1552,256]{1,0:T(8,128)(2,1)} %get-tuple-element.92), channel_id=1, source_target_pairs={{0,16},{4,20},{8,24},{12,28},{16,0},{20,4},{24,8},{28,12},{1,17},{... | collective-permute-start | bytes 2383880 | tf_op jit(solution)/shard_map/ppermute | solution.py:553
  205.9 51.1 %collective-permute-start.15 = (bf16[88,32,128]{2,1,0:T(8,128)(2,1)S(1)}, bf16[88,32,128]{2,1,0:T(8,128)(2,1)S(1)}, u32[]{:S(2)}, u32[]{:S(2)}) collective-permute-start(bf16[88,32,128]{2,1,0:T(8,128)(2,1)S(1)} %copy-done.16), channel_id=1, source_target_pairs={{0,4},{4,0},{8,12},{12,8},{16,20},{20,16},{24,28},{28,24},{1,5},{5... | collective-permute-start | bytes 2162696 | tf_op jit(solution)/shard_map/ppermute | solution.py:536
  208.2 49.7 %collective-permute-start.16 = (bf16[88,32,128]{2,1,0:T(8,128)(2,1)S(1)}, bf16[88,32,128]{2,1,0:T(8,128)(2,1)S(1)}, u32[]{:S(2)}, u32[]{:S(2)}) collective-permute-start(bf16[88,32,128]{2,1,0:T(8,128)(2,1)S(1)} %copy-done.15), channel_id=1, source_target_pairs={{0,8},{4,12},{8,0},{12,4},{16,24},{20,28},{24,16},{28,20},{1,9},{5... | collective-permute-start | bytes 2162696 | tf_op jit(solution)/shard_map/ppermute | solution.py:536
  208.2 60.7 %collective-permute-start.17 = (bf16[88,32,128]{2,1,0:T(8,128)(2,1)S(1)}, bf16[88,32,128]{2,1,0:T(8,128)(2,1)S(1)}, u32[]{:S(2)}, u32[]{:S(2)}) collective-permute-start(bf16[88,32,128]{2,1,0:T(8,128)(2,1)S(1)} %copy-done.14), channel_id=1, source_target_pairs={{0,12},{4,8},{8,4},{12,0},{16,28},{20,24},{24,20},{28,16},{1,13},{... | collective-permute-start | bytes 2162696 | tf_op jit(solution)/shard_map/ppermute | solution.py:536
  230.9 26.1 %copy-start.2 = (bf16[1552,256]{1,0:T(8,128)(2,1)}, bf16[1552,256]{1,0:T(8,128)(2,1)S(1)}, u32[]{:S(2)}) copy-start(bf16[1552,256]{1,0:T(8,128)(2,1)S(1)} %collective-permute-done.8.first_ref) | copy-start | bytes 2383876
  234.1 22.8 %copy-start.3 = (bf16[1552,256]{1,0:T(8,128)(2,1)}, bf16[1552,256]{1,0:T(8,128)(2,1)S(1)}, u32[]{:S(2)}) copy-start(bf16[1552,256]{1,0:T(8,128)(2,1)S(1)} %collective-permute-done.9.second_ref) | copy-start | bytes 2383876
  234.1 60.5 %collective-permute-start.10 = (bf16[1552,256]{1,0:T(8,128)(2,1)}, bf16[1552,256]{1,0:T(8,128)(2,1)S(1)}, u32[]{:S(2)}, u32[]{:S(2)}) collective-permute-start(bf16[1552,256]{1,0:T(8,128)(2,1)} %get-tuple-element.93), channel_id=1, source_target_pairs={{0,16},{4,20},{8,24},{12,28},{16,0},{20,4},{24,8},{28,12},{1,17},{... | collective-permute-start | bytes 2383880 | tf_op jit(solution)/shard_map/ppermute | solution.py:553
  234.2 69.1 %collective-permute-start.11 = (bf16[1552,256]{1,0:T(8,128)(2,1)}, bf16[1552,256]{1,0:T(8,128)(2,1)S(1)}, u32[]{:S(2)}, u32[]{:S(2)}) collective-permute-start(bf16[1552,256]{1,0:T(8,128)(2,1)} %get-tuple-element.94), channel_id=1, source_target_pairs={{0,16},{4,20},{8,24},{12,28},{16,0},{20,4},{24,8},{28,12},{1,17},{... | collective-permute-start | bytes 2383880 | tf_op jit(solution)/shard_map/ppermute | solution.py:553
  257.0 0.9 copy-start.6
  257.9 0.9 copy-start.7
  268.8 0.9 copy-start.8
  269.7 33.6 %collective-permute-start.18 = (bf16[88,32,128]{2,1,0:T(8,128)(2,1)}, bf16[88,32,128]{2,1,0:T(8,128)(2,1)S(1)}, u32[]{:S(2)}, u32[]{:S(2)}) collective-permute-start(bf16[88,32,128]{2,1,0:T(8,128)(2,1)} %get-tuple-element.117), channel_id=1, source_target_pairs={{0,4},{4,0},{8,12},{12,8},{16,20},{20,16},{24,28},{28,24},{1,5},{5... | collective-permute-start | bytes 2162696 | tf_op jit(solution)/shard_map/ppermute | solution.py:536
  271.1 36.2 %collective-permute-start.19 = (bf16[88,32,128]{2,1,0:T(8,128)(2,1)}, bf16[88,32,128]{2,1,0:T(8,128)(2,1)S(1)}, u32[]{:S(2)}, u32[]{:S(2)}) collective-permute-start(bf16[88,32,128]{2,1,0:T(8,128)(2,1)} %get-tuple-element.118), channel_id=1, source_target_pairs={{0,8},{4,12},{8,0},{12,4},{16,24},{20,28},{24,16},{28,20},{1,9},{5... | collective-permute-start | bytes 2162696 | tf_op jit(solution)/shard_map/ppermute | solution.py:536
  271.1 47.6 %collective-permute-start.20 = (bf16[88,32,128]{2,1,0:T(8,128)(2,1)}, bf16[88,32,128]{2,1,0:T(8,128)(2,1)}, u32[]{:S(2)}, u32[]{:S(2)}) collective-permute-start(bf16[88,32,128]{2,1,0:T(8,128)(2,1)} %get-tuple-element.119), channel_id=1, source_target_pairs={{0,12},{4,8},{8,4},{12,0},{16,28},{20,24},{24,20},{28,16},{1,13},{... | collective-permute-start | bytes 2162696 | tf_op jit(solution)/shard_map/ppermute | solution.py:536
  294.6 24.0 %copy-start.4 = (bf16[1552,256]{1,0:T(8,128)(2,1)}, bf16[1552,256]{1,0:T(8,128)(2,1)S(1)}, u32[]{:S(2)}) copy-start(bf16[1552,256]{1,0:T(8,128)(2,1)S(1)} %collective-permute-done.10.first_ref) | copy-start | bytes 2383876
  303.3 15.4 %copy-start.5 = (bf16[1552,256]{1,0:T(8,128)(2,1)}, bf16[1552,256]{1,0:T(8,128)(2,1)S(1)}, u32[]{:S(2)}) copy-start(bf16[1552,256]{1,0:T(8,128)(2,1)S(1)} %collective-permute-done.11.second_ref) | copy-start | bytes 2383876
  303.3 15.4 %copy-start.9 = (bf16[88,32,128]{2,1,0:T(8,128)(2,1)}, bf16[88,32,128]{2,1,0:T(8,128)(2,1)S(1)}, u32[]{:S(2)}) copy-start(bf16[88,32,128]{2,1,0:T(8,128)(2,1)S(1)} %collective-permute-done.18.rest_1_) | copy-start | bytes 2162692
  307.2 11.4 %copy-start.10 = (bf16[88,32,128]{2,1,0:T(8,128)(2,1)}, bf16[88,32,128]{2,1,0:T(8,128)(2,1)S(1)}, u32[]{:S(2)}) copy-start(bf16[88,32,128]{2,1,0:T(8,128)(2,1)S(1)} %collective-permute-done.19.rest_2_) | copy-start | bytes 2162692
  340.5 6.0 %collective-permute-start.21 = (bf16[2,48,384]{2,0,1:T(2,128)(2,1)S(1)}, bf16[2,48,384]{2,0,1:T(2,128)(2,1)S(1)}, u32[]{:S(2)}, u32[]{:S(2)}) collective-permute-start(bf16[2,48,384]{2,0,1:T(2,128)(2,1)S(1)} %slice.128), channel_id=1, source_target_pairs={{0,1},{1,2},{2,3},{4,5},{5,6},{6,7},{8,9},{9,10},{10,11},{12,13},{... | collective-permute-start | bytes 221192 | tf_op jit(solution)/shard_map/ppermute | solution.py:598
  342.9 10.0 %all-to-all-start = ((bf16[4,48,6,96]{3,1,2,0:T(8,128)(2,1)}), bf16[4,48,6,96]{3,1,2,0:T(8,128)(2,1)S(1)}, u32[]{:S(2)}, u32[]{:S(2)}) async-start(bf16[4,48,6,96]{3,1,2,0:T(8,128)(2,1)} %copy.17), calls=%async_computation | async-start | bytes 589824 | tf_op jit(solution)/shard_map/all_to_all | solution.py:606
